TPU v7x, 128 devices: a whole 4x4x4 slice. The times are simulated.
128 devices in a mesh: slab: 32 (over x, y_hi, z), sub: 4 (over y_lo, core).
Axes of the slice: x: 4, y: 4 (y_hi: 2, y_lo: 2; y = y_hi * 2 + y_lo), z: 4, core: 2. Of those that a mesh axis runs over, the one named last changes fastest.
Arguments:
- mm_atoms: float32 [4, 2097152], P(None, ('slab', 'sub')), may hold values from -6 to 6
- neighbours: int32 [16, 2097152], P(None, ('slab', 'sub')), may hold values from 0 to 18431, as said below
- embed_blocks: int32 [128, 8], P(('slab', 'sub')), may hold values from 0 to 127, as said below
- embed_count: int32 [128], P(('slab', 'sub')), may hold values from 1 to 8
- ml_coords: float32 [3, 5120], P(None, ('slab', 'sub')), may hold values from -6 to 6
- ml_species: int32 [5120], P(('slab', 'sub')), may hold values from 0 to 9
- ml_edges: int32 [5120, 32], P(('slab', 'sub')), may hold values from 0 to 5119
- species_table: float32 [10, 256], replicated, may hold values from -6 to 6
- field_weight: float32 [256], replicated, may hold values from -4 to 4
- msg_weight: bfloat16 [2, 256, 256], replicated, may hold values from -0.375 to 0.375
- radial_weight: float32 [2, 8, 256], replicated, may hold values from -6 to 6
- mix_weight: bfloat16 [2, 256, 256], replicated, may hold values from -0.375 to 0.375
- charge_weight: float32 [256], replicated, may hold values from -0.375 to 0.375
- energy_weight: float32 [256], replicated, may hold values from -0.375 to 0.375
Outputs:
- ml_energy: float32 [5120], P(('slab', 'sub'))
- mm_force: float32 [3, 2097152], P(None, ('slab', 'sub'))
Inputs may be any that keep to these rules, and one draw needn't show every extreme that they name: `neighbours`: slot p of 2097152 atom a on any device holds 1024 + a + o with -1024 <= o <= 1024; o = 0 marks an empty slot (an atom paired with itself). `embed_blocks`: the blocks listed for one device are distinct.
All inputs are finite; a program needn't handle non-finite values.
Results may differ from a plain program's by a relative error of at most 0.00055.
Values may be sent and summed in bfloat16 or wider, within the bound.
No kernel may reach another device: no remote copies, remote signals or barrier semaphores. Data moves between devices by JAX's collectives and lax.ppermute only.
A program may use at most 320 MiB of HBM per device.

v0:
```python
import math

import jax
import jax.numpy as jnp
from jax import lax
from jax.sharding import PartitionSpec as P

radial_gamma = 2.0
radial_step = 0.5


def padded(value, sides, width):
    for axis, dim in sides:
        devices, length = (lax.axis_size(axis), value.shape[dim])
        up = [(i, (i + 1) % devices) for i in range(devices)]
        down = [(j, i) for i, j in up]
        last = lax.slice_in_dim(value, length - width, length, axis=dim)
        leading = lax.slice_in_dim(value, 0, width, axis=dim)
        before = lax.ppermute(last, axis, up)
        after = lax.ppermute(leading, axis, down)
        value = jnp.concatenate([before, value, after], axis=dim)
    return value


def square_dist(left, right):
    dist_sq = jnp.zeros((left.shape[1], right.shape[1]), jnp.float32)
    gaps_list = []
    for coord in range(3):
        gap = right[coord][None, :] - left[coord][:, None]
        gaps_list.append(gap)
        dist_sq = dist_sq + gap * gap
    return (dist_sq, gaps_list)


def slot_forces(slots, ml_pos, charges, coupling):
    dist_sq, gaps_list = square_dist(ml_pos, slots)
    weighted = charges[:, None] * (dist_sq + 1.0) ** (-1.5)
    return jnp.stack([coupling * slots[3] * jnp.sum(weighted * gap, axis=0) for gap in gaps_list])


def edge_basis(own_pos, all_pos, edges, nrad):
    partner_pos = all_pos[:, edges]
    gaps = own_pos[:, :, None] - partner_pos
    distance = jnp.sqrt(jnp.sum(gaps * gaps, axis=0))
    basis_mu = radial_step * jnp.arange(nrad, dtype=jnp.float32)
    return jnp.exp(-radial_gamma * (distance[..., None] - basis_mu) ** 2)


def layer_message(basis, edges, all_proj, radial_w):
    radial = jnp.einsum("ikb,bc->ikc", basis, radial_w, precision=lax.Precision.HIGHEST)
    return jnp.mean(radial * all_proj[edges].astype(jnp.float32), axis=1).astype(jnp.bfloat16)


def species_rows(kinds, species_table):
    onehot = (
        kinds[:, None] == jnp.arange(species_table.shape[0], dtype=jnp.int32)[None, :]
    ).astype(jnp.float32)
    return jnp.dot(onehot, species_table, precision=lax.Precision.HIGHEST)


def body(
    mm_atoms,
    neighbours,
    embed_blocks,
    embed_count,
    ml_coords,
    ml_species,
    ml_edges,
    species_table,
    field_weight,
    msg_weight,
    radial_weight,
    mix_weight,
    charge_weight,
    energy_weight,
):
    own_rows = mm_atoms.shape[1]
    nblocks = own_rows // 128
    slots_max = embed_blocks.shape[1]
    nrad = radial_weight.shape[1]
    extended = padded(mm_atoms, ((("slab", "sub"), 1),), own_rows // 16)
    partner = extended[:, neighbours]
    offset_vec = mm_atoms[:3, None, :] - partner[:3]
    dist_sq = jnp.sum(offset_vec * offset_vec, axis=0) + 1.0
    strength = mm_atoms[3][None, :] * partner[3] * dist_sq ** (-1.5)
    pair_force = jnp.sum(strength[None] * offset_vec, axis=1)
    blocks = embed_blocks[0]
    chosen = mm_atoms.reshape(4, nblocks, 128)[:, blocks, :]
    live_slot = (jnp.arange(slots_max, dtype=jnp.int32) < embed_count[0]).astype(jnp.float32)
    chosen = jnp.concatenate([chosen[:3], (chosen[3] * live_slot[:, None])[None]], axis=0)
    chosen = chosen.reshape(4, slots_max * 128)
    shared, ml_all = (
        lax.all_gather(chosen, ("slab", "sub"), axis=1, tiled=True),
        lax.all_gather(ml_coords, ("slab", "sub"), axis=1, tiled=True),
    )
    total_ml = ml_all.shape[1]
    coupling = 4.0 / math.sqrt(total_ml)
    field_coupling = 3.0 / math.sqrt(shared.shape[1])
    field_sq, unused_gaps = square_dist(ml_coords, shared)
    potential = field_coupling * jnp.sum(shared[3][None, :] * lax.rsqrt(field_sq + 1.0), axis=1)
    features = species_rows(ml_species, species_table) + potential[:, None] * field_weight[None, :]
    radial_basis = edge_basis(ml_coords, ml_all, ml_edges, nrad)
    for layer_idx in range(msg_weight.shape[0]):
        projected = jnp.dot(
            features.astype(jnp.bfloat16), msg_weight[layer_idx], preferred_element_type=jnp.float32
        ).astype(jnp.bfloat16)
        all_proj = lax.all_gather(projected, ("slab", "sub"), axis=0, tiled=True)
        message = layer_message(radial_basis, ml_edges, all_proj, radial_weight[layer_idx])
        features = features + jax.nn.silu(
            jnp.dot(message, mix_weight[layer_idx], preferred_element_type=jnp.float32)
        )
    charge = jnp.tanh(jnp.dot(features, charge_weight, precision=lax.Precision.HIGHEST))
    ml_energy = (
        jnp.dot(features, energy_weight, precision=lax.Precision.HIGHEST) + charge * potential
    )
    terms = slot_forces(shared, ml_coords, charge, coupling)
    own_force = lax.psum_scatter(terms, ("slab", "sub"), scatter_dimension=1, tiled=True)
    mm_force = (
        pair_force.reshape(3, nblocks, 128)
        .at[:, blocks, :]
        .add(own_force.reshape(3, slots_max, 128))
    )
    return (ml_energy, mm_force.reshape(3, own_rows))


def solution(mesh):
    in_specs = (
        P(None, ("slab", "sub")),
        P(None, ("slab", "sub")),
        P(("slab", "sub"), None),
        P(("slab", "sub")),
        P(None, ("slab", "sub")),
        P(("slab", "sub")),
        P(("slab", "sub"), None),
        P(),
        P(),
        P(),
        P(),
        P(),
        P(),
        P(),
    )
    out_specs = (P(("slab", "sub")), P(None, ("slab", "sub")))
    return jax.shard_map(body, mesh=mesh, in_specs=in_specs, out_specs=out_specs, check_vma=False)
```

profile of v0, /device:TPU:1, one launch (start us, length us, event | category | flops | bytes accessed | tf_op | source)
XLA Modules:
  0.0 2193.7 jit_solution(700902462591551525)
XLA Ops:
  7.2 0.0 copy-start
  7.2 0.0 all-gather.5.cloned.1.call-start
  7.2 0.7 fusion.46
  8.0 1.5 gather_fusion
  10.2 0.1 fusion.45
  10.2 0.6 pad_maximum_fusion.2
  10.9 0.0 all-gather.5.cloned.1.call-update
  10.9 0.0 all-gather.7.cloned.1.call-start
  10.9 0.8 slice_bitcast_fusion.3
  11.8 196.5 %all-gather.5.cloned.1.call-done = f32[4,131072]{1,0:T(4,128)} async-done(((f32[4,1024]{1,0:T(4,128)}), f32[4,131072]{1,0:T(4,128)}) %all-gather.5.cloned.1.call-update) | async-done | bytes 2097168 | tf_op jit(solution)/shard_map/all_gather | solution.py:93
  208.3 5.9 fusion.51
  214.2 0.8 copy-done.2
  214.9 8.6 multiply_reduce_fusion
  223.6 0.9 convolution_add_fusion
  224.5 1.7 convolution_convert_fusion.1
  226.2 0.0 all-gather.7.cloned.1.call-update
  226.2 0.0 all-gather.9.cloned.1.call-start
  226.2 1.3 fusion.52
  227.6 1.6 collective-permute-start
  229.2 0.8 copy.35
  230.0 0.7 compare_select_fusion.1
  230.7 0.1 copy.37
  230.8 0.1 reshape.114
  230.8 177.6 %all-gather = f32[128,40,3]{1,2,0:T(4,128)S(1)} all-gather(f32[1,40,3]{1,2,0:T(4,128)} %bitcast.123), channel_id=1, replica_groups=mesh['slab'=32,'sub'=4] {'slab','sub'}, dimensions={0}, use_global_device_ids=true | all-gather | bytes 61920 | tf_op jit(solution)/shard_map/all_gather | solution.py:94
  408.4 0.9 copy.36
  409.4 3.1 gather_fusion.1
  412.5 1.3 multiply_reduce_fusion.3
  413.9 1.3 fusion.10
  415.2 0.2 copy.43
  415.5 5.7 all-gather.7.cloned.1.call-done
  421.2 5.2 gather_fusion.2
  426.4 2.1 fusion.6
  428.5 1.1 multiply_add_fusion.1
  429.6 0.0 copy-start.9
  429.6 0.8 convolution_convert_fusion
  430.3 0.0 all-gather.9.cloned.1.call-update
  430.4 0.2 reduce-scatter.4.cloned.1.call-start
  430.6 0.1 broadcast_clamp_fusion
  430.8 0.1 slice.87
  430.9 0.1 pad_maximum_fusion.1
  430.9 5.1 copy.38
  436.0 863.6 %gather_fusion.4 = f32[262144,4]{1,0:T(8,128)} fusion(f32[4,18432]{0,1:T(8,128)} %copy.38, s32[262144]{0:T(1024)S(1)} %broadcast_clamp_fusion), kind=kCustom, calls=%fused_computation.4 | custom fusion | bytes 9437184 | tf_op jit(solution)/shard_map/gather | solution.py:82
  1299.7 0.0 copy-start.21
  1299.7 0.0 copy-start.11
  1299.8 70.9 %copy.39 = f32[16,16384,4]{1,0,2:T(8,128)} copy(f32[16,16384,4]{2,1,0:T(8,128)} %bitcast.35) | data formatting | bytes 8388608 | tf_op jit(solution)/shard_map/gather | solution.py:82
  1370.7 2.3 multiply_reduce_fusion.2
  1373.0 0.0 all-gather.9.cloned.1.call-done
  1373.0 5.2 gather_fusion.3
  1378.3 1.4 fusion.7
  1379.7 0.2 multiply_add_fusion
  1379.9 0.1 fusion.8
  1380.0 0.0 copy-done.5
  1380.1 25.8 %fusion.3 = (f32[131072]{0:T(1024)S(1)}, f32[131072]{0:T(1024)S(1)}, f32[131072]{0:T(1024)S(1)}) fusion(f32[40]{0:T(128)S(1)} %fusion.8, f32[40]{0:T(128)S(1)} %copy-done.18, f32[131072]{0:T(1024)S(1)} %bitcast.111, f32[40]{0:T(128)S(1)} %copy-done.20, f32[131072]{0:T(1024)S(1)} %bitcast.113, f32[40]{0:T(128)S(1)} %copy-done.16, f32[131072]{0:T(1024)} %bitcast.115), kind=kLoop, calls=%fused_computation.15 | loop fusion | flops 83492864 | bytes 3146368 | tf_op jit(solution)/shard_map/reduce_sum | solution.py:38
  1405.9 3.4 fusion.35
  1409.3 1.4 pad_maximum_fusion
  1410.6 30.6 %copy.41 = f32[3,131072]{0,1:T(8,128)} copy(f32[3,131072]{1,0:T(4,128)S(1)} %pad_maximum_fusion) | data formatting | bytes 3145728
  1441.3 0.0 reduce-scatter.4.cloned.1.call-update
  1441.3 1.7 fusion.12
  1443.0 2.6 multiply_reduce_fusion.1
  1445.6 0.7 fusion.9
  1446.3 738.1 %reduce-scatter.4.cloned.1.call-done = f32[1024,3]{1,0:T(8,128)} async-done(((f32[131072,3]{1,0:T(8,128)}), f32[1024,3]{1,0:T(8,128)}) %reduce-scatter.4.cloned.1.call-update) | async-done | bytes 12304
  2184.4 1.2 copy.42
  2185.6 0.8 scatter_fusion
  2186.4 0.7 copy-done.7
  (53 shorter events, 0.1 us)
Async XLA Ops:
  7.2 216.4 %copy-start = (f32[10,256]{1,0:T(8,128)S(1)}, f32[10,256]{1,0:T(8,128)}, u32[]{:S(2)}) copy-start(f32[10,256]{1,0:T(8,128)} %param.21) | copy-start | bytes 30724
  7.2 423.6 %copy-start.1 = (f32[4,16384]{1,0:T(4,128)S(1)}, f32[4,16384]{1,0:T(4,128)}, u32[]{:S(2)}) copy-start(f32[4,16384]{1,0:T(4,128)} %param.14) | copy-start | bytes 786436
  7.2 422.4 %copy-start.8 = (bf16[2,256,256]{2,1,0:T(8,128)(2,1)S(1)}, bf16[2,256,256]{2,1,0:T(8,128)(2,1)}, u32[]{:S(2)}) copy-start(bf16[2,256,256]{2,1,0:T(8,128)(2,1)} %param.23) | copy-start | bytes 786436
  7.2 201.1 %all-gather.5.cloned.1.call-start = ((), (), s32[]{:S(2)}) async-start(), calls=%async_computation.1 | async-start | bytes 2113536 | tf_op jit(solution)/shard_map/all_gather | solution.py:93
  10.9 410.3 %all-gather.7.cloned.1.call-start = ((), (), s32[]{:S(2)}) async-start(), calls=%async_computation.2 | async-start | bytes 2641920 | tf_op jit(solution)/shard_map/all_gather | solution.py:107
  11.7 217.5 %copy-start.17 = (f32[40]{0:T(128)}, f32[40]{0:T(128)S(1)}, u32[]{:S(2)}) copy-start(f32[40]{0:T(128)S(1)} %get-tuple-element.15) | copy-start | bytes 484
  11.7 217.5 %copy-start.19 = (f32[40]{0:T(128)}, f32[40]{0:T(128)S(1)}, u32[]{:S(2)}) copy-start(f32[40]{0:T(128)S(1)} %get-tuple-element.16) | copy-start | bytes 484
  11.7 396.7 %copy-start.15 = (f32[40]{0:T(128)}, f32[40]{0:T(128)S(1)}, u32[]{:S(2)}) copy-start(f32[40]{0:T(128)S(1)} %get-tuple-element.14) | copy-start | bytes 484
  214.1 0.8 copy-start.2
  214.2 9.4 copy-start.4
  214.2 9.4 copy-start.6
  223.5 184.9 %copy-start.13 = (f32[40]{0:T(128)}, f32[40]{0:T(128)S(1)}, u32[]{:S(2)}) copy-start(f32[40]{0:T(128)S(1)} %multiply_reduce_fusion) | copy-start | bytes 484
  226.2 1146.8 %all-gather.9.cloned.1.call-start = ((), (), s32[]{:S(2)}) async-start(), calls=%async_computation.3 | async-start | bytes 2641920 | tf_op jit(solution)/shard_map/all_gather | solution.py:107
  227.6 203.3 %collective-permute-start = (f32[4,1024]{1,0:T(4,128)}, f32[4,1024]{1,0:T(4,128)S(1)}, u32[]{:S(2)}, u32[]{:S(2)}) collective-permute-start(f32[4,1024]{1,0:T(4,128)} %get-tuple-element.12), channel_id=1, source_target_pairs={{0,1},{1,2},{2,3},{3,4},{4,5},{5,6},{6,7},{7,8},{8,9},{9,10},{10,1... | collective-permute-start | bytes 49160 | tf_op jit(solution)/shard_map/ppermute | solution.py:19
  229.2 201.7 %collective-permute-start.1 = (f32[4,1024]{1,0:T(4,128)}, f32[4,1024]{1,0:T(4,128)S(1)}, u32[]{:S(2)}, u32[]{:S(2)}) collective-permute-start(f32[4,1024]{1,0:T(4,128)} %get-tuple-element.13), channel_id=1, source_target_pairs={{1,0},{2,1},{3,2},{4,3},{5,4},{6,5},{7,6},{8,7},{9,8},{10,9},{11,1... | collective-permute-start | bytes 49160 | tf_op jit(solution)/shard_map/ppermute | solution.py:20
  415.4 15.2 copy-start.23
  429.6 870.1 %copy-start.9 = (f32[40,256]{1,0:T(8,128)}, f32[40,256]{1,0:T(8,128)S(1)}, u32[]{:S(2)}) copy-start(f32[40,256]{1,0:T(8,128)S(1)} %multiply_add_fusion.1) | copy-start | bytes 122884
  430.4 1754.0 %reduce-scatter.4.cloned.1.call-start = ((), (), s32[]{:S(2)}) async-start(), calls=%async_computation.4 | async-start | bytes 67633152
  1299.7 78.6 %copy-start.22 = (f32[2,8,256]{2,1,0:T(8,128)S(1)}, f32[2,8,256]{2,1,0:T(8,128)}, u32[]{:S(2)}) copy-start(f32[2,8,256]{2,1,0:T(8,128)} %param.24) | copy-start | bytes 49156
  1299.7 78.6 %copy-start.24 = (f32[8]{0:T(128)S(1)}, f32[8]{0:T(128)}, u32[]{:S(2)}) copy-start(f32[8]{0:T(128)} %copy-done.23) | copy-start | bytes 100
  1299.7 80.0 %copy-start.10 = (f32[40,256]{1,0:T(8,128)S(1)}, f32[40,256]{1,0:T(8,128)}, u32[]{:S(2)}) copy-start(f32[40,256]{1,0:T(8,128)} %copy-done.9) | copy-start | bytes 122884
  1299.7 80.0 %copy-start.21 = (bf16[2,256,256]{2,1,0:T(8,128)(2,1)S(1)}, bf16[2,256,256]{2,1,0:T(8,128)(2,1)}, u32[]{:S(2)}) copy-start(bf16[2,256,256]{2,1,0:T(8,128)(2,1)} %param.25) | copy-start | bytes 786436
  1299.7 80.2 %copy-start.11 = (f32[256]{0:T(256)S(1)}, f32[256]{0:T(256)}, u32[]{:S(2)}) copy-start(f32[256]{0:T(256)} %param.26) | copy-start | bytes 3076
  1299.7 80.3 %copy-start.3 = (f32[1,131072]{1,0:T(1,128)S(1)}, f32[1,131072]{1,0:T(1,128)}, u32[]{:S(2)}) copy-start(f32[1,131072]{1,0:T(1,128)} %copy-done.2) | copy-start | bytes 1572868
  1299.7 80.3 %copy-start.5 = (f32[1,131072]{1,0:T(1,128)S(1)}, f32[1,131072]{1,0:T(1,128)}, u32[]{:S(2)}) copy-start(f32[1,131072]{1,0:T(1,128)} %copy-done.4) | copy-start | bytes 1572868
  1299.7 80.3 %copy-start.16 = (f32[40]{0:T(128)S(1)}, f32[40]{0:T(128)}, u32[]{:S(2)}) copy-start(f32[40]{0:T(128)} %copy-done.15) | copy-start | bytes 484
  1299.7 80.3 %copy-start.18 = (f32[40]{0:T(128)S(1)}, f32[40]{0:T(128)}, u32[]{:S(2)}) copy-start(f32[40]{0:T(128)} %copy-done.17) | copy-start | bytes 484
  1299.8 80.3 %copy-start.20 = (f32[40]{0:T(128)S(1)}, f32[40]{0:T(128)}, u32[]{:S(2)}) copy-start(f32[40]{0:T(128)} %copy-done.19) | copy-start | bytes 484
  1441.3 4.3 copy-start.12
  1441.3 4.4 copy-start.14
  2186.4 0.7 copy-start.7
Sparse Core Ops, SparseCore 0:
  11.0 197.2 all-gather.4
  226.3 194.8 all-gather.6
  430.5 194.8 all-gather.8
  1441.4 742.9 reduce-scatter.3
where the time goes:
time: 2200 us; the launch traced here: 2190 us
  local copies, waits for them, and re-layouts  998 us (45%)
  waiting for transfers between devices  940 us (43%)
  blocking collectives  178 us (8%)
  other arithmetic  51.6 us (2%)
    gather x2, local copies, waits for them, and re-layouts, body(): partner = extended[:, neighbours]  935 us
    unnamed x5, waiting for transfers between devices  738 us
    all_gather x1, waiting for transfers between devices, body(): lax.all_gather(chosen, ('slab', 'sub'), axis=1, tiled=True)  197 us
    all_gather x1, blocking collectives, body(): lax.all_gather(ml_coords, ('slab', 'sub'), axis=1, tiled=True)  178 us
  transfers between devices with their start and end apart: 6, of which 3 were waited for; matrix products, arithmetic and copies ran while one was open for 44% of the time, Pallas kernels for 0%

commit v1 on v0

v1 whole, which is shorter than its diff:
```python
import functools
import math

import jax
import jax.numpy as jnp
from jax import lax
from jax.experimental import pallas as pl
from jax.experimental.pallas import tpu as pltpu
from jax.sharding import Mesh
from jax.sharding import PartitionSpec as P

ALL = ("x", "yh", "z", "yl", "c")
Y = ("yh", "yl")
vmem_mib = lambda size: pltpu.CompilerParams(vmem_limit_bytes=size * 1024 * 1024)
LANES = 128
NDEV = 128
ML_DEV = 40
KNB = 32
EDGES = ML_DEV * KNB
ROWS = 1344
HALO_BLOCKS = 8
PAIR_STEP = 4


def rows0(left, right):
    return lax.dot_general(
        left, right, (((0,), (0,)), ((), ())), preferred_element_type=jnp.float32
    )


def pair_kernel(first, count, left, own, right, nb, after, out, zero, ext):
    own_blocks = own.shape[1] // LANES
    step = pl.program_id(0)

    @pl.when(step == 0)
    def _():
        zero[...] = jnp.zeros_like(zero)
        low, high = first - HALO_BLOCKS, first + count + HALO_BLOCKS
        for src, begin, size in ((left, -HALO_BLOCKS, HALO_BLOCKS), (own, 0, own_blocks), (right, own_blocks, HALO_BLOCKS)):
            start, stop = max(low, begin), min(high, begin + size)
            if start >= stop:
                continue

            def fill(r, carry, src=src, begin=begin):
                rows = src[:, pl.ds(pl.multiple_of((r - begin) * LANES, LANES), LANES)]
                for c in range(4):
                    ext[c, r - low] = jnp.broadcast_to(rows[c : c + 1], (8, LANES))
                return carry

            lax.fori_loop(start, stop, fill, 0)

    blocks = nb.shape[1] // LANES

    def block(j, carry):
        b = step * blocks + j
        lanes = pl.ds(pl.multiple_of(j * LANES, LANES), LANES)
        rel = nb[:, lanes] - (b + first) * LANES
        row = rel >> 7
        lane = rel & 127
        centre = [ext[c, b + HALO_BLOCKS] for c in range(4)]
        total = [jnp.zeros((8, LANES), jnp.float32) for _ in range(3)]
        for h in range(nb.shape[0] // 8):
            near = row[8 * h : 8 * h + 8]
            pick = lane[8 * h : 8 * h + 8]
            got = [jnp.zeros((8, LANES), jnp.float32) for _ in range(4)]
            for k in range(2 * HALO_BLOCKS + 1):
                here = near == k
                for c in range(4):
                    value = jnp.take_along_axis(ext[c, b + k], pick, axis=1, mode="promise_in_bounds")
                    got[c] = jnp.where(here, value, got[c])
            off = [centre[c] - got[c] for c in range(3)]
            inv = lax.rsqrt(off[0] * off[0] + off[1] * off[1] + off[2] * off[2] + 1.0)
            strength = centre[3] * got[3] * (inv * inv * inv)
            for c in range(3):
                total[c] = total[c] + strength * off[c]
        for c in range(3):
            out[c : c + 1, lanes] = jnp.sum(total[c], axis=0, keepdims=True)
        return carry

    lax.fori_loop(0, blocks, block, 0, unroll=PAIR_STEP)


def pair_forces(first, count, left, own, right, neighbours, after):
    wide = PAIR_STEP * LANES
    whole = lambda a: pl.BlockSpec(a.shape, lambda i: (0, 0))
    slots = neighbours.shape[0]
    return pl.pallas_call(
        functools.partial(pair_kernel, first, count),
        grid=(count // PAIR_STEP,),
        out_shape=(
            jax.ShapeDtypeStruct((3, count * LANES), jnp.float32),
            jax.ShapeDtypeStruct((1, HALO_BLOCKS * LANES), jnp.float32),
        ),
        in_specs=[
            whole(left),
            whole(own),
            whole(right),
            pl.BlockSpec((slots, wide), lambda i: (0, i + first // PAIR_STEP)),
            pl.BlockSpec(memory_space=pl.ANY),
        ],
        out_specs=(
            pl.BlockSpec((3, wide), lambda i: (0, i)),
            pl.BlockSpec((1, HALO_BLOCKS * LANES), lambda i: (0, 0)),
        ),
        scratch_shapes=[pltpu.VMEM((4, count + 2 * HALO_BLOCKS, 8, LANES), jnp.float32)],
        compiler_params=vmem_mib(6),
        cost_estimate=pl.CostEstimate(
            flops=count * 10**7, bytes_accessed=count * 16384, transcendentals=count * slots * LANES
        ),
        name="pair_forces",
    )(left, own, right, neighbours, after)


def spread_kernel(coords, species, out):
    rows = [coords[c : c + 1, :] for c in range(3)] + [species[...].astype(jnp.float32)]
    rows = rows[:3] + [jnp.zeros((1, 8), jnp.float32)] + rows[3:] + [jnp.zeros((1, LANES - ML_DEV), jnp.float32)]
    out[:, 0, :] = jnp.broadcast_to(jnp.concatenate(rows, axis=1), (NDEV, 2 * LANES))


def spread(coords, species):
    vmem = pl.BlockSpec(memory_space=pltpu.VMEM)
    return pl.pallas_call(
        spread_kernel,
        out_shape=jax.ShapeDtypeStruct((NDEV, 1, 2 * LANES), jnp.float32),
        in_specs=[vmem, vmem],
        out_specs=vmem,
        name="spread",
    )(coords, species)


def three_parts(value):
    one = value.astype(jnp.bfloat16).astype(jnp.float32)
    rest = value - one
    two = rest.astype(jnp.bfloat16).astype(jnp.float32)
    three = (rest - two).astype(jnp.bfloat16).astype(jnp.float32)
    return one, two, three


def field_kernel(scale, blocks, count, mm, tab, after, pot, atoms, slots, p8, qb):
    turned = tab[:, :LANES].T
    x, y, z = (turned[ML_DEV * c : ML_DEV * (c + 1)] for c in range(3))
    p8[...] = jnp.zeros_like(p8)
    for c, value in enumerate((x, y, z, x * x + y * y + z * z, jnp.ones_like(x))):
        p8[pl.ds(c, ML_DEV, stride=8), :] = value

    def atom_tile(t, carry):
        one, two, three = three_parts(p8[pl.ds(pl.multiple_of(t * 8, 8), 8), :])
        atoms[:, pl.ds(pl.multiple_of(t * LANES, LANES), LANES)] = jnp.concatenate(
            [one, one, two, two, one, three], axis=0
        ).astype(jnp.bfloat16)
        return carry

    lax.fori_loop(0, ML_DEV, atom_tile, 0)
    nslots = blocks.shape[1]
    for s in range(nslots):
        rows = mm[:, pl.ds(pl.multiple_of(blocks[0, s] * LANES, LANES), LANES)]
        q = rows[3:4] * jnp.where(s < count[0], 1.0, 0.0)
        pos = rows[:3]
        norm = jnp.sum(pos * pos, axis=0, keepdims=True) + 1.0
        eight = jnp.concatenate(
            [-2.0 * pos, jnp.ones_like(q), norm, jnp.zeros((3, LANES), jnp.float32)], axis=0
        )
        one, two, three = three_parts(eight)
        slots[:, s * LANES : (s + 1) * LANES] = jnp.concatenate(
            [one, two, one, two, three, one], axis=0
        ).astype(jnp.bfloat16)
        qb[s * LANES : (s + 1) * LANES, :] = jnp.broadcast_to(q, (LANES, LANES)).T

    def tile(i, carry):
        right = atoms[:, pl.ds(pl.multiple_of(i * 256, 256), 256)]
        total = jnp.zeros((8, 256), jnp.float32)
        for s in range(nslots // 2):
            inv = lax.rsqrt(rows0(slots[:, s * 256 : (s + 1) * 256], right))
            q = qb[s * 256 : (s + 1) * 256, :]
            term = inv * jnp.concatenate([q, q], axis=1)
            total = total + jnp.sum(term.reshape(32, 8, 256), axis=0)
        total = scale * jnp.sum(total, axis=0, keepdims=True)
        pot[pl.ds(2 * i, 1), :] = total[:, :LANES]
        pot[pl.ds(2 * i + 1, 1), :] = total[:, LANES:]
        return carry

    lax.fori_loop(0, ML_DEV // 2, tile, 0, unroll=5)


def field(blocks, count, mm, tab, after, scale):
    nslots = blocks.shape[1]
    smem = pl.BlockSpec(memory_space=pltpu.SMEM)
    vmem = pl.BlockSpec(memory_space=pltpu.VMEM)
    return pl.pallas_call(
        functools.partial(field_kernel, scale),
        out_shape=(
            jax.ShapeDtypeStruct((ML_DEV, LANES), jnp.float32),
            pltpu.HBM((48, ML_DEV * LANES), jnp.bfloat16),
            pltpu.HBM((48, nslots * LANES), jnp.bfloat16),
        ),
        in_specs=[smem, smem, vmem, vmem, pl.BlockSpec(memory_space=pl.ANY)],
        out_specs=(vmem,) * 3,
        scratch_shapes=[
            pltpu.VMEM((8 * ML_DEV, LANES), jnp.float32),
            pltpu.VMEM((nslots * LANES, LANES), jnp.float32),
        ],
        compiler_params=vmem_mib(10),
        name="field",
    )(blocks, count, mm, tab, after)


def lane_iota(shape):
    return lax.broadcasted_iota(jnp.int32, shape, 1)


def exact_pick(left, right):
    left = left.astype(jnp.bfloat16)
    parts = [jnp.dot(left, part.astype(jnp.bfloat16), preferred_element_type=jnp.float32) for part in three_parts(right)]
    return (parts[2] + parts[1]) + parts[0]


def exact_sum(left, right):
    right = right.astype(jnp.bfloat16)
    parts = [jnp.dot(part.astype(jnp.bfloat16), right, preferred_element_type=jnp.float32) for part in three_parts(left)]
    return (parts[2] + parts[1]) + parts[0]


def where_is(me, ids):
    own_ids = me * ML_DEV + jnp.minimum(lax.broadcasted_iota(jnp.int32, (ROWS - EDGES, 1), 0), ML_DEV - 1)
    atom = jnp.concatenate([ids, own_ids], axis=0)
    dev = (atom * 52429) >> 21
    return dev, atom - dev * ML_DEV


def geometry_kernel(me, ids, tab, after, basis_out, kinds_out, zero):
    zero[...] = jnp.zeros_like(zero)
    dev, t = where_is(me[0], ids[...])
    at_dev = lane_iota((ROWS, LANES)) == dev
    rows = exact_pick(jnp.where(at_dev, 1.0, 0.0), tab[...])
    lane = lane_iota((1, 2 * LANES))
    place = jnp.where(lane < ML_DEV, lane, jnp.where(lane < 2 * ML_DEV, lane - ML_DEV, lane - 2 * ML_DEV))
    place = jnp.where(lane < LANES, place, lane - LANES)
    place = jnp.where(place < ML_DEV, place, -1)
    rows = jnp.where(place == t, rows, 0.0)
    src = lax.broadcasted_iota(jnp.int32, (2 * LANES, LANES), 0)
    dst = lane_iota((2 * LANES, LANES))
    group = jnp.where(src < ML_DEV, 0, jnp.where(src < 2 * ML_DEV, 1, jnp.where(src < LANES, 2, 3)))
    picked = exact_sum(rows, jnp.where(group == dst, 1.0, 0.0))
    own = picked[EDGES : EDGES + ML_DEV]
    centre = jnp.broadcast_to(own[:, None, :], (ML_DEV, KNB, LANES)).reshape(EDGES, LANES)
    gap = picked[:EDGES] - centre
    lanes = lane_iota((EDGES, LANES))
    dist = jnp.sqrt(exact_sum(jnp.where(lanes < 3, gap * gap, 0.0), jnp.ones((LANES, LANES), jnp.float32)))
    shift = dist - 0.5 * (lanes & 7).astype(jnp.float32)
    one, two, three = three_parts(jnp.exp(-2.0 * (shift * shift)))
    part = lanes >> 3
    value = jnp.where((part < 2) | (part == 4), one, jnp.where(part < 4, two, three))
    basis_out[...] = jnp.where(part < 6, value, 0.0).astype(jnp.bfloat16)
    kind = jnp.broadcast_to(picked[:, 3:4], (ROWS, LANES)).astype(jnp.int32)
    lanes = lane_iota((ROWS, LANES))
    kinds_out[...] = jnp.where((kind == (lanes & 15)) & (lanes < 48), 1.0, 0.0).astype(jnp.bfloat16)


def geometry(me, ids, tab, after):
    smem = pl.BlockSpec(memory_space=pltpu.SMEM)
    vmem = pl.BlockSpec(memory_space=pltpu.VMEM)
    return pl.pallas_call(
        geometry_kernel,
        out_shape=(
            jax.ShapeDtypeStruct((EDGES, LANES), jnp.bfloat16),
            jax.ShapeDtypeStruct((ROWS, LANES), jnp.bfloat16),
            jax.ShapeDtypeStruct((1, LANES), jnp.float32),
        ),
        in_specs=[smem, vmem, vmem, pl.BlockSpec(memory_space=pl.ANY)],
        out_specs=(vmem,) * 3,
        compiler_params=vmem_mib(20),
        name="geometry",
    )(me, ids, tab, after)


def radial_of(basis, weights):
    one, two, three = three_parts(weights)
    rest = jnp.zeros((LANES - 48, weights.shape[1]), jnp.float32)
    stacked = jnp.concatenate([one, two, one, two, three, one, rest], axis=0).astype(jnp.bfloat16)
    return jnp.dot(basis, stacked, preferred_element_type=jnp.float32)


def first_layer_kernel(
    me, ids, pot, basis, kinds, table, field_w, msg, radial_w, mix, feat_out, proj_out
):
    pot_rows = jnp.concatenate([pot[...], jnp.zeros((LANES - ML_DEV, LANES), jnp.float32)], axis=0).T
    dev, t = where_is(me[0], ids[...])
    lanes = lane_iota((ROWS, LANES))
    rows = exact_pick(jnp.where(lanes == dev, 1.0, 0.0), pot_rows)
    pot_of = jnp.sum(jnp.where(lanes == t, rows, 0.0), axis=1, keepdims=True)
    channels = msg.shape[1]
    lines = jnp.concatenate([table[...], jnp.zeros((16 - table.shape[0], channels), jnp.float32)], axis=0)
    lines = jnp.concatenate(three_parts(lines) + (jnp.zeros((LANES - 48, channels), jnp.float32),), axis=0)
    feat = jnp.dot(kinds[...], lines.astype(jnp.bfloat16), preferred_element_type=jnp.float32)
    feat = feat + pot_of * field_w[...]
    proj = jnp.dot(feat[:EDGES].astype(jnp.bfloat16), msg[0], preferred_element_type=jnp.float32)
    proj = proj.astype(jnp.bfloat16).astype(jnp.float32)
    radial = radial_of(basis[...], radial_w[0])
    message = jnp.sum((radial * proj).reshape(ML_DEV, KNB, channels), axis=1) * (1.0 / KNB)
    update = jnp.dot(message.astype(jnp.bfloat16), mix[0], preferred_element_type=jnp.float32)
    feat1 = feat[EDGES : EDGES + ML_DEV] + update * lax.logistic(update)
    feat_out[:, :channels] = feat1
    feat_out[:, channels:] = jnp.broadcast_to(pot_of[EDGES : EDGES + ML_DEV], (ML_DEV, LANES))
    proj_out[...] = jnp.dot(feat1.astype(jnp.bfloat16), msg[1], preferred_element_type=jnp.float32).astype(jnp.bfloat16)


def first_layer(*args):
    channels = args[7].shape[1]
    smem = pl.BlockSpec(memory_space=pltpu.SMEM)
    vmem = pl.BlockSpec(memory_space=pltpu.VMEM)
    return pl.pallas_call(
        first_layer_kernel,
        out_shape=(
            jax.ShapeDtypeStruct((ML_DEV, channels + LANES), jnp.float32),
            jax.ShapeDtypeStruct((ML_DEV, channels), jnp.bfloat16),
        ),
        in_specs=[smem] + [vmem] * 9,
        out_specs=(vmem,) * 2,
        compiler_params=vmem_mib(20),
        name="first_layer",
    )(*args)


def fetch(sources, places, sems):
    copies = [pltpu.make_async_copy(src, dst, sems.at[i]) for i, (src, dst) in enumerate(zip(sources, places))]
    for copy in copies:
        copy.start()
    return copies


def second_layer_kernel(
    me, ids_in, basis_in, feat1, radial_in, mix_in, charge_w, energy_w, p0, p1, p2, p3, p4, p5, p6, p7,
    charge_out, energy_out, proj, ids, basis, feat_v, radial_w, mix, charge_v, energy_v, sems,
):
    parts = (p0, p1, p2, p3, p4, p5, p6, p7)
    size = p0.shape[0]
    copies = fetch(
        (ids_in, basis_in, feat1, radial_in, mix_in, charge_w, energy_w) + parts,
        [ids, basis, feat_v, radial_w, mix, charge_v, energy_v]
        + [proj.at[pl.ds(i * size, size)] for i in range(8)],
        sems,
    )
    copies[0].wait()
    part = 256
    mine = me[0]
    messages = []
    for m in range(EDGES // part):
        here = slice(m * part, (m + 1) * part)
        atom = ids[here, :]
        dev = (atom * 52429) >> 21
        t = atom - dev * ML_DEV
        far_c = (mine ^ dev) & 1
        far_z = ((mine >> 2) - (dev >> 2)) & 3
        far_x = ((mine >> 5) - (dev >> 5)) & 3
        row_of = lambda v: 2 * ((v >> 4) & 1) + ((v >> 1) & 1)
        far_y = (row_of(mine) - row_of(dev)) & 3
        place = ((far_c * 4 + far_y) * 16 + far_x * 4 + far_z) * ML_DEV + t
        pick = (lane_iota((part, 8 * size)) == place).astype(jnp.float32).astype(jnp.bfloat16)
        if m == 0:
            for copy in copies[1:]:
                copy.wait()
        rows = jnp.dot(pick, proj[...], preferred_element_type=jnp.float32)
        radial = radial_of(basis[here, :], radial_w[1])
        messages.append(jnp.sum((radial * rows).reshape(part // KNB, KNB, rows.shape[1]), axis=1) * (1.0 / KNB))
    message = jnp.concatenate(messages, axis=0).astype(jnp.bfloat16)
    update = jnp.dot(message, mix[1], preferred_element_type=jnp.float32)
    channels = update.shape[1]
    feat = feat_v[:, :channels] + update * lax.logistic(update)
    charge = jnp.tanh(jnp.sum(feat * charge_v[...], axis=1, keepdims=True))
    energy = jnp.sum(feat * energy_v[...], axis=1, keepdims=True) + charge * feat_v[:, channels : channels + 1]

    def as_row(column):
        square = jnp.broadcast_to(column, (ML_DEV, LANES))
        return jnp.concatenate([square, jnp.zeros((LANES - ML_DEV, LANES), jnp.float32)], axis=0).T

    charge_out[...] = as_row(charge)
    energy_out[...] = as_row(energy)[:1]


def second_layer(*args):
    smem = pl.BlockSpec(memory_space=pltpu.SMEM)
    vmem = pl.BlockSpec(memory_space=pltpu.VMEM)
    like = lambda a: pltpu.VMEM(a.shape, a.dtype)
    parts = args[8:]
    rows, channels = parts[0].shape
    return pl.pallas_call(
        second_layer_kernel,
        out_shape=(
            jax.ShapeDtypeStruct((NDEV, LANES), jnp.float32),
            pltpu.HBM((1, LANES), jnp.float32),
        ),
        in_specs=[smem] + [pl.BlockSpec(memory_space=pltpu.HBM)] * 15,
        out_specs=(vmem,) * 2,
        scratch_shapes=[pltpu.VMEM((8 * rows, channels), jnp.bfloat16)]
        + [like(a) for a in args[1:8]]
        + [pltpu.SemaphoreType.DMA((15,))],
        compiler_params=vmem_mib(24),
        name="second_layer",
    )(*args)


def embed_kernel(scale, mm, tab, charges, blocks_in, count_in, atoms_in, slots_in, *rest):
    pieces, (out, c8, left, total, blocks, count, atoms, slots, sems) = rest[:-9], rest[-9:]
    begins = [sum(piece.shape[1] for piece in pieces[:i]) for i in range(len(pieces))]
    copies = fetch(
        (atoms_in, slots_in, blocks_in, count_in) + pieces,
        [atoms, slots, blocks, count]
        + [out.at[:, pl.ds(begin, piece.shape[1])] for begin, piece in zip(begins, pieces)],
        sems,
    )
    turned = tab[:, :LANES].T
    charge = charges[...].T[:ML_DEV]
    c8[...] = jnp.zeros_like(c8)
    c8[pl.ds(0, ML_DEV, stride=8), :] = charge
    for c in range(3):
        c8[pl.ds(c + 1, ML_DEV, stride=8), :] = charge * turned[ML_DEV * c : ML_DEV * (c + 1)]

    def charge_tile(t, carry):
        one, two, _ = three_parts(c8[pl.ds(pl.multiple_of(t * 8, 8), 8), :])
        left[:, pl.ds(pl.multiple_of(t * LANES, LANES), LANES)] = jnp.concatenate([one, two], axis=0).astype(
            jnp.bfloat16
        )
        return carry

    lax.fori_loop(0, ML_DEV, charge_tile, 0)
    nslots = blocks.shape[1]
    total[...] = jnp.zeros_like(total)
    copies[0].wait()
    copies[1].wait()

    def tile(i, carry):
        cols = pl.ds(pl.multiple_of(i * 256, 256), 256)
        some = atoms[:, cols]
        lhs = left[:, cols]
        for s in range(nslots // 2):
            inv = lax.rsqrt(rows0(some, slots[:, s * 256 : (s + 1) * 256]))
            cube = inv * inv * inv
            high = cube.astype(jnp.bfloat16)
            low = (cube - high.astype(jnp.float32)).astype(jnp.bfloat16)
            total[:, s * 256 : (s + 1) * 256] += jnp.dot(lhs, high, preferred_element_type=jnp.float32) + jnp.dot(
                lhs, low, preferred_element_type=jnp.float32
            )
        return carry

    lax.fori_loop(0, ML_DEV // 2, tile, 0, unroll=10)
    for copy in copies[2:]:
        copy.wait()
    for s in range(nslots):
        here = pl.ds(pl.multiple_of(blocks[0, s] * LANES, LANES), LANES)
        rows = mm[:, here]
        q = rows[3:4] * (scale * jnp.where(s < count[0], 1.0, 0.0))
        sums = total[:, s * LANES : (s + 1) * LANES]
        sums = sums[:8] + sums[8:]
        out[:, here] += q * (rows[:3] * sums[0:1] - sums[1:4])


def embed(blocks, count, mm, tab, charges, atoms, slots, pieces, scale):
    vmem = pl.BlockSpec(memory_space=pltpu.VMEM)
    return pl.pallas_call(
        functools.partial(embed_kernel, scale),
        out_shape=jax.ShapeDtypeStruct((3, mm.shape[1]), jnp.float32),
        in_specs=[vmem] * 3 + [pl.BlockSpec(memory_space=pltpu.HBM)] * (4 + len(pieces)),
        out_specs=vmem,
        scratch_shapes=[
            pltpu.VMEM((8 * ML_DEV, LANES), jnp.float32),
            pltpu.VMEM((16, ML_DEV * LANES), jnp.bfloat16),
            pltpu.VMEM((16, slots.shape[1]), jnp.float32),
            pltpu.SMEM(blocks.shape, blocks.dtype),
            pltpu.SMEM(count.shape, count.dtype),
            pltpu.VMEM(atoms.shape, atoms.dtype),
            pltpu.VMEM(slots.shape, slots.dtype),
            pltpu.SemaphoreType.DMA((4 + len(pieces),)),
        ],
        compiler_params=vmem_mib(12),
        name="embed_forces",
    )(mm, tab, charges, blocks, count, atoms, slots, *pieces)


def ring_parts(value, axis):
    n = lax.axis_size(axis)
    return [value] + [lax.ppermute(value, axis, [(i, (i + k) % n) for i in range(n)]) for k in range(1, n)]


def stand(value, zero):
    return value + zero[:, : value.shape[1]].astype(value.dtype)


def body(
    mm_atoms,
    neighbours,
    embed_blocks,
    embed_count,
    ml_coords,
    ml_species,
    ml_edges,
    species_table,
    field_weight,
    msg_weight,
    radial_weight,
    mix_weight,
    charge_weight,
    energy_weight,
):
    own_rows = mm_atoms.shape[1]
    kappa = 4.0 / math.sqrt(NDEV * ML_DEV)
    kappa_field = 3.0 / math.sqrt(NDEV * embed_blocks.shape[1] * LANES)
    me = lax.axis_index(ALL)[None]
    tab = lax.all_to_all(spread(ml_coords, ml_species[None]), ALL, 0, 0, tiled=True)
    tab = tab.reshape(NDEV, 2 * LANES)
    ids = ml_edges.reshape(-1, 1)
    blocks = own_rows // LANES
    cuts = (0, 12, 48, 56, 64, 72, 88, blocks - 12, blocks)
    far = ml_coords

    def pairs(i, after, before=far, behind=far):
        return pair_forces(cuts[i], cuts[i + 1] - cuts[i], before, mm_atoms, behind, neighbours, after)

    pieces = [None] * (len(cuts) - 1)
    pieces[1], zero = pairs(1, far)
    pot, atoms, slots = field(embed_blocks, embed_count, mm_atoms, tab, pieces[1], kappa_field)
    basis, kinds, zero = geometry(me, ids, tab, pot)
    pot = stand(functools.reduce(jnp.add, ring_parts(pot, "z")), zero)
    for i, axis in ((2, Y), (3, "x")):
        pieces[i], zero = pairs(i, pot)
        pot = stand(functools.reduce(jnp.add, ring_parts(pot, axis)), zero)
    pot = functools.reduce(jnp.add, ring_parts(pot, "c"))
    feat1, proj = first_layer(
        me, ids, pot, basis, kinds, species_table, field_weight[None], msg_weight, radial_weight, mix_weight
    )
    for i, axis in ((4, "z"), (5, "x")):
        pieces[i], zero = pairs(i, proj)
        proj = stand(jnp.concatenate(ring_parts(proj, axis), axis=0), zero)
    halo = HALO_BLOCKS * LANES
    up = [(i, (i + 1) % NDEV) for i in range(NDEV)]
    down = [(j, i) for i, j in up]
    before = lax.ppermute(stand(mm_atoms[:, own_rows - halo :], zero), ALL, up)
    behind = lax.ppermute(stand(mm_atoms[:, :halo], zero), ALL, down)
    pieces[6], zero = pairs(6, proj)
    parts = ring_parts(proj, Y)
    parts[1:] = [stand(part, zero) for part in parts[1:]]
    parts = parts + [ring_parts(part, "c")[1] for part in parts]
    charges, energy = second_layer(
        me,
        ids,
        basis,
        feat1,
        radial_weight,
        mix_weight,
        charge_weight[None],
        energy_weight[None],
        *parts,
    )
    for i in (0, 7):
        pieces[i], _ = pairs(i, charges, before, behind)
    charges = lax.all_to_all(charges, ALL, 0, 0, tiled=True)
    mm_force = embed(embed_blocks, embed_count, mm_atoms, tab, charges, atoms, slots, pieces, kappa)
    return (energy[0, :ML_DEV], mm_force)


def solution(mesh):
    fine = Mesh(mesh.devices.reshape(4, 2, 4, 2, 2), ALL)
    in_specs = (
        P(None, ALL),
        P(None, ALL),
        P(ALL, None),
        P(ALL),
        P(None, ALL),
        P(ALL),
        P(ALL, None),
        P(),
        P(),
        P(),
        P(),
        P(),
        P(),
        P(),
    )
    out_specs = (P(ALL), P(None, ALL))
    return jax.shard_map(body, mesh=fine, in_specs=in_specs, out_specs=out_specs, check_vma=False)
```

time: 2200 us -> 130 us (0.06)
  local copies, waits for them, and re-layouts: 998 us -> 5.21 us
  waiting for transfers between devices: 940 us -> 14.8 us
  blocking collectives: 178 us -> 0 us
  starting transfers between devices: 1.97 us -> 55.8 us
  Pallas kernels: 0 us -> 51.8 us
  other arithmetic: 51.6 us -> 0.19 us
    gather x6 -> x0, local copies, waits for them, and re-layouts: 950 us -> none  [the longest x2 935 us: body(): partner = extended[:, neighbours]]
    unnamed x5 -> x0, waiting for transfers between devices: 738 us -> none
    all_gather x3 -> x0, waiting for transfers between devices: 202 us -> none  [the longest x1 197 us: body(): lax.all_gather(chosen, ('slab', 'sub'), axis=1, tiled=True)]
    all_gather x1 -> x0, blocking collectives: 178 us -> none  [body(): lax.all_gather(ml_coords, ('slab', 'sub'), axis=1, tiled=True)]
    pallas_call x0 -> x14, Pallas kernels: none -> 51.8 us  [the longest x8 24.9 us: pair_forces(): pl.pallas_call(functools.partial(pair_kernel, first, count), grid=(count...]
    reduce_sum x5 -> x0, other arithmetic: 40.7 us -> none  [the longest x1 25.8 us: slot_forces(): jnp.sum(weighted * gap, axis=0)]
    ppermute x2 -> x25, starting transfers between devices: 1.63 us -> 35 us  [the longest x23 34.4 us: ring_parts(): lax.ppermute(value, axis, [(i, (i + k) % n) for i in range(n)])]
    unnamed x54 -> x34, local copies, waits for them, and re-layouts: 34.4 us -> 3.96 us
  transfers between devices with their start and end apart: 6 -> 27, of which waited for: 3 -> 13; matrix products, arithmetic and copies ran while one was open for 44% -> 1% of each run, Pallas kernels for 0% -> 26%
where the time goes in v1:
time: 130 us
  starting transfers between devices  55.8 us (43%)
  Pallas kernels  51.8 us (40%)
  waiting for transfers between devices  14.8 us (11%)
  local copies, waits for them, and re-layouts  5.21 us (4%)
  between operations  1.81 us (1%)
    ppermute x23, starting transfers between devices, ring_parts(): lax.ppermute(value, axis, [(i, (i + k) % n) for i in range(n)])  34.4 us
    pallas_call x8, Pallas kernels, pair_forces(): pl.pallas_call(functools.partial(pair_kernel, first, count), grid=(count...  24.9 us
    all_to_all x1, starting transfers between devices, body(): lax.all_to_all(spread(ml_coords, ml_species[None]), ALL, 0, 0, tiled=True)  11.5 us
    ppermute x23, waiting for transfers between devices, ring_parts(): lax.ppermute(value, axis, [(i, (i + k) % n) for i in range(n)])  9.73 us
    all_to_all x1, starting transfers between devices, body(): charges = lax.all_to_all(charges, ALL, 0, 0, tiled=True)  9.26 us
    pallas_call x1, Pallas kernels, embed(): pl.pallas_call(functools.partial(embed_kernel, scale), out_shape=jax.Shap...  8.22 us
    pallas_call x1, Pallas kernels, second_layer(): pl.pallas_call(second_layer_kernel, out_shape=(jax.ShapeDtypeStruct((NDEV...  7.22 us
    pallas_call x1, Pallas kernels, field(): pl.pallas_call(functools.partial(field_kernel, scale), out_shape=(jax.Sha...  5.2 us
  transfers between devices with their start and end apart: 27, of which 13 were waited for; matrix products, arithmetic and copies ran while one was open for 1% of the time, Pallas kernels for 26%

profile of v1, /device:TPU:1, one launch (start us, length us, event | category | flops | bytes accessed | tf_op | source)
XLA Modules:
  0.0 129.6 jit_solution(11630073062191768852)
XLA Ops:
  0.6 1.5 %spread.1 = f32[128,1,256]{2,1,0:T(1,128)} custom-call(f32[3,40]{1,0:T(4,128)} %right.11, s32[1,40]{1,0:T(1,128)} %bitcast.29), custom_call_target="tpu_custom_call" | custom-call | tf_op jit(solution)/shard_map/spread/pallas_call | solution.py:122
  2.1 11.5 %all-to-all-start = ((f32[128,1,256]{2,1,0:T(1,128)}), f32[128,1,256]{2,1,0:T(1,128)S(1)}, u32[]{:S(2)}, u32[]{:S(2)}) async-start(f32[128,1,256]{2,1,0:T(1,128)} %spread.1), calls=%async_computation | async-start | bytes 262144 | tf_op jit(solution)/shard_map/all_to_all | solution.py:508
  14.3 0.0 copy-start
  14.3 1.2 copy-done
  15.5 6.6 %pair_forces.8 = (f32[3,4608]{1,0:T(4,128)S(1)}, f32[1,1024]{1,0:T(1,128)}) custom-call(f32[3,40]{1,0:T(4,128)S(1)} %copy-done.6, f32[4,16384]{1,0:T(4,128)S(1)} %copy-done.2, f32[3,40]{1,0:T(4,128)S(1)} %copy-done.6, s32[16,16384]{1,0:T(8,128)S(1)} %copy-done, f32[3,40]{1,0:T(4,128)S(1)} %copy-done.6), custom_call_target="tpu_custom_call" | custom-call | flops 360000000 | bytes 589824 | tf_op jit(solution)/shard_map/pair_forces/pallas_call | solution.py:87
  22.2 1.7 %all-to-all-done = f32[128,1,256]{2,1,0:T(1,128)S(1)} async-done(((f32[128,1,256]{2,1,0:T(1,128)}), f32[128,1,256]{2,1,0:T(1,128)S(1)}, u32[]{:S(2)}, u32[]{:S(2)}) %all-to-all-start) | async-done | bytes 131104 | tf_op jit(solution)/shard_map/all_to_all | solution.py:508
  23.9 0.6 copy-done.10
  24.5 5.2 %field.1 = (f32[40,128]{1,0:T(8,128)S(1)}, bf16[48,5120]{1,0:T(8,128)(2,1)}, bf16[48,1024]{1,0:T(8,128)(2,1)}) custom-call(s32[1,8]{1,0:T(1,128)S(1)} %copy-done.10, s32[1]{0:T(128)S(6)} %copy.31.count.count_in, f32[4,16384]{1,0:T(4,128)S(1)} %copy-done.2, f32[128,256]{1,0:T(8,128)S(1)} %bitcast.20, f32[3,4608]{1,0:T(4,128)S(1)} %get-tuple-element.25.after.rest_1_), custom_call_target="tpu_custom_call" | custom-call | tf_op jit(solution)/shard_map/field/pallas_call | solution.py:189
  29.7 0.6 collective-permute-start
  30.3 2.2 %collective-permute-start.1 = (f32[40,128]{1,0:T(8,128)S(1)}, f32[40,128]{1,0:T(8,128)S(1)}, u32[]{:S(2)}, u32[]{:S(2)}) collective-permute-start(f32[40,128]{1,0:T(8,128)S(1)} %get-tuple-element.26.after), channel_id=1, source_target_pairs={{0,8},{4,12},{8,0},{12,4},{1,9},{5,13},{9,1},{13,5},{2,10},{6,14},... | collective-permute-start | bytes 61448 | tf_op jit(solution)/shard_map/ppermute | solution.py:481
  32.6 0.9 collective-permute-start.2
  33.5 0.1 copy.23
  33.6 0.7 reshape.14.ids.ids_in
  34.3 2.9 %geometry.1 = (bf16[1280,128]{1,0:T(8,128)(2,1)S(1)}, bf16[1344,128]{1,0:T(8,128)(2,1)S(1)}, f32[1,128]{1,0:T(1,128)S(1)}) custom-call(s32[1]{0:T(128)} %bitcast.me, s32[1280,1]{1,0:T(8,128)S(1)} %reshape.14.ids.ids_in, f32[128,256]{1,0:T(8,128)S(1)} %bitcast.21, f32[40,128]{1,0:T(8,128)S(1)} %get-tuple-element.26.after), custom_call_target="tpu_custom_call" | custom-call | tf_op jit(solution)/shard_map/geometry/pallas_call | solution.py:262
  37.2 1.6 %pair_forces.9 = (f32[3,1024]{1,0:T(4,128)S(1)}, f32[1,1024]{1,0:T(1,128)S(1)}) custom-call(f32[3,40]{1,0:T(4,128)S(1)} %copy-done.6, f32[4,16384]{1,0:T(4,128)S(1)} %copy-done.2, f32[3,40]{1,0:T(4,128)S(1)} %copy-done.6, s32[16,16384]{1,0:T(8,128)S(1)} %copy-done.1, f32[40,128]{1,0:T(8,128)S(1)} %add_add_fusion.2.after), custom_call_target="tpu_custom_call" | custom-call | flops 80000000 | bytes 131072 | tf_op jit(solution)/shard_map/pair_forces/pallas_call | solution.py:87
  38.8 1.3 %collective-permute-start.3 = (f32[40,128]{1,0:T(8,128)S(1)}, f32[40,128]{1,0:T(8,128)S(1)}, u32[]{:S(2)}, u32[]{:S(2)}) collective-permute-start(f32[40,128]{1,0:T(8,128)S(1)} %add_add_fusion.2.after), channel_id=1, source_target_pairs={{0,2},{2,16},{16,18},{18,0},{1,3},{3,17},{17,19},{19,1},{4,6},{6,2... | collective-permute-start | bytes 61448 | tf_op jit(solution)/shard_map/ppermute | solution.py:481
  40.1 2.5 %collective-permute-start.4 = (f32[40,128]{1,0:T(8,128)S(1)}, f32[40,128]{1,0:T(8,128)S(1)}, u32[]{:S(2)}, u32[]{:S(2)}) collective-permute-start(f32[40,128]{1,0:T(8,128)S(1)} %add_add_fusion.2.after), channel_id=1, source_target_pairs={{0,16},{2,18},{16,0},{18,2},{1,17},{3,19},{17,1},{19,3},{4,20},{6,... | collective-permute-start | bytes 61448 | tf_op jit(solution)/shard_map/ppermute | solution.py:481
  42.6 1.1 collective-permute-start.5
  43.7 0.5 collective-permute-done.4
  44.2 1.5 %collective-permute-done.5 = f32[40,128]{1,0:T(8,128)S(1)} collective-permute-done((f32[40,128]{1,0:T(8,128)S(1)}, f32[40,128]{1,0:T(8,128)S(1)}, u32[]{:S(2)}, u32[]{:S(2)}) %collective-permute-start.5) | collective-permute-done | bytes 20512 | tf_op jit(solution)/shard_map/ppermute | solution.py:481
  45.7 1.3 collective-permute-start.6
  47.0 2.4 %collective-permute-start.7 = (f32[40,128]{1,0:T(8,128)S(1)}, f32[40,128]{1,0:T(8,128)S(1)}, u32[]{:S(2)}, u32[]{:S(2)}) collective-permute-start(f32[40,128]{1,0:T(8,128)S(1)} %add_add_fusion.1.after), channel_id=1, source_target_pairs={{0,64},{32,96},{64,0},{96,32},{1,65},{33,97},{65,1},{97,33},{2,66}... | collective-permute-start | bytes 61448 | tf_op jit(solution)/shard_map/ppermute | solution.py:481
  49.4 1.2 collective-permute-start.8
  50.6 1.6 %pair_forces.10 = (f32[3,1024]{1,0:T(4,128)S(1)}, f32[1,1024]{1,0:T(1,128)S(1)}) custom-call(f32[3,40]{1,0:T(4,128)S(1)} %copy-done.6, f32[4,16384]{1,0:T(4,128)S(1)} %copy-done.2, f32[3,40]{1,0:T(4,128)S(1)} %copy-done.6, s32[16,16384]{1,0:T(8,128)S(1)} %copy-done.1, f32[40,128]{1,0:T(8,128)S(1)} %add_add_fusion.1.after), custom_call_target="tpu_custom_call" | custom-call | flops 80000000 | bytes 131072 | tf_op jit(solution)/shard_map/pair_forces/pallas_call | solution.py:87
  52.2 0.2 collective-permute-done.8
  52.4 3.9 %collective-permute-start.9 = (f32[40,128]{1,0:T(8,128)S(1)}, f32[40,128]{1,0:T(8,128)S(1)}, u32[]{:S(2)}, u32[]{:S(2)}) collective-permute-start(f32[40,128]{1,0:T(8,128)S(1)} %add_add_fusion), channel_id=1, source_target_pairs={{0,1},{1,0},{2,3},{3,2},{4,5},{5,4},{6,7},{7,6},{8,9},{9,8},{10,11... | collective-permute-start | bytes 61448 | tf_op jit(solution)/shard_map/ppermute | solution.py:481
  56.3 0.8 collective-permute-done.9
  57.2 0.6 copy-done.11
  57.8 1.9 %first_layer.1 = (f32[40,384]{1,0:T(8,128)S(1)}, bf16[40,256]{1,0:T(8,128)(2,1)S(1)}) custom-call(s32[1]{0:T(128)} %bitcast.me, s32[1280,1]{1,0:T(8,128)S(1)} %reshape.14.ids.ids_in, f32[40,128]{1,0:T(8,128)S(1)} %add.152.pot, bf16[1280,128]{1,0:T(8,128)(2,1)S(1)} %get-tuple-element.27.basis.basis_in, bf16[1344,128]{1,0:T(8,128)(2,1)S(1)} %get-tuple-element.31.kinds, ...), custom_call_target="tpu_custom_call" | custom-call | tf_op jit(solution)/shard_map/first_layer/pallas_call | solution.py:311
  59.8 0.6 collective-permute-start.10
  60.3 1.7 %collective-permute-start.11 = (bf16[40,256]{1,0:T(8,128)(2,1)S(1)}, bf16[40,256]{1,0:T(8,128)(2,1)S(1)}, u32[]{:S(2)}, u32[]{:S(2)}) collective-permute-start(bf16[40,256]{1,0:T(8,128)(2,1)S(1)} %get-tuple-element.33.after), channel_id=1, source_target_pairs={{0,8},{4,12},{8,0},{12,4},{1,9},{5,13},{9,1},{13,5},{2,10},{6,14},... | collective-permute-start | bytes 61448 | tf_op jit(solution)/shard_map/ppermute | solution.py:481
  62.0 1.0 collective-permute-start.12
  63.0 1.6 %pair_forces.11 = (f32[3,1024]{1,0:T(4,128)S(1)}, f32[1,1024]{1,0:T(1,128)S(1)}) custom-call(f32[3,40]{1,0:T(4,128)S(1)} %copy-done.6, f32[4,16384]{1,0:T(4,128)S(1)} %copy-done.2, f32[3,40]{1,0:T(4,128)S(1)} %copy-done.6, s32[16,16384]{1,0:T(8,128)S(1)} %copy-done.1, bf16[40,256]{1,0:T(8,128)(2,1)S(1)} %get-tuple-element.33.after), custom_call_target="tpu_custom_call" | custom-call | flops 80000000 | bytes 131072 | tf_op jit(solution)/shard_map/pair_forces/pallas_call | solution.py:87
  64.5 0.0 collective-permute-done.11
  64.6 0.4 collective-permute-done.12
  65.0 0.1 collective-permute-start.13
  65.0 3.5 %collective-permute-start.14 = (bf16[160,256]{1,0:T(8,128)(2,1)S(1)}, bf16[160,256]{1,0:T(8,128)(2,1)S(1)}, u32[]{:S(2)}, u32[]{:S(2)}) collective-permute-start(bf16[160,256]{1,0:T(8,128)(2,1)S(1)} %maximum_add_fusion.1.after), channel_id=1, source_target_pairs={{0,64},{32,96},{64,0},{96,32},{1,65},{33,97},{65,1},{97,33},{2,66}... | collective-permute-start | bytes 245768 | tf_op jit(solution)/shard_map/ppermute | solution.py:481
  68.6 3.0 %pair_forces.12 = (f32[3,2048]{1,0:T(4,128)S(1)}, f32[1,1024]{1,0:T(1,128)S(1)}) custom-call(f32[3,40]{1,0:T(4,128)S(1)} %copy-done.6, f32[4,16384]{1,0:T(4,128)S(1)} %copy-done.2, f32[3,40]{1,0:T(4,128)S(1)} %copy-done.6, s32[16,16384]{1,0:T(8,128)S(1)} %copy-done.1, bf16[160,256]{1,0:T(8,128)(2,1)S(1)} %maximum_add_fusion.1.after), custom_call_target="tpu_custom_call" | custom-call | flops 160000000 | bytes 262144 | tf_op jit(solution)/shard_map/pair_forces/pallas_call | solution.py:87
  71.6 0.7 collective-permute-done.15
  72.3 0.1 maximum_add_fusion.after.p0
  72.4 0.1 collective-permute-start.16
  72.5 3.5 %collective-permute-start.17 = (bf16[640,256]{1,0:T(8,128)(2,1)S(1)}, bf16[640,256]{1,0:T(8,128)(2,1)S(1)}, u32[]{:S(2)}, u32[]{:S(2)}) collective-permute-start(bf16[640,256]{1,0:T(8,128)(2,1)S(1)} %maximum_add_fusion.after.p0), channel_id=1, source_target_pairs={{0,16},{2,18},{16,0},{18,2},{1,17},{3,19},{17,1},{19,3},{4,20},{6,... | collective-permute-start | bytes 983048 | tf_op jit(solution)/shard_map/ppermute | solution.py:481
  76.0 3.6 %collective-permute-start.19 = (bf16[640,256]{1,0:T(8,128)(2,1)S(1)}, bf16[640,256]{1,0:T(8,128)(2,1)S(1)}, u32[]{:S(2)}, u32[]{:S(2)}) collective-permute-start(bf16[640,256]{1,0:T(8,128)(2,1)S(1)} %maximum_add_fusion.after.p0), channel_id=1, source_target_pairs={{0,1},{1,0},{2,3},{3,2},{4,5},{5,4},{6,7},{7,6},{8,9},{9,8},{10,11... | collective-permute-start | bytes 983048 | tf_op jit(solution)/shard_map/ppermute | solution.py:481
  79.6 5.2 %pair_forces.13 = (f32[3,3584]{1,0:T(4,128)S(1)}, f32[1,1024]{1,0:T(1,128)S(1)}) custom-call(f32[3,40]{1,0:T(4,128)S(1)} %copy-done.6, f32[4,16384]{1,0:T(4,128)S(1)} %copy-done.2, f32[3,40]{1,0:T(4,128)S(1)} %copy-done.6, s32[16,16384]{1,0:T(8,128)S(1)} %copy-done.1, bf16[640,256]{1,0:T(8,128)(2,1)S(1)} %maximum_add_fusion.after.p0), custom_call_target="tpu_custom_call" | custom-call | flops 280000000 | bytes 458752 | tf_op jit(solution)/shard_map/pair_forces/pallas_call | solution.py:87
  84.8 2.6 %collective-permute-done.17 = bf16[640,256]{1,0:T(8,128)(2,1)S(1)} collective-permute-done((bf16[640,256]{1,0:T(8,128)(2,1)S(1)}, bf16[640,256]{1,0:T(8,128)(2,1)S(1)}, u32[]{:S(2)}, u32[]{:S(2)}) %collective-permute-start.17) | collective-permute-done | bytes 327712 | tf_op jit(solution)/shard_map/ppermute | solution.py:481
  87.5 1.9 %collective-permute-done.18 = bf16[640,256]{1,0:T(8,128)(2,1)S(1)} collective-permute-done((bf16[640,256]{1,0:T(8,128)(2,1)S(1)}, bf16[640,256]{1,0:T(8,128)(2,1)S(1)}, u32[]{:S(2)}, u32[]{:S(2)}) %collective-permute-start.18) | collective-permute-done | bytes 327712 | tf_op jit(solution)/shard_map/ppermute | solution.py:481
  89.4 0.1 broadcast_add_fusion
  89.5 2.4 %collective-permute-start.20 = (bf16[640,256]{1,0:T(8,128)(2,1)S(1)}, bf16[640,256]{1,0:T(8,128)(2,1)S(1)}, u32[]{:S(2)}, u32[]{:S(2)}) collective-permute-start(bf16[640,256]{1,0:T(8,128)(2,1)S(1)} %get-tuple-element.52.p1), channel_id=1, source_target_pairs={{0,1},{1,0},{2,3},{3,2},{4,5},{5,4},{6,7},{7,6},{8,9},{9,8},{10,11... | collective-permute-start | bytes 983048 | tf_op jit(solution)/shard_map/ppermute | solution.py:481
  91.8 0.1 collective-permute-start.21
  91.9 0.4 collective-permute-start.22
  92.4 0.4 collective-permute-start.23
  92.8 0.2 collective-permute-start.24
  92.9 0.1 collective-permute-done.20.p5
  93.1 0.5 collective-permute-done.21.p6
  93.6 0.5 collective-permute-done.22.p7
  94.0 0.7 copy-done.12
  94.7 7.2 %second_layer.1 = (f32[128,128]{1,0:T(8,128)}, f32[1,128]{1,0:T(1,128)}) custom-call(s32[1]{0:T(128)} %bitcast.me, s32[1280,1]{1,0:T(8,128)S(1)} %reshape.14.ids.ids_in, bf16[1280,128]{1,0:T(8,128)(2,1)S(1)} %get-tuple-element.27.basis.basis_in, f32[40,384]{1,0:T(8,128)S(1)} %get-tuple-element.32.feat1, f32[2,8,256]{2,1,0:T(8,128)S(1)} %copy-done.8, ...), custom_call_target="tpu_custom_call" | custom-call | tf_op jit(solution)/shard_map/second_layer/pallas_call | solution.py:386
  101.9 9.3 %all-to-all-start.1 = ((f32[128,1,128]{2,1,0:T(1,128)}), f32[128,1,128]{2,1,0:T(1,128)S(1)}, u32[]{:S(2)}, u32[]{:S(2)}) async-start(f32[128,1,128]{2,1,0:T(1,128)} %bitcast.10), calls=%async_computation.1 | async-start | bytes 131072 | tf_op jit(solution)/shard_map/all_to_all | solution.py:555
  111.2 0.7 copy-done.15
  111.9 0.5 slice_bitcast_fusion
  112.4 2.7 %pair_forces.15 = (f32[3,1536]{1,0:T(4,128)S(1)}, f32[1,1024]{1,0:T(1,128)}) custom-call(f32[4,1024]{1,0:T(4,128)S(1)} %collective-permute-done.23.left, f32[4,16384]{1,0:T(4,128)S(1)} %copy-done.2, f32[4,1024]{1,0:T(4,128)S(1)} %collective-permute-done.24.right, s32[16,16384]{1,0:T(8,128)S(1)} %copy-done.1, f32[128,128]{1,0:T(8,128)} %get-tuple-element.38.after), custom_call_target="tpu_custom_call" | custom-call | flops 120000000 | bytes 196608 | tf_op jit(solution)/shard_map/pair_forces/pallas_call | solution.py:87
  115.1 2.7 %pair_forces.14 = (f32[3,1536]{1,0:T(4,128)S(1)}, f32[1,1024]{1,0:T(1,128)}) custom-call(f32[4,1024]{1,0:T(4,128)S(1)} %collective-permute-done.23.left, f32[4,16384]{1,0:T(4,128)S(1)} %copy-done.2, f32[4,1024]{1,0:T(4,128)S(1)} %collective-permute-done.24.right, s32[16,16384]{1,0:T(8,128)S(1)} %copy-done.1, f32[128,128]{1,0:T(8,128)} %get-tuple-element.38.after), custom_call_target="tpu_custom_call" | custom-call | flops 120000000 | bytes 196608 | tf_op jit(solution)/shard_map/pair_forces/pallas_call | solution.py:87
  117.7 3.4 %all-to-all-done.1 = f32[128,1,128]{2,1,0:T(1,128)S(1)} async-done(((f32[128,1,128]{2,1,0:T(1,128)}), f32[128,1,128]{2,1,0:T(1,128)S(1)}, u32[]{:S(2)}, u32[]{:S(2)}) %all-to-all-start.1) | async-done | bytes 65568 | tf_op jit(solution)/shard_map/all_to_all | solution.py:555
  121.2 8.2 %embed_forces.1 = f32[3,16384]{1,0:T(4,128)} custom-call(f32[4,16384]{1,0:T(4,128)S(1)} %copy-done.2, f32[128,256]{1,0:T(8,128)S(1)} %bitcast.22, f32[128,128]{1,0:T(8,128)S(1)} %bitcast.23, s32[1,8]{1,0:T(1,128)S(1)} %copy-done.10, s32[1]{0:T(128)S(6)} %copy.31.count.count_in, bf16[48,5120]{1,0:T(8,128)(2,1)S(1)} %copy-done.4, ...), custom_call_target="tpu_custom_call" | custom-call | tf_op jit(solution)/shard_map/embed_forces/pallas_call | solution.py:459
  (53 shorter events, 0.2 us)
Async XLA Ops:
  0.6 13.7 %copy-start.2 = (f32[4,16384]{1,0:T(4,128)S(1)}, f32[4,16384]{1,0:T(4,128)}, u32[]{:S(2)}) copy-start(f32[4,16384]{1,0:T(4,128)} %mm.3) | copy-start | bytes 786436
  2.1 12.2 %copy-start.6 = (f32[3,40]{1,0:T(4,128)S(1)}, f32[3,40]{1,0:T(4,128)}, u32[]{:S(2)}) copy-start(f32[3,40]{1,0:T(4,128)} %right.11) | copy-start | bytes 1444
  2.1 21.7 %all-to-all-start = ((f32[128,1,256]{2,1,0:T(1,128)}), f32[128,1,256]{2,1,0:T(1,128)S(1)}, u32[]{:S(2)}, u32[]{:S(2)}) async-start(f32[128,1,256]{2,1,0:T(1,128)} %spread.1), calls=%async_computation | async-start | bytes 262144 | tf_op jit(solution)/shard_map/all_to_all | solution.py:508
  14.3 1.2 copy-start
  23.8 0.7 copy-start.10
  23.9 9.6 %copy-start.14 = (s32[40,32]{0,1:T(8,128)S(1)}, s32[40,32]{0,1:T(8,128)}, u32[]{:S(2)}) copy-start(s32[40,32]{0,1:T(8,128)} %param.20) | copy-start | bytes 15364
  24.5 12.7 %copy-start.1 = (s32[16,16384]{1,0:T(8,128)S(1)}, s32[16,16384]{1,0:T(8,128)}, u32[]{:S(2)}) copy-start(s32[16,16384]{1,0:T(8,128)} %nb.15) | copy-start | bytes 3145732
  29.7 7.4 %collective-permute-start = (f32[40,128]{1,0:T(8,128)S(1)}, f32[40,128]{1,0:T(8,128)S(1)}, u32[]{:S(2)}, u32[]{:S(2)}) collective-permute-start(f32[40,128]{1,0:T(8,128)S(1)} %get-tuple-element.26.after), channel_id=1, source_target_pairs={{0,4},{4,8},{8,12},{12,0},{1,5},{5,9},{9,13},{13,1},{2,6},{6,10},{... | collective-permute-start | bytes 61448 | tf_op jit(solution)/shard_map/ppermute | solution.py:481
  30.3 6.8 %collective-permute-start.1 = (f32[40,128]{1,0:T(8,128)S(1)}, f32[40,128]{1,0:T(8,128)S(1)}, u32[]{:S(2)}, u32[]{:S(2)}) collective-permute-start(f32[40,128]{1,0:T(8,128)S(1)} %get-tuple-element.26.after), channel_id=1, source_target_pairs={{0,8},{4,12},{8,0},{12,4},{1,9},{5,13},{9,1},{13,5},{2,10},{6,14},... | collective-permute-start | bytes 61448 | tf_op jit(solution)/shard_map/ppermute | solution.py:481
  32.6 4.6 %collective-permute-start.2 = (f32[40,128]{1,0:T(8,128)S(1)}, f32[40,128]{1,0:T(8,128)S(1)}, u32[]{:S(2)}, u32[]{:S(2)}) collective-permute-start(f32[40,128]{1,0:T(8,128)S(1)} %get-tuple-element.26.after), channel_id=1, source_target_pairs={{0,12},{4,0},{8,4},{12,8},{1,13},{5,1},{9,5},{13,9},{2,14},{6,2},{... | collective-permute-start | bytes 61448 | tf_op jit(solution)/shard_map/ppermute | solution.py:481
  38.8 5.0 %collective-permute-start.3 = (f32[40,128]{1,0:T(8,128)S(1)}, f32[40,128]{1,0:T(8,128)S(1)}, u32[]{:S(2)}, u32[]{:S(2)}) collective-permute-start(f32[40,128]{1,0:T(8,128)S(1)} %add_add_fusion.2.after), channel_id=1, source_target_pairs={{0,2},{2,16},{16,18},{18,0},{1,3},{3,17},{17,19},{19,1},{4,6},{6,2... | collective-permute-start | bytes 61448 | tf_op jit(solution)/shard_map/ppermute | solution.py:481
  40.1 4.1 %collective-permute-start.4 = (f32[40,128]{1,0:T(8,128)S(1)}, f32[40,128]{1,0:T(8,128)S(1)}, u32[]{:S(2)}, u32[]{:S(2)}) collective-permute-start(f32[40,128]{1,0:T(8,128)S(1)} %add_add_fusion.2.after), channel_id=1, source_target_pairs={{0,16},{2,18},{16,0},{18,2},{1,17},{3,19},{17,1},{19,3},{4,20},{6,... | collective-permute-start | bytes 61448 | tf_op jit(solution)/shard_map/ppermute | solution.py:481
  42.6 3.1 %collective-permute-start.5 = (f32[40,128]{1,0:T(8,128)S(1)}, f32[40,128]{1,0:T(8,128)S(1)}, u32[]{:S(2)}, u32[]{:S(2)}) collective-permute-start(f32[40,128]{1,0:T(8,128)S(1)} %add_add_fusion.2.after), channel_id=1, source_target_pairs={{0,18},{2,0},{16,2},{18,16},{1,19},{3,1},{17,3},{19,17},{4,22},{6,... | collective-permute-start | bytes 61448 | tf_op jit(solution)/shard_map/ppermute | solution.py:481
  45.7 6.5 %collective-permute-start.6 = (f32[40,128]{1,0:T(8,128)S(1)}, f32[40,128]{1,0:T(8,128)S(1)}, u32[]{:S(2)}, u32[]{:S(2)}) collective-permute-start(f32[40,128]{1,0:T(8,128)S(1)} %add_add_fusion.1.after), channel_id=1, source_target_pairs={{0,32},{32,64},{64,96},{96,0},{1,33},{33,65},{65,97},{97,1},{2,34}... | collective-permute-start | bytes 61448 | tf_op jit(solution)/shard_map/ppermute | solution.py:481
  47.0 5.2 %collective-permute-start.7 = (f32[40,128]{1,0:T(8,128)S(1)}, f32[40,128]{1,0:T(8,128)S(1)}, u32[]{:S(2)}, u32[]{:S(2)}) collective-permute-start(f32[40,128]{1,0:T(8,128)S(1)} %add_add_fusion.1.after), channel_id=1, source_target_pairs={{0,64},{32,96},{64,0},{96,32},{1,65},{33,97},{65,1},{97,33},{2,66}... | collective-permute-start | bytes 61448 | tf_op jit(solution)/shard_map/ppermute | solution.py:481
  49.4 2.9 %collective-permute-start.8 = (f32[40,128]{1,0:T(8,128)S(1)}, f32[40,128]{1,0:T(8,128)S(1)}, u32[]{:S(2)}, u32[]{:S(2)}) collective-permute-start(f32[40,128]{1,0:T(8,128)S(1)} %add_add_fusion.1.after), channel_id=1, source_target_pairs={{0,96},{32,0},{64,32},{96,64},{1,97},{33,1},{65,33},{97,65},{2,98}... | collective-permute-start | bytes 61448 | tf_op jit(solution)/shard_map/ppermute | solution.py:481
  50.6 6.6 %copy-start.3 = (bf16[2,256,256]{2,1,0:T(8,128)(2,1)S(1)}, bf16[2,256,256]{2,1,0:T(8,128)(2,1)}, u32[]{:S(2)}) copy-start(bf16[2,256,256]{2,1,0:T(8,128)(2,1)} %mix_in.1) | copy-start | bytes 786436
  50.6 6.6 %copy-start.5 = (bf16[2,256,256]{2,1,0:T(8,128)(2,1)S(1)}, bf16[2,256,256]{2,1,0:T(8,128)(2,1)}, u32[]{:S(2)}) copy-start(bf16[2,256,256]{2,1,0:T(8,128)(2,1)} %msg.1) | copy-start | bytes 786436
  52.4 4.8 %copy-start.8 = (f32[2,8,256]{2,1,0:T(8,128)S(1)}, f32[2,8,256]{2,1,0:T(8,128)}, u32[]{:S(2)}) copy-start(f32[2,8,256]{2,1,0:T(8,128)} %radial_in.1) | copy-start | bytes 49156
  52.4 4.8 %copy-start.9 = (f32[10,256]{1,0:T(8,128)S(1)}, f32[10,256]{1,0:T(8,128)}, u32[]{:S(2)}) copy-start(f32[10,256]{1,0:T(8,128)} %table.1) | copy-start | bytes 30724
  52.4 4.8 %collective-permute-start.9 = (f32[40,128]{1,0:T(8,128)S(1)}, f32[40,128]{1,0:T(8,128)S(1)}, u32[]{:S(2)}, u32[]{:S(2)}) collective-permute-start(f32[40,128]{1,0:T(8,128)S(1)} %add_add_fusion), channel_id=1, source_target_pairs={{0,1},{1,0},{2,3},{3,2},{4,5},{5,4},{6,7},{7,6},{8,9},{9,8},{10,11... | collective-permute-start | bytes 61448 | tf_op jit(solution)/shard_map/ppermute | solution.py:481
  57.2 0.7 copy-start.11
  59.8 4.8 %collective-permute-start.10 = (bf16[40,256]{1,0:T(8,128)(2,1)S(1)}, bf16[40,256]{1,0:T(8,128)(2,1)S(1)}, u32[]{:S(2)}, u32[]{:S(2)}) collective-permute-start(bf16[40,256]{1,0:T(8,128)(2,1)S(1)} %get-tuple-element.33.after), channel_id=1, source_target_pairs={{0,4},{4,8},{8,12},{12,0},{1,5},{5,9},{9,13},{13,1},{2,6},{6,10},{... | collective-permute-start | bytes 61448 | tf_op jit(solution)/shard_map/ppermute | solution.py:481
  60.3 4.2 %collective-permute-start.11 = (bf16[40,256]{1,0:T(8,128)(2,1)S(1)}, bf16[40,256]{1,0:T(8,128)(2,1)S(1)}, u32[]{:S(2)}, u32[]{:S(2)}) collective-permute-start(bf16[40,256]{1,0:T(8,128)(2,1)S(1)} %get-tuple-element.33.after), channel_id=1, source_target_pairs={{0,8},{4,12},{8,0},{12,4},{1,9},{5,13},{9,1},{13,5},{2,10},{6,14},... | collective-permute-start | bytes 61448 | tf_op jit(solution)/shard_map/ppermute | solution.py:481
  62.0 2.9 %collective-permute-start.12 = (bf16[40,256]{1,0:T(8,128)(2,1)S(1)}, bf16[40,256]{1,0:T(8,128)(2,1)S(1)}, u32[]{:S(2)}, u32[]{:S(2)}) collective-permute-start(bf16[40,256]{1,0:T(8,128)(2,1)S(1)} %get-tuple-element.33.after), channel_id=1, source_target_pairs={{0,12},{4,0},{8,4},{12,8},{1,13},{5,1},{9,5},{13,9},{2,14},{6,2},{... | collective-permute-start | bytes 61448 | tf_op jit(solution)/shard_map/ppermute | solution.py:481
  65.0 6.7 %collective-permute-start.13 = (bf16[160,256]{1,0:T(8,128)(2,1)S(1)}, bf16[160,256]{1,0:T(8,128)(2,1)S(1)}, u32[]{:S(2)}, u32[]{:S(2)}) collective-permute-start(bf16[160,256]{1,0:T(8,128)(2,1)S(1)} %maximum_add_fusion.1.after), channel_id=1, source_target_pairs={{0,32},{32,64},{64,96},{96,0},{1,33},{33,65},{65,97},{97,1},{2,34}... | collective-permute-start | bytes 245768 | tf_op jit(solution)/shard_map/ppermute | solution.py:481
  65.0 6.6 %collective-permute-start.14 = (bf16[160,256]{1,0:T(8,128)(2,1)S(1)}, bf16[160,256]{1,0:T(8,128)(2,1)S(1)}, u32[]{:S(2)}, u32[]{:S(2)}) collective-permute-start(bf16[160,256]{1,0:T(8,128)(2,1)S(1)} %maximum_add_fusion.1.after), channel_id=1, source_target_pairs={{0,64},{32,96},{64,0},{96,32},{1,65},{33,97},{65,1},{97,33},{2,66}... | collective-permute-start | bytes 245768 | tf_op jit(solution)/shard_map/ppermute | solution.py:481
  68.6 3.8 %collective-permute-start.15 = (bf16[160,256]{1,0:T(8,128)(2,1)S(1)}, bf16[160,256]{1,0:T(8,128)(2,1)S(1)}, u32[]{:S(2)}, u32[]{:S(2)}) collective-permute-start(bf16[160,256]{1,0:T(8,128)(2,1)S(1)} %maximum_add_fusion.1.after), channel_id=1, source_target_pairs={{0,96},{32,0},{64,32},{96,64},{1,97},{33,1},{65,33},{97,65},{2,98}... | collective-permute-start | bytes 245768 | tf_op jit(solution)/shard_map/ppermute | solution.py:481
  72.4 12.4 %collective-permute-start.16 = (bf16[640,256]{1,0:T(8,128)(2,1)S(1)}, bf16[640,256]{1,0:T(8,128)(2,1)S(1)}, u32[]{:S(2)}, u32[]{:S(2)}) collective-permute-start(bf16[640,256]{1,0:T(8,128)(2,1)S(1)} %maximum_add_fusion.after.p0), channel_id=1, source_target_pairs={{0,2},{2,16},{16,18},{18,0},{1,3},{3,17},{17,19},{19,1},{4,6},{6,2... | collective-permute-start | bytes 983048 | tf_op jit(solution)/shard_map/ppermute | solution.py:481
  72.5 15.0 %collective-permute-start.17 = (bf16[640,256]{1,0:T(8,128)(2,1)S(1)}, bf16[640,256]{1,0:T(8,128)(2,1)S(1)}, u32[]{:S(2)}, u32[]{:S(2)}) collective-permute-start(bf16[640,256]{1,0:T(8,128)(2,1)S(1)} %maximum_add_fusion.after.p0), channel_id=1, source_target_pairs={{0,16},{2,18},{16,0},{18,2},{1,17},{3,19},{17,1},{19,3},{4,20},{6,... | collective-permute-start | bytes 983048 | tf_op jit(solution)/shard_map/ppermute | solution.py:481
  76.0 13.4 %collective-permute-start.18 = (bf16[640,256]{1,0:T(8,128)(2,1)S(1)}, bf16[640,256]{1,0:T(8,128)(2,1)S(1)}, u32[]{:S(2)}, u32[]{:S(2)}) collective-permute-start(bf16[640,256]{1,0:T(8,128)(2,1)S(1)} %maximum_add_fusion.after.p0), channel_id=1, source_target_pairs={{0,18},{2,0},{16,2},{18,16},{1,19},{3,1},{17,3},{19,17},{4,22},{6,... | collective-permute-start | bytes 983048 | tf_op jit(solution)/shard_map/ppermute | solution.py:481
  76.0 16.8 %collective-permute-start.19 = (bf16[640,256]{1,0:T(8,128)(2,1)S(1)}, bf16[640,256]{1,0:T(8,128)(2,1)S(1)}, u32[]{:S(2)}, u32[]{:S(2)}) collective-permute-start(bf16[640,256]{1,0:T(8,128)(2,1)S(1)} %maximum_add_fusion.after.p0), channel_id=1, source_target_pairs={{0,1},{1,0},{2,3},{3,2},{4,5},{5,4},{6,7},{7,6},{8,9},{9,8},{10,11... | collective-permute-start | bytes 983048 | tf_op jit(solution)/shard_map/ppermute | solution.py:481
  89.4 4.6 %copy-start.13 = (f32[256]{0:T(256)S(1)}, f32[256]{0:T(256)}, u32[]{:S(2)}) copy-start(f32[256]{0:T(256)} %param.27) | copy-start | bytes 3076
  89.5 3.6 %collective-permute-start.20 = (bf16[640,256]{1,0:T(8,128)(2,1)S(1)}, bf16[640,256]{1,0:T(8,128)(2,1)S(1)}, u32[]{:S(2)}, u32[]{:S(2)}) collective-permute-start(bf16[640,256]{1,0:T(8,128)(2,1)S(1)} %get-tuple-element.52.p1), channel_id=1, source_target_pairs={{0,1},{1,0},{2,3},{3,2},{4,5},{5,4},{6,7},{7,6},{8,9},{9,8},{10,11... | collective-permute-start | bytes 983048 | tf_op jit(solution)/shard_map/ppermute | solution.py:481
  91.8 1.7 %collective-permute-start.21 = (bf16[640,256]{1,0:T(8,128)(2,1)S(1)}, bf16[640,256]{1,0:T(8,128)(2,1)S(1)}, u32[]{:S(2)}, u32[]{:S(2)}) collective-permute-start(bf16[640,256]{1,0:T(8,128)(2,1)S(1)} %get-tuple-element.51.p2), channel_id=1, source_target_pairs={{0,1},{1,0},{2,3},{3,2},{4,5},{5,4},{6,7},{7,6},{8,9},{9,8},{10,11... | collective-permute-start | bytes 983048 | tf_op jit(solution)/shard_map/ppermute | solution.py:481
  91.9 2.1 %collective-permute-start.22 = (bf16[640,256]{1,0:T(8,128)(2,1)S(1)}, bf16[640,256]{1,0:T(8,128)(2,1)S(1)}, u32[]{:S(2)}, u32[]{:S(2)}) collective-permute-start(bf16[640,256]{1,0:T(8,128)(2,1)S(1)} %get-tuple-element.50.p3), channel_id=1, source_target_pairs={{0,1},{1,0},{2,3},{3,2},{4,5},{5,4},{6,7},{7,6},{8,9},{9,8},{10,11... | collective-permute-start | bytes 983048 | tf_op jit(solution)/shard_map/ppermute | solution.py:481
  92.4 20.0 %collective-permute-start.23 = (f32[4,1024]{1,0:T(4,128)S(1)}, f32[4,1024]{1,0:T(4,128)S(1)}, u32[]{:S(2)}, u32[]{:S(2)}) collective-permute-start(f32[4,1024]{1,0:T(4,128)S(1)} %get-tuple-element.49), channel_id=1, source_target_pairs={{0,1},{1,2},{2,3},{3,4},{4,5},{5,6},{6,7},{7,8},{8,9},{9,10},{10,1... | collective-permute-start | bytes 49160 | tf_op jit(solution)/shard_map/ppermute | solution.py:536
  92.8 19.6 %collective-permute-start.24 = (f32[4,1024]{1,0:T(4,128)S(1)}, f32[4,1024]{1,0:T(4,128)S(1)}, u32[]{:S(2)}, u32[]{:S(2)}) collective-permute-start(f32[4,1024]{1,0:T(4,128)S(1)} %get-tuple-element.48), channel_id=1, source_target_pairs={{1,0},{2,1},{3,2},{4,3},{5,4},{6,5},{7,6},{8,7},{9,8},{10,9},{11,1... | collective-permute-start | bytes 49160 | tf_op jit(solution)/shard_map/ppermute | solution.py:537
  94.0 0.7 copy-start.12
  101.9 19.2 %all-to-all-start.1 = ((f32[128,1,128]{2,1,0:T(1,128)}), f32[128,1,128]{2,1,0:T(1,128)S(1)}, u32[]{:S(2)}, u32[]{:S(2)}) async-start(f32[128,1,128]{2,1,0:T(1,128)} %bitcast.10), calls=%async_computation.1 | async-start | bytes 131072 | tf_op jit(solution)/shard_map/all_to_all | solution.py:555
  111.2 0.7 copy-start.15
  115.1 6.1 %copy-start.4 = (bf16[48,5120]{1,0:T(8,128)(2,1)S(1)}, bf16[48,5120]{1,0:T(8,128)(2,1)}, u32[]{:S(2)}) copy-start(bf16[48,5120]{1,0:T(8,128)(2,1)} %get-tuple-element.39.atoms_in) | copy-start | bytes 1474564
  115.1 6.1 %copy-start.7 = (bf16[48,1024]{1,0:T(8,128)(2,1)S(1)}, bf16[48,1024]{1,0:T(8,128)(2,1)}, u32[]{:S(2)}) copy-start(bf16[48,1024]{1,0:T(8,128)(2,1)} %get-tuple-element.40.slots_in) | copy-start | bytes 294916

commit v2 on v1

--- a/solution.py
+++ b/solution.py
@@ -10,7 +10,7 @@
 from jax.sharding import PartitionSpec as P
 
 ALL = ("x", "yh", "z", "yl", "c")
-Y = ("yh", "yl")
+STAGES = ((2, 0, 1), (0, 1, 2))
 vmem_mib = lambda size: pltpu.CompilerParams(vmem_limit_bytes=size * 1024 * 1024)
 LANES = 128
 NDEV = 128
@@ -28,7 +28,8 @@
     )
 
 
-def pair_kernel(first, count, left, own, right, nb, after, out, zero, ext):
+def pair_kernel(first, count, left, own, right, nb, *rest):
+    out, zero, ext = rest[-3:]
     own_blocks = own.shape[1] // LANES
     step = pl.program_id(0)
 
@@ -96,7 +97,7 @@
             whole(own),
             whole(right),
             pl.BlockSpec((slots, wide), lambda i: (0, i + first // PAIR_STEP)),
-            pl.BlockSpec(memory_space=pl.ANY),
+            *[pl.BlockSpec(memory_space=pl.ANY)] * len(after),
         ],
         out_specs=(
             pl.BlockSpec((3, wide), lambda i: (0, i)),
@@ -108,7 +109,7 @@
             flops=count * 10**7, bytes_accessed=count * 16384, transcendentals=count * slots * LANES
         ),
         name="pair_forces",
-    )(left, own, right, neighbours, after)
+    )(left, own, right, neighbours, *after)
 
 
 def spread_kernel(coords, species, out):
@@ -136,7 +137,8 @@
     return one, two, three
 
 
-def field_kernel(scale, blocks, count, mm, tab, after, pot, atoms, slots, p8, qb):
+def field_kernel(scale, blocks_in, count_in, mm, tab, after, pot, atoms, slots, p8, qb, blocks, count, sems):
+    copies = fetch((blocks_in, count_in), (blocks, count), sems)
     turned = tab[:, :LANES].T
     x, y, z = (turned[ML_DEV * c : ML_DEV * (c + 1)] for c in range(3))
     p8[...] = jnp.zeros_like(p8)
@@ -151,6 +153,8 @@
         return carry
 
     lax.fori_loop(0, ML_DEV, atom_tile, 0)
+    for copy in copies:
+        copy.wait()
     nslots = blocks.shape[1]
     for s in range(nslots):
         rows = mm[:, pl.ds(pl.multiple_of(blocks[0, s] * LANES, LANES), LANES)]
@@ -184,7 +188,7 @@
 
 def field(blocks, count, mm, tab, after, scale):
     nslots = blocks.shape[1]
-    smem = pl.BlockSpec(memory_space=pltpu.SMEM)
+    hbm = pl.BlockSpec(memory_space=pltpu.HBM)
     vmem = pl.BlockSpec(memory_space=pltpu.VMEM)
     return pl.pallas_call(
         functools.partial(field_kernel, scale),
@@ -193,11 +197,14 @@
             pltpu.HBM((48, ML_DEV * LANES), jnp.bfloat16),
             pltpu.HBM((48, nslots * LANES), jnp.bfloat16),
         ),
-        in_specs=[smem, smem, vmem, vmem, pl.BlockSpec(memory_space=pl.ANY)],
+        in_specs=[hbm, hbm, vmem, vmem, pl.BlockSpec(memory_space=pl.ANY)],
         out_specs=(vmem,) * 3,
         scratch_shapes=[
             pltpu.VMEM((8 * ML_DEV, LANES), jnp.float32),
             pltpu.VMEM((nslots * LANES, LANES), jnp.float32),
+            pltpu.SMEM(blocks.shape, blocks.dtype),
+            pltpu.SMEM(count.shape, count.dtype),
+            pltpu.SemaphoreType.DMA((2,)),
         ],
         compiler_params=vmem_mib(10),
         name="field",
@@ -227,8 +234,9 @@
     return dev, atom - dev * ML_DEV
 
 
-def geometry_kernel(me, ids, tab, after, basis_out, kinds_out, zero):
+def geometry_kernel(me, ids, tab, field_w, charge_w, energy_w, after, basis_out, kinds_out, rows_out, zero):
     zero[...] = jnp.zeros_like(zero)
+    rows_out[...] = jnp.concatenate([field_w[...], charge_w[...], energy_w[...], field_w[...]], axis=0)
     dev, t = where_is(me[0], ids[...])
     at_dev = lane_iota((ROWS, LANES)) == dev
     rows = exact_pick(jnp.where(at_dev, 1.0, 0.0), tab[...])
@@ -256,7 +264,7 @@
     kinds_out[...] = jnp.where((kind == (lanes & 15)) & (lanes < 48), 1.0, 0.0).astype(jnp.bfloat16)
 
 
-def geometry(me, ids, tab, after):
+def geometry(me, ids, tab, field_w, charge_w, energy_w, after):
     smem = pl.BlockSpec(memory_space=pltpu.SMEM)
     vmem = pl.BlockSpec(memory_space=pltpu.VMEM)
     return pl.pallas_call(
@@ -264,13 +272,14 @@
         out_shape=(
             jax.ShapeDtypeStruct((EDGES, LANES), jnp.bfloat16),
             jax.ShapeDtypeStruct((ROWS, LANES), jnp.bfloat16),
+            jax.ShapeDtypeStruct((4, field_w.shape[1]), jnp.float32),
             jax.ShapeDtypeStruct((1, LANES), jnp.float32),
         ),
-        in_specs=[smem, vmem, vmem, pl.BlockSpec(memory_space=pl.ANY)],
-        out_specs=(vmem,) * 3,
+        in_specs=[smem] + [vmem] * 5 + [pl.BlockSpec(memory_space=pl.ANY)],
+        out_specs=(vmem,) * 4,
         compiler_params=vmem_mib(20),
         name="geometry",
-    )(me, ids, tab, after)
+    )(me, ids, tab, field_w, charge_w, energy_w, after)
 
 
 def radial_of(basis, weights):
@@ -292,7 +301,7 @@
     lines = jnp.concatenate([table[...], jnp.zeros((16 - table.shape[0], channels), jnp.float32)], axis=0)
     lines = jnp.concatenate(three_parts(lines) + (jnp.zeros((LANES - 48, channels), jnp.float32),), axis=0)
     feat = jnp.dot(kinds[...], lines.astype(jnp.bfloat16), preferred_element_type=jnp.float32)
-    feat = feat + pot_of * field_w[...]
+    feat = feat + pot_of * field_w[:1]
     proj = jnp.dot(feat[:EDGES].astype(jnp.bfloat16), msg[0], preferred_element_type=jnp.float32)
     proj = proj.astype(jnp.bfloat16).astype(jnp.float32)
     radial = radial_of(basis[...], radial_w[0])
@@ -329,14 +338,14 @@
 
 
 def second_layer_kernel(
-    me, ids_in, basis_in, feat1, radial_in, mix_in, charge_w, energy_w, p0, p1, p2, p3, p4, p5, p6, p7,
-    charge_out, energy_out, proj, ids, basis, feat_v, radial_w, mix, charge_v, energy_v, sems,
+    me, ids_in, basis_in, feat1, radial_in, mix_in, rows_in, p0, p1, p2, p3, p4, p5, p6, p7,
+    charge_out, energy_out, proj, ids, basis, feat_v, radial_w, mix, lines, sems,
 ):
     parts = (p0, p1, p2, p3, p4, p5, p6, p7)
     size = p0.shape[0]
     copies = fetch(
-        (ids_in, basis_in, feat1, radial_in, mix_in, charge_w, energy_w) + parts,
-        [ids, basis, feat_v, radial_w, mix, charge_v, energy_v]
+        (ids_in, basis_in, feat1, radial_in, mix_in, rows_in) + parts,
+        [ids, basis, feat_v, radial_w, mix, lines]
         + [proj.at[pl.ds(i * size, size)] for i in range(8)],
         sems,
     )
@@ -354,8 +363,12 @@
         far_x = ((mine >> 5) - (dev >> 5)) & 3
         row_of = lambda v: 2 * ((v >> 4) & 1) + ((v >> 1) & 1)
         far_y = (row_of(mine) - row_of(dev)) & 3
-        place = ((far_c * 4 + far_y) * 16 + far_x * 4 + far_z) * ML_DEV + t
-        pick = (lane_iota((part, 8 * size)) == place).astype(jnp.float32).astype(jnp.bfloat16)
+        odd = (dev & 1) == 1
+        far = (far_x, far_y, far_z)
+        k1, k2, k3 = (jnp.where(odd, far[STAGES[1][i]], far[STAGES[0][i]]) for i in range(3))
+        place = ((far_c * 4 + k3) * 16 + k2 * 4 + k1) * ML_DEV + t
+        same = lane_iota((part, 8 * size)).astype(jnp.int16) == place.astype(jnp.int16)
+        pick = jnp.where(same, jnp.bfloat16(1), jnp.bfloat16(0))
         if m == 0:
             for copy in copies[1:]:
                 copy.wait()
@@ -366,8 +379,8 @@
     update = jnp.dot(message, mix[1], preferred_element_type=jnp.float32)
     channels = update.shape[1]
     feat = feat_v[:, :channels] + update * lax.logistic(update)
-    charge = jnp.tanh(jnp.sum(feat * charge_v[...], axis=1, keepdims=True))
-    energy = jnp.sum(feat * energy_v[...], axis=1, keepdims=True) + charge * feat_v[:, channels : channels + 1]
+    charge = jnp.tanh(jnp.sum(feat * lines[1:2], axis=1, keepdims=True))
+    energy = jnp.sum(feat * lines[2:3], axis=1, keepdims=True) + charge * feat_v[:, channels : channels + 1]
 
     def as_row(column):
         square = jnp.broadcast_to(column, (ML_DEV, LANES))
@@ -381,7 +394,7 @@
     smem = pl.BlockSpec(memory_space=pltpu.SMEM)
     vmem = pl.BlockSpec(memory_space=pltpu.VMEM)
     like = lambda a: pltpu.VMEM(a.shape, a.dtype)
-    parts = args[8:]
+    parts = args[7:]
     rows, channels = parts[0].shape
     return pl.pallas_call(
         second_layer_kernel,
@@ -389,11 +402,11 @@
             jax.ShapeDtypeStruct((NDEV, LANES), jnp.float32),
             pltpu.HBM((1, LANES), jnp.float32),
         ),
-        in_specs=[smem] + [pl.BlockSpec(memory_space=pltpu.HBM)] * 15,
+        in_specs=[smem] + [pl.BlockSpec(memory_space=pltpu.HBM)] * 14,
         out_specs=(vmem,) * 2,
         scratch_shapes=[pltpu.VMEM((8 * rows, channels), jnp.bfloat16)]
-        + [like(a) for a in args[1:8]]
-        + [pltpu.SemaphoreType.DMA((15,))],
+        + [like(a) for a in args[1:7]]
+        + [pltpu.SemaphoreType.DMA((14,))],
         compiler_params=vmem_mib(24),
         name="second_layer",
     )(*args)
@@ -474,6 +487,20 @@
         compiler_params=vmem_mib(12),
         name="embed_forces",
     )(mm, tab, charges, blocks, count, atoms, slots, *pieces)
+
+
+def stage_parts(value, stage):
+    parts = [value]
+    for k in range(1, 4):
+        pairs = []
+        for dev in range(NDEV):
+            at = [dev >> 5, 2 * ((dev >> 4) & 1) + ((dev >> 1) & 1), (dev >> 2) & 3]
+            axis = STAGES[dev & 1][stage]
+            at[axis] = (at[axis] + k) % 4
+            x, y, z = at
+            pairs.append((dev, (x << 5) + ((y >> 1) << 4) + (z << 2) + ((y & 1) << 1) + (dev & 1)))
+        parts.append(lax.ppermute(value, ALL, pairs))
+    return parts
 
 
 def ring_parts(value, axis):
@@ -509,34 +536,36 @@
     tab = tab.reshape(NDEV, 2 * LANES)
     ids = ml_edges.reshape(-1, 1)
     blocks = own_rows // LANES
-    cuts = (0, 12, 48, 56, 64, 72, 88, blocks - 12, blocks)
+    cuts = (0, 12, 48, 56, 64, 80, blocks - 12, blocks)
     far = ml_coords
 
-    def pairs(i, after, before=far, behind=far):
+    def pairs(i, *after, before=far, behind=far):
         return pair_forces(cuts[i], cuts[i + 1] - cuts[i], before, mm_atoms, behind, neighbours, after)
 
     pieces = [None] * (len(cuts) - 1)
     pieces[1], zero = pairs(1, far)
     pot, atoms, slots = field(embed_blocks, embed_count, mm_atoms, tab, pieces[1], kappa_field)
-    basis, kinds, zero = geometry(me, ids, tab, pot)
-    pot = stand(functools.reduce(jnp.add, ring_parts(pot, "z")), zero)
-    for i, axis in ((2, Y), (3, "x")):
-        pieces[i], zero = pairs(i, pot)
-        pot = stand(functools.reduce(jnp.add, ring_parts(pot, axis)), zero)
+    basis, kinds, rows, zero = geometry(
+        me, ids, tab, field_weight[None], charge_weight[None], energy_weight[None], pot
+    )
+    pot = stand(functools.reduce(jnp.add, stage_parts(pot, 0)), zero)
+    pot = functools.reduce(jnp.add, stage_parts(pot, 1))
+    pieces[2], zero = pairs(2, pot)
+    pot = stand(functools.reduce(jnp.add, stage_parts(pot, 2)), zero)
     pot = functools.reduce(jnp.add, ring_parts(pot, "c"))
     feat1, proj = first_layer(
-        me, ids, pot, basis, kinds, species_table, field_weight[None], msg_weight, radial_weight, mix_weight
+        me, ids, pot, basis, kinds, species_table, rows, msg_weight, radial_weight, mix_weight
     )
-    for i, axis in ((4, "z"), (5, "x")):
+    for i, stage in ((3, 0), (4, 1)):
         pieces[i], zero = pairs(i, proj)
-        proj = stand(jnp.concatenate(ring_parts(proj, axis), axis=0), zero)
+        proj = stand(jnp.concatenate(stage_parts(proj, stage), axis=0), zero)
     halo = HALO_BLOCKS * LANES
     up = [(i, (i + 1) % NDEV) for i in range(NDEV)]
     down = [(j, i) for i, j in up]
     before = lax.ppermute(stand(mm_atoms[:, own_rows - halo :], zero), ALL, up)
     behind = lax.ppermute(stand(mm_atoms[:, :halo], zero), ALL, down)
-    pieces[6], zero = pairs(6, proj)
-    parts = ring_parts(proj, Y)
+    pieces[5], zero = pairs(5, proj)
+    parts = stage_parts(proj, 2)
     parts[1:] = [stand(part, zero) for part in parts[1:]]
     parts = parts + [ring_parts(part, "c")[1] for part in parts]
     charges, energy = second_layer(
@@ -546,12 +575,11 @@
         feat1,
         radial_weight,
         mix_weight,
-        charge_weight[None],
-        energy_weight[None],
+        rows,
         *parts,
     )
-    for i in (0, 7):
-        pieces[i], _ = pairs(i, charges, before, behind)
+    for i in (0, 6):
+        pieces[i], _ = pairs(i, charges, before=before, behind=behind)
     charges = lax.all_to_all(charges, ALL, 0, 0, tiled=True)
     mm_force = embed(embed_blocks, embed_count, mm_atoms, tab, charges, atoms, slots, pieces, kappa)
     return (energy[0, :ML_DEV], mm_force)

time: 130 us -> 123 us (0.946)
  waiting for transfers between devices: 14.8 us -> 10.3 us
    ppermute x23 -> x5, starting transfers between devices: 34.4 us -> 9.6 us  [ring_parts(): lax.ppermute(value, axis, [(i, (i + k) % n) for i in range(n)])]
    ppermute x0 -> x18, starting transfers between devices: none -> 23.7 us  [stage_parts(): parts.append(lax.ppermute(value, ALL, pairs))]
    ppermute x23 -> x5, waiting for transfers between devices: 9.73 us -> 1.88 us  [ring_parts(): lax.ppermute(value, axis, [(i, (i + k) % n) for i in range(n)])]
    ppermute x0 -> x18, waiting for transfers between devices: none -> 3.39 us  [stage_parts(): parts.append(lax.ppermute(value, ALL, pairs))]
    pallas_call x8 -> x7, Pallas kernels: 24.9 us -> 25.1 us  [pair_forces(): pl.pallas_call(functools.partial(pair_kernel, first, count), grid=(count...]
  transfers between devices with their start and end apart: 27 -> 27, of which waited for: 13 -> 11; matrix products, arithmetic and copies ran while one was open for 1% -> 1% of each run, Pallas kernels for 26% -> 28%
where the time goes in v2:
time: 123 us
  starting transfers between devices  54.5 us (44%)
  Pallas kernels  51 us (41%)
  waiting for transfers between devices  10.3 us (8%)
  local copies, waits for them, and re-layouts  5.2 us (4%)
  between operations  1.83 us (1%)
    pallas_call x7, Pallas kernels, pair_forces(): pl.pallas_call(functools.partial(pair_kernel, first, count), grid=(count...  25.1 us
    ppermute x18, starting transfers between devices, stage_parts(): parts.append(lax.ppermute(value, ALL, pairs))  23.7 us
    all_to_all x1, starting transfers between devices, body(): lax.all_to_all(spread(ml_coords, ml_species[None]), ALL, 0, 0, tiled=True)  11.5 us
    ppermute x5, starting transfers between devices, ring_parts(): lax.ppermute(value, axis, [(i, (i + k) % n) for i in range(n)])  9.6 us
    all_to_all x1, starting transfers between devices, body(): charges = lax.all_to_all(charges, ALL, 0, 0, tiled=True)  9.09 us
    pallas_call x1, Pallas kernels, embed(): pl.pallas_call(functools.partial(embed_kernel, scale), out_shape=jax.Shap...  8.21 us
    pallas_call x1, Pallas kernels, second_layer(): pl.pallas_call(second_layer_kernel, out_shape=(jax.ShapeDtypeStruct((NDEV...  6.72 us
    pallas_call x1, Pallas kernels, field(): pl.pallas_call(functools.partial(field_kernel, scale), out_shape=(jax.Sha...  4.69 us
  transfers between devices with their start and end apart: 27, of which 11 were waited for; matrix products, arithmetic and copies ran while one was open for 1% of the time, Pallas kernels for 28%

profile of v2, /device:TPU:1, one launch (start us, length us, event | category | flops | bytes accessed | tf_op | source)
XLA Modules:
  0.0 123.0 jit_solution(12892535538331003820)
XLA Ops:
  0.6 1.5 %spread.1 = f32[128,1,256]{2,1,0:T(1,128)} custom-call(f32[3,40]{1,0:T(4,128)} %right.9, s32[1,40]{1,0:T(1,128)} %bitcast.27), custom_call_target="tpu_custom_call" | custom-call | tf_op jit(solution)/shard_map/spread/pallas_call | solution.py:123
  2.1 11.5 %all-to-all-start = ((f32[128,1,256]{2,1,0:T(1,128)}), f32[128,1,256]{2,1,0:T(1,128)S(1)}, u32[]{:S(2)}, u32[]{:S(2)}) async-start(f32[128,1,256]{2,1,0:T(1,128)} %spread.1), calls=%async_computation | async-start | bytes 262144 | tf_op jit(solution)/shard_map/all_to_all | solution.py:535
  14.3 0.0 copy-start
  14.3 1.2 copy-done
  15.5 6.7 %pair_forces.7 = (f32[3,4608]{1,0:T(4,128)S(1)}, f32[1,1024]{1,0:T(1,128)}) custom-call(f32[3,40]{1,0:T(4,128)S(1)} %copy-done.6, f32[4,16384]{1,0:T(4,128)S(1)} %copy-done.2, f32[3,40]{1,0:T(4,128)S(1)} %copy-done.6, s32[16,16384]{1,0:T(8,128)S(1)} %copy-done, f32[3,40]{1,0:T(4,128)S(1)} %copy-done.6), custom_call_target="tpu_custom_call" | custom-call | flops 360000000 | bytes 589824 | tf_op jit(solution)/shard_map/pair_forces/pallas_call | solution.py:88
  22.3 1.6 %all-to-all-done = f32[128,1,256]{2,1,0:T(1,128)S(1)} async-done(((f32[128,1,256]{2,1,0:T(1,128)}), f32[128,1,256]{2,1,0:T(1,128)S(1)}, u32[]{:S(2)}, u32[]{:S(2)}) %all-to-all-start) | async-done | bytes 131104 | tf_op jit(solution)/shard_map/all_to_all | solution.py:535
  23.8 0.0 copy-start.10
  23.9 0.0 copy-start.14
  23.9 0.6 copy-done.10
  24.5 4.7 %field.1 = (f32[40,128]{1,0:T(8,128)S(1)}, bf16[48,5120]{1,0:T(8,128)(2,1)}, bf16[48,1024]{1,0:T(8,128)(2,1)}) custom-call(s32[1,8]{1,0:T(1,128)S(1)} %copy-done.10, s32[1]{0:T(128)S(6)} %copy.31.count_in, f32[4,16384]{1,0:T(4,128)S(1)} %copy-done.2, f32[128,256]{1,0:T(8,128)S(1)} %bitcast.18, f32[3,4608]{1,0:T(4,128)S(1)} %get-tuple-element.24.after.rest_1_), custom_call_target="tpu_custom_call" | custom-call | tf_op jit(solution)/shard_map/field/pallas_call | solution.py:193
  29.2 0.4 collective-permute-start
  29.6 1.9 %collective-permute-start.1 = (f32[40,128]{1,0:T(8,128)S(1)}, f32[40,128]{1,0:T(8,128)S(1)}, u32[]{:S(2)}, u32[]{:S(2)}) collective-permute-start(f32[40,128]{1,0:T(8,128)S(1)} %get-tuple-element.25.after), channel_id=1, source_target_pairs={{0,8},{1,65},{2,10},{3,67},{4,12},{5,69},{6,14},{7,71},{8,0},{9,73... | collective-permute-start | bytes 61448 | tf_op jit(solution)/shard_map/ppermute | solution.py:502
  31.5 1.2 collective-permute-start.2
  32.7 0.1 copy.23
  32.8 0.7 reshape.14.ids.ids_in
  33.5 0.0 copy-start.11
  33.5 0.7 copy-done.11
  34.2 2.9 %geometry.1 = (bf16[1280,128]{1,0:T(8,128)(2,1)S(1)}, bf16[1344,128]{1,0:T(8,128)(2,1)S(1)}, f32[4,256]{1,0:T(4,128)S(1)}, f32[1,128]{1,0:T(1,128)S(1)}) custom-call(s32[1]{0:T(128)} %bitcast.me, s32[1280,1]{1,0:T(8,128)S(1)} %reshape.14.ids.ids_in, f32[128,256]{1,0:T(8,128)S(1)} %bitcast.19, f32[1,256]{1,0:T(1,128)S(1)} %bitcast.23, f32[1,256]{1,0:T(1,128)S(1)} %bitcast.24, ...), custom_call_target="tpu_custom_call" | custom-call | tf_op jit(solution)/shard_map/geometry/pallas_call | solution.py:270
  37.0 0.0 collective-permute-done
  37.1 1.3 %collective-permute-start.3 = (f32[40,128]{1,0:T(8,128)S(1)}, f32[40,128]{1,0:T(8,128)S(1)}, u32[]{:S(2)}, u32[]{:S(2)}) collective-permute-start(f32[40,128]{1,0:T(8,128)S(1)} %add_add_fusion.2), channel_id=1, source_target_pairs={{0,32},{1,3},{2,34},{3,17},{4,36},{5,7},{6,38},{7,21},{8,40},{9,11... | collective-permute-start | bytes 61448 | tf_op jit(solution)/shard_map/ppermute | solution.py:502
  38.3 2.5 %collective-permute-start.4 = (f32[40,128]{1,0:T(8,128)S(1)}, f32[40,128]{1,0:T(8,128)S(1)}, u32[]{:S(2)}, u32[]{:S(2)}) collective-permute-start(f32[40,128]{1,0:T(8,128)S(1)} %add_add_fusion.2), channel_id=1, source_target_pairs={{0,64},{1,17},{2,66},{3,19},{4,68},{5,21},{6,70},{7,23},{8,72},{9,... | collective-permute-start | bytes 61448 | tf_op jit(solution)/shard_map/ppermute | solution.py:502
  40.8 1.1 collective-permute-start.5
  41.9 0.5 collective-permute-done.4
  42.5 1.0 collective-permute-done.5
  43.4 1.8 %collective-permute-start.6 = (f32[40,128]{1,0:T(8,128)S(1)}, f32[40,128]{1,0:T(8,128)S(1)}, u32[]{:S(2)}, u32[]{:S(2)}) collective-permute-start(f32[40,128]{1,0:T(8,128)S(1)} %add_add_fusion.1.rest_0_), channel_id=1, source_target_pairs={{0,2},{1,5},{2,16},{3,7},{4,6},{5,9},{6,20},{7,11},{8,10},{9,13},{... | collective-permute-start | bytes 61448 | tf_op jit(solution)/shard_map/ppermute | solution.py:502
  45.3 2.7 %collective-permute-start.7 = (f32[40,128]{1,0:T(8,128)S(1)}, f32[40,128]{1,0:T(8,128)S(1)}, u32[]{:S(2)}, u32[]{:S(2)}) collective-permute-start(f32[40,128]{1,0:T(8,128)S(1)} %add_add_fusion.1.rest_0_), channel_id=1, source_target_pairs={{0,16},{1,9},{2,18},{3,11},{4,20},{5,13},{6,22},{7,15},{8,24},{9,1... | collective-permute-start | bytes 61448 | tf_op jit(solution)/shard_map/ppermute | solution.py:502
  47.9 0.9 collective-permute-start.8
  48.8 1.6 %pair_forces.8 = (f32[3,1024]{1,0:T(4,128)S(1)}, f32[1,1024]{1,0:T(1,128)S(1)}) custom-call(f32[3,40]{1,0:T(4,128)S(1)} %copy-done.6, f32[4,16384]{1,0:T(4,128)S(1)} %copy-done.2, f32[3,40]{1,0:T(4,128)S(1)} %copy-done.6, s32[16,16384]{1,0:T(8,128)S(1)} %copy-done.1, f32[40,128]{1,0:T(8,128)S(1)} %add_add_fusion.1.rest_0_), custom_call_target="tpu_custom_call" | custom-call | flops 80000000 | bytes 131072 | tf_op jit(solution)/shard_map/pair_forces/pallas_call | solution.py:88
  50.5 0.4 collective-permute-done.8
  50.9 4.1 %collective-permute-start.9 = (f32[40,128]{1,0:T(8,128)S(1)}, f32[40,128]{1,0:T(8,128)S(1)}, u32[]{:S(2)}, u32[]{:S(2)}) collective-permute-start(f32[40,128]{1,0:T(8,128)S(1)} %add_add_fusion), channel_id=1, source_target_pairs={{0,1},{1,0},{2,3},{3,2},{4,5},{5,4},{6,7},{7,6},{8,9},{9,8},{10,11... | collective-permute-start | bytes 61448 | tf_op jit(solution)/shard_map/ppermute | solution.py:508
  55.0 0.8 collective-permute-done.9
  55.9 0.7 copy-done.8
  56.5 0.0 copy-done.9
  56.6 1.9 %first_layer.1 = (f32[40,384]{1,0:T(8,128)S(1)}, bf16[40,256]{1,0:T(8,128)(2,1)S(1)}) custom-call(s32[1]{0:T(128)} %bitcast.me, s32[1280,1]{1,0:T(8,128)S(1)} %reshape.14.ids.ids_in, f32[40,128]{1,0:T(8,128)S(1)} %add.139.pot, bf16[1280,128]{1,0:T(8,128)(2,1)S(1)} %get-tuple-element.26.basis.basis_in, bf16[1344,128]{1,0:T(8,128)(2,1)S(1)} %get-tuple-element.29.kinds, ...), custom_call_target="tpu_custom_call" | custom-call | tf_op jit(solution)/shard_map/first_layer/pallas_call | solution.py:320
  58.5 3.6 %collective-permute-start.11 = (bf16[40,256]{1,0:T(8,128)(2,1)S(1)}, bf16[40,256]{1,0:T(8,128)(2,1)S(1)}, u32[]{:S(2)}, u32[]{:S(2)}) collective-permute-start(bf16[40,256]{1,0:T(8,128)(2,1)S(1)} %get-tuple-element.32.rest_0_), channel_id=1, source_target_pairs={{0,8},{1,65},{2,10},{3,67},{4,12},{5,69},{6,14},{7,71},{8,0},{9,73... | collective-permute-start | bytes 61448 | tf_op jit(solution)/shard_map/ppermute | solution.py:502
  62.1 0.0 collective-permute-start.12
  62.1 1.6 %pair_forces.9 = (f32[3,1024]{1,0:T(4,128)S(1)}, f32[1,1024]{1,0:T(1,128)S(1)}) custom-call(f32[3,40]{1,0:T(4,128)S(1)} %copy-done.6, f32[4,16384]{1,0:T(4,128)S(1)} %copy-done.2, f32[3,40]{1,0:T(4,128)S(1)} %copy-done.6, s32[16,16384]{1,0:T(8,128)S(1)} %copy-done.1, bf16[40,256]{1,0:T(8,128)(2,1)S(1)} %get-tuple-element.32.rest_0_), custom_call_target="tpu_custom_call" | custom-call | flops 80000000 | bytes 131072 | tf_op jit(solution)/shard_map/pair_forces/pallas_call | solution.py:88
  63.7 1.0 collective-permute-done.12
  64.7 0.1 collective-permute-start.13
  64.8 3.5 %collective-permute-start.14 = (bf16[160,256]{1,0:T(8,128)(2,1)S(1)}, bf16[160,256]{1,0:T(8,128)(2,1)S(1)}, u32[]{:S(2)}, u32[]{:S(2)}) collective-permute-start(bf16[160,256]{1,0:T(8,128)(2,1)S(1)} %maximum_add_fusion.1.rest_0_), channel_id=1, source_target_pairs={{0,64},{1,17},{2,66},{3,19},{4,68},{5,21},{6,70},{7,23},{8,72},{9,... | collective-permute-start | bytes 245768 | tf_op jit(solution)/shard_map/ppermute | solution.py:502
  68.3 3.1 %pair_forces.10 = (f32[3,2048]{1,0:T(4,128)S(1)}, f32[1,1024]{1,0:T(1,128)S(1)}) custom-call(f32[3,40]{1,0:T(4,128)S(1)} %copy-done.6, f32[4,16384]{1,0:T(4,128)S(1)} %copy-done.2, f32[3,40]{1,0:T(4,128)S(1)} %copy-done.6, s32[16,16384]{1,0:T(8,128)S(1)} %copy-done.1, bf16[160,256]{1,0:T(8,128)(2,1)S(1)} %maximum_add_fusion.1.rest_0_), custom_call_target="tpu_custom_call" | custom-call | flops 160000000 | bytes 262144 | tf_op jit(solution)/shard_map/pair_forces/pallas_call | solution.py:88
  71.4 0.5 collective-permute-done.15
  71.9 0.1 maximum_add_fusion.rest_0_.p0
  71.9 0.3 collective-permute-start.16
  72.3 1.3 %collective-permute-start.17 = (bf16[640,256]{1,0:T(8,128)(2,1)S(1)}, bf16[640,256]{1,0:T(8,128)(2,1)S(1)}, u32[]{:S(2)}, u32[]{:S(2)}) collective-permute-start(bf16[640,256]{1,0:T(8,128)(2,1)S(1)} %maximum_add_fusion.rest_0_.p0), channel_id=1, source_target_pairs={{0,16},{1,9},{2,18},{3,11},{4,20},{5,13},{6,22},{7,15},{8,24},{9,1... | collective-permute-start | bytes 983048 | tf_op jit(solution)/shard_map/ppermute | solution.py:502
  73.6 1.2 collective-permute-start.18
  74.8 3.1 %collective-permute-start.19 = (bf16[640,256]{1,0:T(8,128)(2,1)S(1)}, bf16[640,256]{1,0:T(8,128)(2,1)S(1)}, u32[]{:S(2)}, u32[]{:S(2)}) collective-permute-start(bf16[640,256]{1,0:T(8,128)(2,1)S(1)} %maximum_add_fusion.rest_0_.p0), channel_id=1, source_target_pairs={{0,1},{1,0},{2,3},{3,2},{4,5},{5,4},{6,7},{7,6},{8,9},{9,8},{10,11... | collective-permute-start | bytes 983048 | tf_op jit(solution)/shard_map/ppermute | solution.py:508
  77.9 6.7 %pair_forces.11 = (f32[3,4608]{1,0:T(4,128)S(1)}, f32[1,1024]{1,0:T(1,128)S(1)}) custom-call(f32[3,40]{1,0:T(4,128)S(1)} %copy-done.6, f32[4,16384]{1,0:T(4,128)S(1)} %copy-done.2, f32[3,40]{1,0:T(4,128)S(1)} %copy-done.6, s32[16,16384]{1,0:T(8,128)S(1)} %copy-done.1, bf16[640,256]{1,0:T(8,128)(2,1)S(1)} %maximum_add_fusion.rest_0_.p0), custom_call_target="tpu_custom_call" | custom-call | flops 360000000 | bytes 589824 | tf_op jit(solution)/shard_map/pair_forces/pallas_call | solution.py:88
  84.7 0.1 broadcast_add_fusion
  84.8 1.8 %collective-permute-start.20 = (bf16[640,256]{1,0:T(8,128)(2,1)S(1)}, bf16[640,256]{1,0:T(8,128)(2,1)S(1)}, u32[]{:S(2)}, u32[]{:S(2)}) collective-permute-start(bf16[640,256]{1,0:T(8,128)(2,1)S(1)} %get-tuple-element.50.p1), channel_id=1, source_target_pairs={{0,1},{1,0},{2,3},{3,2},{4,5},{5,4},{6,7},{7,6},{8,9},{9,8},{10,11... | collective-permute-start | bytes 983048 | tf_op jit(solution)/shard_map/ppermute | solution.py:508
  86.6 0.1 collective-permute-start.21
  86.7 0.4 collective-permute-start.22
  87.1 0.6 collective-permute-start.23
  87.8 0.1 collective-permute-done.20.p5
  87.9 0.5 collective-permute-done.21.p6
  88.3 0.5 collective-permute-done.22.p7
  88.8 6.7 %second_layer.1 = (f32[128,128]{1,0:T(8,128)}, f32[1,128]{1,0:T(1,128)}) custom-call(s32[1]{0:T(128)} %bitcast.me, s32[1280,1]{1,0:T(8,128)S(1)} %reshape.14.ids.ids_in, bf16[1280,128]{1,0:T(8,128)(2,1)S(1)} %get-tuple-element.26.basis.basis_in, f32[40,384]{1,0:T(8,128)S(1)} %get-tuple-element.31.feat1, f32[2,8,256]{2,1,0:T(8,128)S(1)} %copy-done.8, ...), custom_call_target="tpu_custom_call" | custom-call | tf_op jit(solution)/shard_map/second_layer/pallas_call | solution.py:399
  95.5 9.1 %all-to-all-start.1 = ((f32[128,1,128]{2,1,0:T(1,128)}), f32[128,1,128]{2,1,0:T(1,128)S(1)}, u32[]{:S(2)}, u32[]{:S(2)}) async-start(f32[128,1,128]{2,1,0:T(1,128)} %bitcast.9), calls=%async_computation.1 | async-start | bytes 131072 | tf_op jit(solution)/shard_map/all_to_all | solution.py:583
  104.6 0.6 copy-done.15
  105.2 0.5 slice_bitcast_fusion
  105.8 2.7 %pair_forces.13 = (f32[3,1536]{1,0:T(4,128)S(1)}, f32[1,1024]{1,0:T(1,128)}) custom-call(f32[4,1024]{1,0:T(4,128)S(1)} %collective-permute-done.23.left, f32[4,16384]{1,0:T(4,128)S(1)} %copy-done.2, f32[4,1024]{1,0:T(4,128)S(1)} %collective-permute-done.24.right, s32[16,16384]{1,0:T(8,128)S(1)} %copy-done.1, f32[128,128]{1,0:T(8,128)} %get-tuple-element.37.rest_0_), custom_call_target="tpu_custom_call" | custom-call | flops 120000000 | bytes 196608 | tf_op jit(solution)/shard_map/pair_forces/pallas_call | solution.py:88
  108.5 2.7 %pair_forces.12 = (f32[3,1536]{1,0:T(4,128)S(1)}, f32[1,1024]{1,0:T(1,128)}) custom-call(f32[4,1024]{1,0:T(4,128)S(1)} %collective-permute-done.23.left, f32[4,16384]{1,0:T(4,128)S(1)} %copy-done.2, f32[4,1024]{1,0:T(4,128)S(1)} %collective-permute-done.24.right, s32[16,16384]{1,0:T(8,128)S(1)} %copy-done.1, f32[128,128]{1,0:T(8,128)} %get-tuple-element.37.rest_0_), custom_call_target="tpu_custom_call" | custom-call | flops 120000000 | bytes 196608 | tf_op jit(solution)/shard_map/pair_forces/pallas_call | solution.py:88
  111.2 3.4 %all-to-all-done.1 = f32[128,1,128]{2,1,0:T(1,128)S(1)} async-done(((f32[128,1,128]{2,1,0:T(1,128)}), f32[128,1,128]{2,1,0:T(1,128)S(1)}, u32[]{:S(2)}, u32[]{:S(2)}) %all-to-all-start.1) | async-done | bytes 65568 | tf_op jit(solution)/shard_map/all_to_all | solution.py:583
  114.6 8.2 %embed_forces.1 = f32[3,16384]{1,0:T(4,128)} custom-call(f32[4,16384]{1,0:T(4,128)S(1)} %copy-done.2, f32[128,256]{1,0:T(8,128)S(1)} %bitcast.20, f32[128,128]{1,0:T(8,128)S(1)} %bitcast.21, s32[1,8]{1,0:T(1,128)S(1)} %copy-done.10, s32[1]{0:T(128)S(6)} %copy.31.count_in, bf16[48,5120]{1,0:T(8,128)(2,1)S(1)} %copy-done.4, bf16[48,1024]{1,0:T(8,128)(2,1)S(1)} %copy-done.7, ...), custom_call_target="tpu_custom_call" | custom-call | tf_op jit(solution)/shard_map/embed_forces/pallas_call | solution.py:472
  (51 shorter events, 0.2 us)
Async XLA Ops:
  0.6 13.7 %copy-start.2 = (f32[4,16384]{1,0:T(4,128)S(1)}, f32[4,16384]{1,0:T(4,128)}, u32[]{:S(2)}) copy-start(f32[4,16384]{1,0:T(4,128)} %mm.3) | copy-start | bytes 786436
  2.1 12.2 %copy-start.6 = (f32[3,40]{1,0:T(4,128)S(1)}, f32[3,40]{1,0:T(4,128)}, u32[]{:S(2)}) copy-start(f32[3,40]{1,0:T(4,128)} %right.9) | copy-start | bytes 1444
  2.1 21.7 %all-to-all-start = ((f32[128,1,256]{2,1,0:T(1,128)}), f32[128,1,256]{2,1,0:T(1,128)S(1)}, u32[]{:S(2)}, u32[]{:S(2)}) async-start(f32[128,1,256]{2,1,0:T(1,128)} %spread.1), calls=%async_computation | async-start | bytes 262144 | tf_op jit(solution)/shard_map/all_to_all | solution.py:535
  14.3 1.2 copy-start
  23.8 0.7 copy-start.10
  23.9 8.8 %copy-start.14 = (s32[40,32]{0,1:T(8,128)S(1)}, s32[40,32]{0,1:T(8,128)}, u32[]{:S(2)}) copy-start(s32[40,32]{0,1:T(8,128)} %param.20) | copy-start | bytes 15364
  24.5 24.3 %copy-start.1 = (s32[16,16384]{1,0:T(8,128)S(1)}, s32[16,16384]{1,0:T(8,128)}, u32[]{:S(2)}) copy-start(s32[16,16384]{1,0:T(8,128)} %nb.13) | copy-start | bytes 3145732
  29.2 7.8 %collective-permute-start = (f32[40,128]{1,0:T(8,128)S(1)}, f32[40,128]{1,0:T(8,128)S(1)}, u32[]{:S(2)}, u32[]{:S(2)}) collective-permute-start(f32[40,128]{1,0:T(8,128)S(1)} %get-tuple-element.25.after), channel_id=1, source_target_pairs={{0,4},{1,33},{2,6},{3,35},{4,8},{5,37},{6,10},{7,39},{8,12},{9,41}... | collective-permute-start | bytes 61448 | tf_op jit(solution)/shard_map/ppermute | solution.py:502
  29.6 7.4 %collective-permute-start.1 = (f32[40,128]{1,0:T(8,128)S(1)}, f32[40,128]{1,0:T(8,128)S(1)}, u32[]{:S(2)}, u32[]{:S(2)}) collective-permute-start(f32[40,128]{1,0:T(8,128)S(1)} %get-tuple-element.25.after), channel_id=1, source_target_pairs={{0,8},{1,65},{2,10},{3,67},{4,12},{5,69},{6,14},{7,71},{8,0},{9,73... | collective-permute-start | bytes 61448 | tf_op jit(solution)/shard_map/ppermute | solution.py:502
  31.5 5.5 %collective-permute-start.2 = (f32[40,128]{1,0:T(8,128)S(1)}, f32[40,128]{1,0:T(8,128)S(1)}, u32[]{:S(2)}, u32[]{:S(2)}) collective-permute-start(f32[40,128]{1,0:T(8,128)S(1)} %get-tuple-element.25.after), channel_id=1, source_target_pairs={{0,12},{1,97},{2,14},{3,99},{4,0},{5,101},{6,2},{7,103},{8,4},{9,1... | collective-permute-start | bytes 61448 | tf_op jit(solution)/shard_map/ppermute | solution.py:502
  32.8 0.7 copy-start.12
  32.8 0.7 copy-start.13
  33.5 0.7 copy-start.11
  37.1 4.8 %collective-permute-start.3 = (f32[40,128]{1,0:T(8,128)S(1)}, f32[40,128]{1,0:T(8,128)S(1)}, u32[]{:S(2)}, u32[]{:S(2)}) collective-permute-start(f32[40,128]{1,0:T(8,128)S(1)} %add_add_fusion.2), channel_id=1, source_target_pairs={{0,32},{1,3},{2,34},{3,17},{4,36},{5,7},{6,38},{7,21},{8,40},{9,11... | collective-permute-start | bytes 61448 | tf_op jit(solution)/shard_map/ppermute | solution.py:502
  38.3 4.1 %collective-permute-start.4 = (f32[40,128]{1,0:T(8,128)S(1)}, f32[40,128]{1,0:T(8,128)S(1)}, u32[]{:S(2)}, u32[]{:S(2)}) collective-permute-start(f32[40,128]{1,0:T(8,128)S(1)} %add_add_fusion.2), channel_id=1, source_target_pairs={{0,64},{1,17},{2,66},{3,19},{4,68},{5,21},{6,70},{7,23},{8,72},{9,... | collective-permute-start | bytes 61448 | tf_op jit(solution)/shard_map/ppermute | solution.py:502
  40.8 2.6 %collective-permute-start.5 = (f32[40,128]{1,0:T(8,128)S(1)}, f32[40,128]{1,0:T(8,128)S(1)}, u32[]{:S(2)}, u32[]{:S(2)}) collective-permute-start(f32[40,128]{1,0:T(8,128)S(1)} %add_add_fusion.2), channel_id=1, source_target_pairs={{0,96},{1,19},{2,98},{3,1},{4,100},{5,23},{6,102},{7,5},{8,104},{9... | collective-permute-start | bytes 61448 | tf_op jit(solution)/shard_map/ppermute | solution.py:502
  43.4 7.0 %collective-permute-start.6 = (f32[40,128]{1,0:T(8,128)S(1)}, f32[40,128]{1,0:T(8,128)S(1)}, u32[]{:S(2)}, u32[]{:S(2)}) collective-permute-start(f32[40,128]{1,0:T(8,128)S(1)} %add_add_fusion.1.rest_0_), channel_id=1, source_target_pairs={{0,2},{1,5},{2,16},{3,7},{4,6},{5,9},{6,20},{7,11},{8,10},{9,13},{... | collective-permute-start | bytes 61448 | tf_op jit(solution)/shard_map/ppermute | solution.py:502
  45.3 5.2 %collective-permute-start.7 = (f32[40,128]{1,0:T(8,128)S(1)}, f32[40,128]{1,0:T(8,128)S(1)}, u32[]{:S(2)}, u32[]{:S(2)}) collective-permute-start(f32[40,128]{1,0:T(8,128)S(1)} %add_add_fusion.1.rest_0_), channel_id=1, source_target_pairs={{0,16},{1,9},{2,18},{3,11},{4,20},{5,13},{6,22},{7,15},{8,24},{9,1... | collective-permute-start | bytes 61448 | tf_op jit(solution)/shard_map/ppermute | solution.py:502
  47.9 2.9 %collective-permute-start.8 = (f32[40,128]{1,0:T(8,128)S(1)}, f32[40,128]{1,0:T(8,128)S(1)}, u32[]{:S(2)}, u32[]{:S(2)}) collective-permute-start(f32[40,128]{1,0:T(8,128)S(1)} %add_add_fusion.1.rest_0_), channel_id=1, source_target_pairs={{0,18},{1,13},{2,0},{3,15},{4,22},{5,1},{6,4},{7,3},{8,26},{9,5},{... | collective-permute-start | bytes 61448 | tf_op jit(solution)/shard_map/ppermute | solution.py:502
  48.8 7.0 %copy-start.3 = (bf16[2,256,256]{2,1,0:T(8,128)(2,1)S(1)}, bf16[2,256,256]{2,1,0:T(8,128)(2,1)}, u32[]{:S(2)}) copy-start(bf16[2,256,256]{2,1,0:T(8,128)(2,1)} %mix_in.1) | copy-start | bytes 786436
  48.8 7.0 %copy-start.5 = (bf16[2,256,256]{2,1,0:T(8,128)(2,1)S(1)}, bf16[2,256,256]{2,1,0:T(8,128)(2,1)}, u32[]{:S(2)}) copy-start(bf16[2,256,256]{2,1,0:T(8,128)(2,1)} %msg.1) | copy-start | bytes 786436
  50.9 5.0 %collective-permute-start.9 = (f32[40,128]{1,0:T(8,128)S(1)}, f32[40,128]{1,0:T(8,128)S(1)}, u32[]{:S(2)}, u32[]{:S(2)}) collective-permute-start(f32[40,128]{1,0:T(8,128)S(1)} %add_add_fusion), channel_id=1, source_target_pairs={{0,1},{1,0},{2,3},{3,2},{4,5},{5,4},{6,7},{7,6},{8,9},{9,8},{10,11... | collective-permute-start | bytes 61448 | tf_op jit(solution)/shard_map/ppermute | solution.py:508
  55.8 0.7 copy-start.8
  55.8 0.7 copy-start.9
  58.5 5.2 %collective-permute-start.10 = (bf16[40,256]{1,0:T(8,128)(2,1)S(1)}, bf16[40,256]{1,0:T(8,128)(2,1)S(1)}, u32[]{:S(2)}, u32[]{:S(2)}) collective-permute-start(bf16[40,256]{1,0:T(8,128)(2,1)S(1)} %get-tuple-element.32.rest_0_), channel_id=1, source_target_pairs={{0,4},{1,33},{2,6},{3,35},{4,8},{5,37},{6,10},{7,39},{8,12},{9,41}... | collective-permute-start | bytes 61448 | tf_op jit(solution)/shard_map/ppermute | solution.py:502
  58.5 5.2 %collective-permute-start.11 = (bf16[40,256]{1,0:T(8,128)(2,1)S(1)}, bf16[40,256]{1,0:T(8,128)(2,1)S(1)}, u32[]{:S(2)}, u32[]{:S(2)}) collective-permute-start(bf16[40,256]{1,0:T(8,128)(2,1)S(1)} %get-tuple-element.32.rest_0_), channel_id=1, source_target_pairs={{0,8},{1,65},{2,10},{3,67},{4,12},{5,69},{6,14},{7,71},{8,0},{9,73... | collective-permute-start | bytes 61448 | tf_op jit(solution)/shard_map/ppermute | solution.py:502
  62.1 2.6 %collective-permute-start.12 = (bf16[40,256]{1,0:T(8,128)(2,1)S(1)}, bf16[40,256]{1,0:T(8,128)(2,1)S(1)}, u32[]{:S(2)}, u32[]{:S(2)}) collective-permute-start(bf16[40,256]{1,0:T(8,128)(2,1)S(1)} %get-tuple-element.32.rest_0_), channel_id=1, source_target_pairs={{0,12},{1,97},{2,14},{3,99},{4,0},{5,101},{6,2},{7,103},{8,4},{9,1... | collective-permute-start | bytes 61448 | tf_op jit(solution)/shard_map/ppermute | solution.py:502
  64.7 6.7 %collective-permute-start.13 = (bf16[160,256]{1,0:T(8,128)(2,1)S(1)}, bf16[160,256]{1,0:T(8,128)(2,1)S(1)}, u32[]{:S(2)}, u32[]{:S(2)}) collective-permute-start(bf16[160,256]{1,0:T(8,128)(2,1)S(1)} %maximum_add_fusion.1.rest_0_), channel_id=1, source_target_pairs={{0,32},{1,3},{2,34},{3,17},{4,36},{5,7},{6,38},{7,21},{8,40},{9,11... | collective-permute-start | bytes 245768 | tf_op jit(solution)/shard_map/ppermute | solution.py:502
  64.8 6.6 %collective-permute-start.14 = (bf16[160,256]{1,0:T(8,128)(2,1)S(1)}, bf16[160,256]{1,0:T(8,128)(2,1)S(1)}, u32[]{:S(2)}, u32[]{:S(2)}) collective-permute-start(bf16[160,256]{1,0:T(8,128)(2,1)S(1)} %maximum_add_fusion.1.rest_0_), channel_id=1, source_target_pairs={{0,64},{1,17},{2,66},{3,19},{4,68},{5,21},{6,70},{7,23},{8,72},{9,... | collective-permute-start | bytes 245768 | tf_op jit(solution)/shard_map/ppermute | solution.py:502
  68.3 3.6 %collective-permute-start.15 = (bf16[160,256]{1,0:T(8,128)(2,1)S(1)}, bf16[160,256]{1,0:T(8,128)(2,1)S(1)}, u32[]{:S(2)}, u32[]{:S(2)}) collective-permute-start(bf16[160,256]{1,0:T(8,128)(2,1)S(1)} %maximum_add_fusion.1.rest_0_), channel_id=1, source_target_pairs={{0,96},{1,19},{2,98},{3,1},{4,100},{5,23},{6,102},{7,5},{8,104},{9... | collective-permute-start | bytes 245768 | tf_op jit(solution)/shard_map/ppermute | solution.py:502
  71.9 12.7 %collective-permute-start.16 = (bf16[640,256]{1,0:T(8,128)(2,1)S(1)}, bf16[640,256]{1,0:T(8,128)(2,1)S(1)}, u32[]{:S(2)}, u32[]{:S(2)}) collective-permute-start(bf16[640,256]{1,0:T(8,128)(2,1)S(1)} %maximum_add_fusion.rest_0_.p0), channel_id=1, source_target_pairs={{0,2},{1,5},{2,16},{3,7},{4,6},{5,9},{6,20},{7,11},{8,10},{9,13},{... | collective-permute-start | bytes 983048 | tf_op jit(solution)/shard_map/ppermute | solution.py:502
  72.3 12.4 %collective-permute-start.17 = (bf16[640,256]{1,0:T(8,128)(2,1)S(1)}, bf16[640,256]{1,0:T(8,128)(2,1)S(1)}, u32[]{:S(2)}, u32[]{:S(2)}) collective-permute-start(bf16[640,256]{1,0:T(8,128)(2,1)S(1)} %maximum_add_fusion.rest_0_.p0), channel_id=1, source_target_pairs={{0,16},{1,9},{2,18},{3,11},{4,20},{5,13},{6,22},{7,15},{8,24},{9,1... | collective-permute-start | bytes 983048 | tf_op jit(solution)/shard_map/ppermute | solution.py:502
  73.6 11.1 %collective-permute-start.18 = (bf16[640,256]{1,0:T(8,128)(2,1)S(1)}, bf16[640,256]{1,0:T(8,128)(2,1)S(1)}, u32[]{:S(2)}, u32[]{:S(2)}) collective-permute-start(bf16[640,256]{1,0:T(8,128)(2,1)S(1)} %maximum_add_fusion.rest_0_.p0), channel_id=1, source_target_pairs={{0,18},{1,13},{2,0},{3,15},{4,22},{5,1},{6,4},{7,3},{8,26},{9,5},{... | collective-permute-start | bytes 983048 | tf_op jit(solution)/shard_map/ppermute | solution.py:502
  74.8 13.0 %collective-permute-start.19 = (bf16[640,256]{1,0:T(8,128)(2,1)S(1)}, bf16[640,256]{1,0:T(8,128)(2,1)S(1)}, u32[]{:S(2)}, u32[]{:S(2)}) collective-permute-start(bf16[640,256]{1,0:T(8,128)(2,1)S(1)} %maximum_add_fusion.rest_0_.p0), channel_id=1, source_target_pairs={{0,1},{1,0},{2,3},{3,2},{4,5},{5,4},{6,7},{7,6},{8,9},{9,8},{10,11... | collective-permute-start | bytes 983048 | tf_op jit(solution)/shard_map/ppermute | solution.py:508
  84.8 3.1 %collective-permute-start.20 = (bf16[640,256]{1,0:T(8,128)(2,1)S(1)}, bf16[640,256]{1,0:T(8,128)(2,1)S(1)}, u32[]{:S(2)}, u32[]{:S(2)}) collective-permute-start(bf16[640,256]{1,0:T(8,128)(2,1)S(1)} %get-tuple-element.50.p1), channel_id=1, source_target_pairs={{0,1},{1,0},{2,3},{3,2},{4,5},{5,4},{6,7},{7,6},{8,9},{9,8},{10,11... | collective-permute-start | bytes 983048 | tf_op jit(solution)/shard_map/ppermute | solution.py:508
  86.6 1.7 %collective-permute-start.21 = (bf16[640,256]{1,0:T(8,128)(2,1)S(1)}, bf16[640,256]{1,0:T(8,128)(2,1)S(1)}, u32[]{:S(2)}, u32[]{:S(2)}) collective-permute-start(bf16[640,256]{1,0:T(8,128)(2,1)S(1)} %get-tuple-element.49.p2), channel_id=1, source_target_pairs={{0,1},{1,0},{2,3},{3,2},{4,5},{5,4},{6,7},{7,6},{8,9},{9,8},{10,11... | collective-permute-start | bytes 983048 | tf_op jit(solution)/shard_map/ppermute | solution.py:508
  86.7 2.1 %collective-permute-start.22 = (bf16[640,256]{1,0:T(8,128)(2,1)S(1)}, bf16[640,256]{1,0:T(8,128)(2,1)S(1)}, u32[]{:S(2)}, u32[]{:S(2)}) collective-permute-start(bf16[640,256]{1,0:T(8,128)(2,1)S(1)} %get-tuple-element.48.p3), channel_id=1, source_target_pairs={{0,1},{1,0},{2,3},{3,2},{4,5},{5,4},{6,7},{7,6},{8,9},{9,8},{10,11... | collective-permute-start | bytes 983048 | tf_op jit(solution)/shard_map/ppermute | solution.py:508
  87.1 18.6 %collective-permute-start.23 = (f32[4,1024]{1,0:T(4,128)S(1)}, f32[4,1024]{1,0:T(4,128)S(1)}, u32[]{:S(2)}, u32[]{:S(2)}) collective-permute-start(f32[4,1024]{1,0:T(4,128)S(1)} %get-tuple-element.47), channel_id=1, source_target_pairs={{0,1},{1,2},{2,3},{3,4},{4,5},{5,6},{6,7},{7,8},{8,9},{9,10},{10,1... | collective-permute-start | bytes 49160 | tf_op jit(solution)/shard_map/ppermute | solution.py:565
  87.8 18.0 %collective-permute-start.24 = (f32[4,1024]{1,0:T(4,128)S(1)}, f32[4,1024]{1,0:T(4,128)S(1)}, u32[]{:S(2)}, u32[]{:S(2)}) collective-permute-start(f32[4,1024]{1,0:T(4,128)S(1)} %get-tuple-element.46), channel_id=1, source_target_pairs={{1,0},{2,1},{3,2},{4,3},{5,4},{6,5},{7,6},{8,7},{9,8},{10,9},{11,1... | collective-permute-start | bytes 49160 | tf_op jit(solution)/shard_map/ppermute | solution.py:566
  95.5 19.1 %all-to-all-start.1 = ((f32[128,1,128]{2,1,0:T(1,128)}), f32[128,1,128]{2,1,0:T(1,128)S(1)}, u32[]{:S(2)}, u32[]{:S(2)}) async-start(f32[128,1,128]{2,1,0:T(1,128)} %bitcast.9), calls=%async_computation.1 | async-start | bytes 131072 | tf_op jit(solution)/shard_map/all_to_all | solution.py:583
  104.6 0.6 copy-start.15
  108.5 6.1 %copy-start.4 = (bf16[48,5120]{1,0:T(8,128)(2,1)S(1)}, bf16[48,5120]{1,0:T(8,128)(2,1)}, u32[]{:S(2)}) copy-start(bf16[48,5120]{1,0:T(8,128)(2,1)} %get-tuple-element.38.atoms_in) | copy-start | bytes 1474564
  108.5 6.1 %copy-start.7 = (bf16[48,1024]{1,0:T(8,128)(2,1)S(1)}, bf16[48,1024]{1,0:T(8,128)(2,1)}, u32[]{:S(2)}) copy-start(bf16[48,1024]{1,0:T(8,128)(2,1)} %get-tuple-element.39.slots_in) | copy-start | bytes 294916

commit v3 on v2

--- a/solution.py
+++ b/solution.py
@@ -536,23 +536,23 @@
     tab = tab.reshape(NDEV, 2 * LANES)
     ids = ml_edges.reshape(-1, 1)
     blocks = own_rows // LANES
-    cuts = (0, 12, 48, 56, 64, 80, blocks - 12, blocks)
+    cuts = (0, 12, 44, 52, 60, 76, 100, blocks - 12, blocks)
     far = ml_coords
 
     def pairs(i, *after, before=far, behind=far):
         return pair_forces(cuts[i], cuts[i + 1] - cuts[i], before, mm_atoms, behind, neighbours, after)
 
     pieces = [None] * (len(cuts) - 1)
-    pieces[1], zero = pairs(1, far)
+    pieces[1], zero = pairs(1, embed_blocks, radial_weight)
     pot, atoms, slots = field(embed_blocks, embed_count, mm_atoms, tab, pieces[1], kappa_field)
     basis, kinds, rows, zero = geometry(
         me, ids, tab, field_weight[None], charge_weight[None], energy_weight[None], pot
     )
+    pot = functools.reduce(jnp.add, ring_parts(pot, "c"))
     pot = stand(functools.reduce(jnp.add, stage_parts(pot, 0)), zero)
     pot = functools.reduce(jnp.add, stage_parts(pot, 1))
     pieces[2], zero = pairs(2, pot)
     pot = stand(functools.reduce(jnp.add, stage_parts(pot, 2)), zero)
-    pot = functools.reduce(jnp.add, ring_parts(pot, "c"))
     feat1, proj = first_layer(
         me, ids, pot, basis, kinds, species_table, rows, msg_weight, radial_weight, mix_weight
     )
@@ -578,7 +578,8 @@
         rows,
         *parts,
     )
-    for i in (0, 6):
+    pieces[6], _ = pairs(6, charges)
+    for i in (0, 7):
         pieces[i], _ = pairs(i, charges, before=before, behind=behind)
     charges = lax.all_to_all(charges, ALL, 0, 0, tiled=True)
     mm_force = embed(embed_blocks, embed_count, mm_atoms, tab, charges, atoms, slots, pieces, kappa)

time: 123 us -> 122 us (level)
  waiting for transfers between devices: 10.3 us -> 6.62 us
  starting transfers between devices: 54.5 us -> 57.2 us
    ppermute x5, starting transfers between devices: 9.6 us -> 12.9 us  [ring_parts(): lax.ppermute(value, axis, [(i, (i + k) % n) for i in range(n)])]
    all_to_all x1, waiting for transfers between devices: 3.43 us -> 0.3 us  [body(): charges = lax.all_to_all(charges, ALL, 0, 0, tiled=True)]
    pallas_call x7 -> x8, Pallas kernels: 25.1 us -> 25.2 us  [pair_forces(): pl.pallas_call(functools.partial(pair_kernel, first, count), grid=(count...]
  transfers between devices with their start and end apart: 27 -> 27, of which waited for: 11 -> 11; matrix products, arithmetic and copies ran while one was open for 1% -> 1% of each run, Pallas kernels for 28% -> 29%
where the time goes in v3:
time: 122 us
  starting transfers between devices  57.2 us (47%)
  Pallas kernels  51.1 us (42%)
  waiting for transfers between devices  6.62 us (5%)
  local copies, waits for them, and re-layouts  4.6 us (4%)
  between operations  1.85 us (2%)
    pallas_call x8, Pallas kernels, pair_forces(): pl.pallas_call(functools.partial(pair_kernel, first, count), grid=(count...  25.2 us
    ppermute x18, starting transfers between devices, stage_parts(): parts.append(lax.ppermute(value, ALL, pairs))  23.1 us
    ppermute x5, starting transfers between devices, ring_parts(): lax.ppermute(value, axis, [(i, (i + k) % n) for i in range(n)])  12.9 us
    all_to_all x1, starting transfers between devices, body(): lax.all_to_all(spread(ml_coords, ml_species[None]), ALL, 0, 0, tiled=True)  11.5 us
    all_to_all x1, starting transfers between devices, body(): charges = lax.all_to_all(charges, ALL, 0, 0, tiled=True)  9.06 us
    pallas_call x1, Pallas kernels, embed(): pl.pallas_call(functools.partial(embed_kernel, scale), out_shape=jax.Shap...  8.21 us
    pallas_call x1, Pallas kernels, second_layer(): pl.pallas_call(second_layer_kernel, out_shape=(jax.ShapeDtypeStruct((NDEV...  6.73 us
    pallas_call x1, Pallas kernels, field(): pl.pallas_call(functools.partial(field_kernel, scale), out_shape=(jax.Sha...  4.69 us
  transfers between devices with their start and end apart: 27, of which 11 were waited for; matrix products, arithmetic and copies ran while one was open for 1% of the time, Pallas kernels for 29%

profile of v3, /device:TPU:1, one launch (start us, length us, event | category | flops | bytes accessed | tf_op | source)
XLA Modules:
  0.0 121.6 jit_solution(7733730688756719716)
XLA Ops:
  0.6 1.5 %spread.1 = f32[128,1,256]{2,1,0:T(1,128)} custom-call(f32[3,40]{1,0:T(4,128)} %right.11, s32[1,40]{1,0:T(1,128)} %bitcast.27), custom_call_target="tpu_custom_call" | custom-call | tf_op jit(solution)/shard_map/spread/pallas_call | solution.py:123
  2.1 11.5 %all-to-all-start = ((f32[128,1,256]{2,1,0:T(1,128)}), f32[128,1,256]{2,1,0:T(1,128)S(1)}, u32[]{:S(2)}, u32[]{:S(2)}) async-start(f32[128,1,256]{2,1,0:T(1,128)} %spread.1), calls=%async_computation | async-start | bytes 262144 | tf_op jit(solution)/shard_map/all_to_all | solution.py:535
  13.6 0.0 copy-start.10
  14.4 1.2 %copy-done = s32[16,16384]{1,0:T(8,128)S(1)} copy-done((s32[16,16384]{1,0:T(8,128)S(1)}, s32[16,16384]{1,0:T(8,128)}, u32[]{:S(2)}) %copy-start) | copy-done | bytes 1048600
  15.6 6.0 %pair_forces.8 = (f32[3,4096]{1,0:T(4,128)S(1)}, f32[1,1024]{1,0:T(1,128)}) custom-call(f32[3,40]{1,0:T(4,128)S(1)} %copy-done.5, f32[4,16384]{1,0:T(4,128)S(1)} %copy-done.2, f32[3,40]{1,0:T(4,128)S(1)} %copy-done.5, s32[16,16384]{1,0:T(8,128)S(1)} %copy-done, s32[1,8]{1,0:T(1,128)S(1)} %copy-done.10, f32[2,8,256]{2,1,0:T(8,128)S(1)} %copy-done.7), custom_call_target="tpu_custom_call" | custom-call | flops 320000000 | bytes 524288 | tf_op jit(solution)/shard_map/pair_forces/pallas_call | solution.py:88
  21.6 2.3 %all-to-all-done = f32[128,1,256]{2,1,0:T(1,128)S(1)} async-done(((f32[128,1,256]{2,1,0:T(1,128)}), f32[128,1,256]{2,1,0:T(1,128)S(1)}, u32[]{:S(2)}, u32[]{:S(2)}) %all-to-all-start) | async-done | bytes 131104 | tf_op jit(solution)/shard_map/all_to_all | solution.py:535
  23.9 0.0 copy-start.1
  23.9 4.7 %field.1 = (f32[40,128]{1,0:T(8,128)S(1)}, bf16[48,5120]{1,0:T(8,128)(2,1)}, bf16[48,1024]{1,0:T(8,128)(2,1)}) custom-call(s32[1,8]{1,0:T(1,128)S(1)} %copy-done.10, s32[1]{0:T(128)S(6)} %copy.31.count_in, f32[4,16384]{1,0:T(4,128)S(1)} %copy-done.2, f32[128,256]{1,0:T(8,128)S(1)} %bitcast.18, f32[3,4096]{1,0:T(4,128)S(1)} %get-tuple-element.25.after.rest_1_), custom_call_target="tpu_custom_call" | custom-call | tf_op jit(solution)/shard_map/field/pallas_call | solution.py:193
  28.6 0.5 collective-permute-start
  29.0 0.8 collective-permute-done
  29.9 0.3 collective-permute-start.1
  30.2 1.8 %collective-permute-start.2 = (f32[40,128]{1,0:T(8,128)S(1)}, f32[40,128]{1,0:T(8,128)S(1)}, u32[]{:S(2)}, u32[]{:S(2)}) collective-permute-start(f32[40,128]{1,0:T(8,128)S(1)} %add.124), channel_id=1, source_target_pairs={{0,8},{1,65},{2,10},{3,67},{4,12},{5,69},{6,14},{7,71},{8,0},{9,73... | collective-permute-start | bytes 61448 | tf_op jit(solution)/shard_map/ppermute | solution.py:502
  32.0 0.7 collective-permute-start.3
  32.7 0.1 copy.23
  32.7 0.7 reshape.14.ids.ids_in
  33.4 0.0 copy-start.11
  33.5 0.7 copy-done.11
  34.1 2.9 %geometry.1 = (bf16[1280,128]{1,0:T(8,128)(2,1)S(1)}, bf16[1344,128]{1,0:T(8,128)(2,1)S(1)}, f32[4,256]{1,0:T(4,128)S(1)}, f32[1,128]{1,0:T(1,128)S(1)}) custom-call(s32[1]{0:T(128)} %bitcast.me, s32[1280,1]{1,0:T(8,128)S(1)} %reshape.14.ids.ids_in, f32[128,256]{1,0:T(8,128)S(1)} %bitcast.19, f32[1,256]{1,0:T(1,128)S(1)} %bitcast.23, f32[1,256]{1,0:T(1,128)S(1)} %bitcast.24, ...), custom_call_target="tpu_custom_call" | custom-call | tf_op jit(solution)/shard_map/geometry/pallas_call | solution.py:270
  37.0 1.2 collective-permute-start.4
  38.2 2.5 %collective-permute-start.5 = (f32[40,128]{1,0:T(8,128)S(1)}, f32[40,128]{1,0:T(8,128)S(1)}, u32[]{:S(2)}, u32[]{:S(2)}) collective-permute-start(f32[40,128]{1,0:T(8,128)S(1)} %add_add_fusion.2), channel_id=1, source_target_pairs={{0,64},{1,17},{2,66},{3,19},{4,68},{5,21},{6,70},{7,23},{8,72},{9,... | collective-permute-start | bytes 61448 | tf_op jit(solution)/shard_map/ppermute | solution.py:502
  40.7 1.1 collective-permute-start.6
  41.8 0.5 collective-permute-done.5
  42.4 1.0 collective-permute-done.6
  43.3 1.8 %collective-permute-start.7 = (f32[40,128]{1,0:T(8,128)S(1)}, f32[40,128]{1,0:T(8,128)S(1)}, u32[]{:S(2)}, u32[]{:S(2)}) collective-permute-start(f32[40,128]{1,0:T(8,128)S(1)} %add_add_fusion.1.rest_0_), channel_id=1, source_target_pairs={{0,2},{1,5},{2,16},{3,7},{4,6},{5,9},{6,20},{7,11},{8,10},{9,13},{... | collective-permute-start | bytes 61448 | tf_op jit(solution)/shard_map/ppermute | solution.py:502
  45.1 2.6 %collective-permute-start.8 = (f32[40,128]{1,0:T(8,128)S(1)}, f32[40,128]{1,0:T(8,128)S(1)}, u32[]{:S(2)}, u32[]{:S(2)}) collective-permute-start(f32[40,128]{1,0:T(8,128)S(1)} %add_add_fusion.1.rest_0_), channel_id=1, source_target_pairs={{0,16},{1,9},{2,18},{3,11},{4,20},{5,13},{6,22},{7,15},{8,24},{9,1... | collective-permute-start | bytes 61448 | tf_op jit(solution)/shard_map/ppermute | solution.py:502
  47.8 0.9 collective-permute-start.9
  48.7 1.6 %pair_forces.9 = (f32[3,1024]{1,0:T(4,128)S(1)}, f32[1,1024]{1,0:T(1,128)S(1)}) custom-call(f32[3,40]{1,0:T(4,128)S(1)} %copy-done.5, f32[4,16384]{1,0:T(4,128)S(1)} %copy-done.2, f32[3,40]{1,0:T(4,128)S(1)} %copy-done.5, s32[16,16384]{1,0:T(8,128)S(1)} %copy-done.1, f32[40,128]{1,0:T(8,128)S(1)} %add_add_fusion.1.rest_0_), custom_call_target="tpu_custom_call" | custom-call | flops 80000000 | bytes 131072 | tf_op jit(solution)/shard_map/pair_forces/pallas_call | solution.py:88
  50.4 0.3 collective-permute-done.9
  50.8 0.7 copy-done.9
  51.4 1.9 %first_layer.1 = (f32[40,384]{1,0:T(8,128)S(1)}, bf16[40,256]{1,0:T(8,128)(2,1)S(1)}) custom-call(s32[1]{0:T(128)} %bitcast.me, s32[1280,1]{1,0:T(8,128)S(1)} %reshape.14.ids.ids_in, f32[40,128]{1,0:T(8,128)S(1)} %add_add_fusion.pot, bf16[1280,128]{1,0:T(8,128)(2,1)S(1)} %get-tuple-element.27.basis.basis_in, bf16[1344,128]{1,0:T(8,128)(2,1)S(1)} %get-tuple-element.30.kinds, ...), custom_call_target="tpu_custom_call" | custom-call | tf_op jit(solution)/shard_map/first_layer/pallas_call | solution.py:320
  53.4 0.3 collective-permute-start.10
  53.7 0.9 collective-permute-start.11
  54.6 1.6 %collective-permute-start.12 = (bf16[40,256]{1,0:T(8,128)(2,1)S(1)}, bf16[40,256]{1,0:T(8,128)(2,1)S(1)}, u32[]{:S(2)}, u32[]{:S(2)}) collective-permute-start(bf16[40,256]{1,0:T(8,128)(2,1)S(1)} %get-tuple-element.33.rest_0_), channel_id=1, source_target_pairs={{0,12},{1,97},{2,14},{3,99},{4,0},{5,101},{6,2},{7,103},{8,4},{9,1... | collective-permute-start | bytes 61448 | tf_op jit(solution)/shard_map/ppermute | solution.py:502
  56.1 1.6 %pair_forces.10 = (f32[3,1024]{1,0:T(4,128)S(1)}, f32[1,1024]{1,0:T(1,128)S(1)}) custom-call(f32[3,40]{1,0:T(4,128)S(1)} %copy-done.5, f32[4,16384]{1,0:T(4,128)S(1)} %copy-done.2, f32[3,40]{1,0:T(4,128)S(1)} %copy-done.5, s32[16,16384]{1,0:T(8,128)S(1)} %copy-done.1, bf16[40,256]{1,0:T(8,128)(2,1)S(1)} %get-tuple-element.33.rest_0_), custom_call_target="tpu_custom_call" | custom-call | flops 80000000 | bytes 131072 | tf_op jit(solution)/shard_map/pair_forces/pallas_call | solution.py:88
  57.7 0.1 collective-permute-done.11
  57.8 0.2 collective-permute-done.12
  58.0 0.1 collective-permute-start.13
  58.1 3.2 %collective-permute-start.14 = (bf16[160,256]{1,0:T(8,128)(2,1)S(1)}, bf16[160,256]{1,0:T(8,128)(2,1)S(1)}, u32[]{:S(2)}, u32[]{:S(2)}) collective-permute-start(bf16[160,256]{1,0:T(8,128)(2,1)S(1)} %maximum_add_fusion.1.rest_0_), channel_id=1, source_target_pairs={{0,64},{1,17},{2,66},{3,19},{4,68},{5,21},{6,70},{7,23},{8,72},{9,... | collective-permute-start | bytes 245768 | tf_op jit(solution)/shard_map/ppermute | solution.py:502
  61.3 0.2 collective-permute-start.15
  61.5 3.0 %pair_forces.11 = (f32[3,2048]{1,0:T(4,128)S(1)}, f32[1,1024]{1,0:T(1,128)S(1)}) custom-call(f32[3,40]{1,0:T(4,128)S(1)} %copy-done.5, f32[4,16384]{1,0:T(4,128)S(1)} %copy-done.2, f32[3,40]{1,0:T(4,128)S(1)} %copy-done.5, s32[16,16384]{1,0:T(8,128)S(1)} %copy-done.1, bf16[160,256]{1,0:T(8,128)(2,1)S(1)} %maximum_add_fusion.1.rest_0_), custom_call_target="tpu_custom_call" | custom-call | flops 160000000 | bytes 262144 | tf_op jit(solution)/shard_map/pair_forces/pallas_call | solution.py:88
  64.6 0.0 collective-permute-done.15
  64.6 0.1 maximum_add_fusion.rest_0_.p0
  64.7 0.6 collective-permute-start.16
  65.2 2.8 %collective-permute-start.17 = (bf16[640,256]{1,0:T(8,128)(2,1)S(1)}, bf16[640,256]{1,0:T(8,128)(2,1)S(1)}, u32[]{:S(2)}, u32[]{:S(2)}) collective-permute-start(bf16[640,256]{1,0:T(8,128)(2,1)S(1)} %maximum_add_fusion.rest_0_.p0), channel_id=1, source_target_pairs={{0,16},{1,9},{2,18},{3,11},{4,20},{5,13},{6,22},{7,15},{8,24},{9,1... | collective-permute-start | bytes 983048 | tf_op jit(solution)/shard_map/ppermute | solution.py:502
  68.1 0.6 collective-permute-start.18
  68.6 7.9 %collective-permute-start.19 = (bf16[640,256]{1,0:T(8,128)(2,1)S(1)}, bf16[640,256]{1,0:T(8,128)(2,1)S(1)}, u32[]{:S(2)}, u32[]{:S(2)}) collective-permute-start(bf16[640,256]{1,0:T(8,128)(2,1)S(1)} %maximum_add_fusion.rest_0_.p0), channel_id=1, source_target_pairs={{0,1},{1,0},{2,3},{3,2},{4,5},{5,4},{6,7},{7,6},{8,9},{9,8},{10,11... | collective-permute-start | bytes 983048 | tf_op jit(solution)/shard_map/ppermute | solution.py:508
  76.5 4.5 %pair_forces.12 = (f32[3,3072]{1,0:T(4,128)S(1)}, f32[1,1024]{1,0:T(1,128)S(1)}) custom-call(f32[3,40]{1,0:T(4,128)S(1)} %copy-done.5, f32[4,16384]{1,0:T(4,128)S(1)} %copy-done.2, f32[3,40]{1,0:T(4,128)S(1)} %copy-done.5, s32[16,16384]{1,0:T(8,128)S(1)} %copy-done.1, bf16[640,256]{1,0:T(8,128)(2,1)S(1)} %maximum_add_fusion.rest_0_.p0), custom_call_target="tpu_custom_call" | custom-call | flops 240000000 | bytes 393216 | tf_op jit(solution)/shard_map/pair_forces/pallas_call | solution.py:88
  81.1 0.1 broadcast_add_fusion
  81.1 4.1 %collective-permute-start.20 = (bf16[640,256]{1,0:T(8,128)(2,1)S(1)}, bf16[640,256]{1,0:T(8,128)(2,1)S(1)}, u32[]{:S(2)}, u32[]{:S(2)}) collective-permute-start(bf16[640,256]{1,0:T(8,128)(2,1)S(1)} %get-tuple-element.52.p1), channel_id=1, source_target_pairs={{0,1},{1,0},{2,3},{3,2},{4,5},{5,4},{6,7},{7,6},{8,9},{9,8},{10,11... | collective-permute-start | bytes 983048 | tf_op jit(solution)/shard_map/ppermute | solution.py:508
  85.2 0.1 collective-permute-start.21
  85.3 0.4 collective-permute-start.22
  85.7 0.6 collective-permute-start.23
  86.3 0.1 collective-permute-done.20.p5
  86.4 0.5 collective-permute-done.21.p6
  86.9 0.5 collective-permute-done.22.p7
  87.4 6.7 %second_layer.1 = (f32[128,128]{1,0:T(8,128)}, f32[1,128]{1,0:T(1,128)}) custom-call(s32[1]{0:T(128)} %bitcast.me, s32[1280,1]{1,0:T(8,128)S(1)} %reshape.14.ids.ids_in, bf16[1280,128]{1,0:T(8,128)(2,1)S(1)} %get-tuple-element.27.basis.basis_in, f32[40,384]{1,0:T(8,128)S(1)} %get-tuple-element.32.feat1, f32[2,8,256]{2,1,0:T(8,128)S(1)} %copy-done.7, ...), custom_call_target="tpu_custom_call" | custom-call | tf_op jit(solution)/shard_map/second_layer/pallas_call | solution.py:399
  94.1 9.1 %all-to-all-start.1 = ((f32[128,1,128]{2,1,0:T(1,128)}), f32[128,1,128]{2,1,0:T(1,128)S(1)}, u32[]{:S(2)}, u32[]{:S(2)}) async-start(f32[128,1,128]{2,1,0:T(1,128)} %bitcast.9), calls=%async_computation.1 | async-start | bytes 131072 | tf_op jit(solution)/shard_map/all_to_all | solution.py:584
  103.2 0.7 copy-done.15
  103.9 0.5 slice_bitcast_fusion
  104.4 2.7 %pair_forces.15 = (f32[3,1536]{1,0:T(4,128)S(1)}, f32[1,1024]{1,0:T(1,128)}) custom-call(f32[4,1024]{1,0:T(4,128)S(1)} %collective-permute-done.23.left, f32[4,16384]{1,0:T(4,128)S(1)} %copy-done.2, f32[4,1024]{1,0:T(4,128)S(1)} %collective-permute-done.24.right, s32[16,16384]{1,0:T(8,128)S(1)} %copy-done.1, f32[128,128]{1,0:T(8,128)} %get-tuple-element.38.rest_0_), custom_call_target="tpu_custom_call" | custom-call | flops 120000000 | bytes 196608 | tf_op jit(solution)/shard_map/pair_forces/pallas_call | solution.py:88
  107.1 2.7 %pair_forces.13 = (f32[3,1536]{1,0:T(4,128)S(1)}, f32[1,1024]{1,0:T(1,128)}) custom-call(f32[4,1024]{1,0:T(4,128)S(1)} %collective-permute-done.23.left, f32[4,16384]{1,0:T(4,128)S(1)} %copy-done.2, f32[4,1024]{1,0:T(4,128)S(1)} %collective-permute-done.24.right, s32[16,16384]{1,0:T(8,128)S(1)} %copy-done.1, f32[128,128]{1,0:T(8,128)} %get-tuple-element.38.rest_0_), custom_call_target="tpu_custom_call" | custom-call | flops 120000000 | bytes 196608 | tf_op jit(solution)/shard_map/pair_forces/pallas_call | solution.py:88
  109.8 3.1 %pair_forces.14 = (f32[3,2048]{1,0:T(4,128)S(1)}, f32[1,1024]{1,0:T(1,128)}) custom-call(f32[3,40]{1,0:T(4,128)S(1)} %copy-done.5, f32[4,16384]{1,0:T(4,128)S(1)} %copy-done.2, f32[3,40]{1,0:T(4,128)S(1)} %copy-done.5, s32[16,16384]{1,0:T(8,128)S(1)} %copy-done.1, f32[128,128]{1,0:T(8,128)} %get-tuple-element.38.rest_0_), custom_call_target="tpu_custom_call" | custom-call | flops 160000000 | bytes 262144 | tf_op jit(solution)/shard_map/pair_forces/pallas_call | solution.py:88
  112.9 0.3 all-to-all-done.1
  113.2 8.2 %embed_forces.1 = f32[3,16384]{1,0:T(4,128)} custom-call(f32[4,16384]{1,0:T(4,128)S(1)} %copy-done.2, f32[128,256]{1,0:T(8,128)S(1)} %bitcast.20, f32[128,128]{1,0:T(8,128)S(1)} %bitcast.21, s32[1,8]{1,0:T(1,128)S(1)} %copy-done.10, s32[1]{0:T(128)S(6)} %copy.31.count_in, bf16[48,5120]{1,0:T(8,128)(2,1)S(1)} %copy-done.4, bf16[48,1024]{1,0:T(8,128)(2,1)S(1)} %copy-done.8, ...), custom_call_target="tpu_custom_call" | custom-call | tf_op jit(solution)/shard_map/embed_forces/pallas_call | solution.py:472
  (52 shorter events, 0.2 us)
Async XLA Ops:
  0.6 13.7 %copy-start.2 = (f32[4,16384]{1,0:T(4,128)S(1)}, f32[4,16384]{1,0:T(4,128)}, u32[]{:S(2)}) copy-start(f32[4,16384]{1,0:T(4,128)} %mm.3) | copy-start | bytes 786436
  2.1 12.2 %copy-start.5 = (f32[3,40]{1,0:T(4,128)S(1)}, f32[3,40]{1,0:T(4,128)}, u32[]{:S(2)}) copy-start(f32[3,40]{1,0:T(4,128)} %right.11) | copy-start | bytes 1444
  2.1 12.2 %copy-start.7 = (f32[2,8,256]{2,1,0:T(8,128)S(1)}, f32[2,8,256]{2,1,0:T(8,128)}, u32[]{:S(2)}) copy-start(f32[2,8,256]{2,1,0:T(8,128)} %radial_in.1) | copy-start | bytes 49156
  2.1 21.7 %all-to-all-start = ((f32[128,1,256]{2,1,0:T(1,128)}), f32[128,1,256]{2,1,0:T(1,128)S(1)}, u32[]{:S(2)}, u32[]{:S(2)}) async-start(f32[128,1,256]{2,1,0:T(1,128)} %spread.1), calls=%async_computation | async-start | bytes 262144 | tf_op jit(solution)/shard_map/all_to_all | solution.py:535
  13.6 0.7 copy-start.10
  14.4 1.2 %copy-start = (s32[16,16384]{1,0:T(8,128)S(1)}, s32[16,16384]{1,0:T(8,128)}, u32[]{:S(2)}) copy-start(s32[16,16384]{1,0:T(8,128)} %nb.15) | copy-start | bytes 3145732
  23.8 8.8 %copy-start.14 = (s32[40,32]{0,1:T(8,128)S(1)}, s32[40,32]{0,1:T(8,128)}, u32[]{:S(2)}) copy-start(s32[40,32]{0,1:T(8,128)} %param.20) | copy-start | bytes 15364
  23.9 24.9 %copy-start.1 = (s32[16,16384]{1,0:T(8,128)S(1)}, s32[16,16384]{1,0:T(8,128)}, u32[]{:S(2)}) copy-start(s32[16,16384]{1,0:T(8,128)} %nb.15) | copy-start | bytes 3145732
  28.6 1.3 %collective-permute-start = (f32[40,128]{1,0:T(8,128)S(1)}, f32[40,128]{1,0:T(8,128)S(1)}, u32[]{:S(2)}, u32[]{:S(2)}) collective-permute-start(f32[40,128]{1,0:T(8,128)S(1)} %get-tuple-element.26.after), channel_id=1, source_target_pairs={{0,1},{1,0},{2,3},{3,2},{4,5},{5,4},{6,7},{7,6},{8,9},{9,8},{10,11... | collective-permute-start | bytes 61448 | tf_op jit(solution)/shard_map/ppermute | solution.py:508
  29.9 7.1 %collective-permute-start.1 = (f32[40,128]{1,0:T(8,128)S(1)}, f32[40,128]{1,0:T(8,128)S(1)}, u32[]{:S(2)}, u32[]{:S(2)}) collective-permute-start(f32[40,128]{1,0:T(8,128)S(1)} %add.124), channel_id=1, source_target_pairs={{0,4},{1,33},{2,6},{3,35},{4,8},{5,37},{6,10},{7,39},{8,12},{9,41}... | collective-permute-start | bytes 61448 | tf_op jit(solution)/shard_map/ppermute | solution.py:502
  30.2 6.8 %collective-permute-start.2 = (f32[40,128]{1,0:T(8,128)S(1)}, f32[40,128]{1,0:T(8,128)S(1)}, u32[]{:S(2)}, u32[]{:S(2)}) collective-permute-start(f32[40,128]{1,0:T(8,128)S(1)} %add.124), channel_id=1, source_target_pairs={{0,8},{1,65},{2,10},{3,67},{4,12},{5,69},{6,14},{7,71},{8,0},{9,73... | collective-permute-start | bytes 61448 | tf_op jit(solution)/shard_map/ppermute | solution.py:502
  32.0 5.1 %collective-permute-start.3 = (f32[40,128]{1,0:T(8,128)S(1)}, f32[40,128]{1,0:T(8,128)S(1)}, u32[]{:S(2)}, u32[]{:S(2)}) collective-permute-start(f32[40,128]{1,0:T(8,128)S(1)} %add.124), channel_id=1, source_target_pairs={{0,12},{1,97},{2,14},{3,99},{4,0},{5,101},{6,2},{7,103},{8,4},{9,1... | collective-permute-start | bytes 61448 | tf_op jit(solution)/shard_map/ppermute | solution.py:502
  32.7 0.7 copy-start.12
  32.7 0.7 copy-start.13
  33.4 0.7 copy-start.11
  37.0 4.8 %collective-permute-start.4 = (f32[40,128]{1,0:T(8,128)S(1)}, f32[40,128]{1,0:T(8,128)S(1)}, u32[]{:S(2)}, u32[]{:S(2)}) collective-permute-start(f32[40,128]{1,0:T(8,128)S(1)} %add_add_fusion.2), channel_id=1, source_target_pairs={{0,32},{1,3},{2,34},{3,17},{4,36},{5,7},{6,38},{7,21},{8,40},{9,11... | collective-permute-start | bytes 61448 | tf_op jit(solution)/shard_map/ppermute | solution.py:502
  38.2 4.1 %collective-permute-start.5 = (f32[40,128]{1,0:T(8,128)S(1)}, f32[40,128]{1,0:T(8,128)S(1)}, u32[]{:S(2)}, u32[]{:S(2)}) collective-permute-start(f32[40,128]{1,0:T(8,128)S(1)} %add_add_fusion.2), channel_id=1, source_target_pairs={{0,64},{1,17},{2,66},{3,19},{4,68},{5,21},{6,70},{7,23},{8,72},{9,... | collective-permute-start | bytes 61448 | tf_op jit(solution)/shard_map/ppermute | solution.py:502
  40.7 2.6 %collective-permute-start.6 = (f32[40,128]{1,0:T(8,128)S(1)}, f32[40,128]{1,0:T(8,128)S(1)}, u32[]{:S(2)}, u32[]{:S(2)}) collective-permute-start(f32[40,128]{1,0:T(8,128)S(1)} %add_add_fusion.2), channel_id=1, source_target_pairs={{0,96},{1,19},{2,98},{3,1},{4,100},{5,23},{6,102},{7,5},{8,104},{9... | collective-permute-start | bytes 61448 | tf_op jit(solution)/shard_map/ppermute | solution.py:502
  43.3 7.0 %collective-permute-start.7 = (f32[40,128]{1,0:T(8,128)S(1)}, f32[40,128]{1,0:T(8,128)S(1)}, u32[]{:S(2)}, u32[]{:S(2)}) collective-permute-start(f32[40,128]{1,0:T(8,128)S(1)} %add_add_fusion.1.rest_0_), channel_id=1, source_target_pairs={{0,2},{1,5},{2,16},{3,7},{4,6},{5,9},{6,20},{7,11},{8,10},{9,13},{... | collective-permute-start | bytes 61448 | tf_op jit(solution)/shard_map/ppermute | solution.py:502
  45.1 5.2 %collective-permute-start.8 = (f32[40,128]{1,0:T(8,128)S(1)}, f32[40,128]{1,0:T(8,128)S(1)}, u32[]{:S(2)}, u32[]{:S(2)}) collective-permute-start(f32[40,128]{1,0:T(8,128)S(1)} %add_add_fusion.1.rest_0_), channel_id=1, source_target_pairs={{0,16},{1,9},{2,18},{3,11},{4,20},{5,13},{6,22},{7,15},{8,24},{9,1... | collective-permute-start | bytes 61448 | tf_op jit(solution)/shard_map/ppermute | solution.py:502
  47.8 2.9 %collective-permute-start.9 = (f32[40,128]{1,0:T(8,128)S(1)}, f32[40,128]{1,0:T(8,128)S(1)}, u32[]{:S(2)}, u32[]{:S(2)}) collective-permute-start(f32[40,128]{1,0:T(8,128)S(1)} %add_add_fusion.1.rest_0_), channel_id=1, source_target_pairs={{0,18},{1,13},{2,0},{3,15},{4,22},{5,1},{6,4},{7,3},{8,26},{9,5},{... | collective-permute-start | bytes 61448 | tf_op jit(solution)/shard_map/ppermute | solution.py:502
  48.7 2.0 %copy-start.3 = (bf16[2,256,256]{2,1,0:T(8,128)(2,1)S(1)}, bf16[2,256,256]{2,1,0:T(8,128)(2,1)}, u32[]{:S(2)}) copy-start(bf16[2,256,256]{2,1,0:T(8,128)(2,1)} %mix_in.1) | copy-start | bytes 786436
  48.7 2.0 %copy-start.6 = (bf16[2,256,256]{2,1,0:T(8,128)(2,1)S(1)}, bf16[2,256,256]{2,1,0:T(8,128)(2,1)}, u32[]{:S(2)}) copy-start(bf16[2,256,256]{2,1,0:T(8,128)(2,1)} %msg.1) | copy-start | bytes 786436
  50.7 0.7 copy-start.9
  53.4 4.4 %collective-permute-start.10 = (bf16[40,256]{1,0:T(8,128)(2,1)S(1)}, bf16[40,256]{1,0:T(8,128)(2,1)S(1)}, u32[]{:S(2)}, u32[]{:S(2)}) collective-permute-start(bf16[40,256]{1,0:T(8,128)(2,1)S(1)} %get-tuple-element.33.rest_0_), channel_id=1, source_target_pairs={{0,4},{1,33},{2,6},{3,35},{4,8},{5,37},{6,10},{7,39},{8,12},{9,41}... | collective-permute-start | bytes 61448 | tf_op jit(solution)/shard_map/ppermute | solution.py:502
  53.7 4.1 %collective-permute-start.11 = (bf16[40,256]{1,0:T(8,128)(2,1)S(1)}, bf16[40,256]{1,0:T(8,128)(2,1)S(1)}, u32[]{:S(2)}, u32[]{:S(2)}) collective-permute-start(bf16[40,256]{1,0:T(8,128)(2,1)S(1)} %get-tuple-element.33.rest_0_), channel_id=1, source_target_pairs={{0,8},{1,65},{2,10},{3,67},{4,12},{5,69},{6,14},{7,71},{8,0},{9,73... | collective-permute-start | bytes 61448 | tf_op jit(solution)/shard_map/ppermute | solution.py:502
  54.6 3.5 %collective-permute-start.12 = (bf16[40,256]{1,0:T(8,128)(2,1)S(1)}, bf16[40,256]{1,0:T(8,128)(2,1)S(1)}, u32[]{:S(2)}, u32[]{:S(2)}) collective-permute-start(bf16[40,256]{1,0:T(8,128)(2,1)S(1)} %get-tuple-element.33.rest_0_), channel_id=1, source_target_pairs={{0,12},{1,97},{2,14},{3,99},{4,0},{5,101},{6,2},{7,103},{8,4},{9,1... | collective-permute-start | bytes 61448 | tf_op jit(solution)/shard_map/ppermute | solution.py:502
  58.0 6.5 %collective-permute-start.13 = (bf16[160,256]{1,0:T(8,128)(2,1)S(1)}, bf16[160,256]{1,0:T(8,128)(2,1)S(1)}, u32[]{:S(2)}, u32[]{:S(2)}) collective-permute-start(bf16[160,256]{1,0:T(8,128)(2,1)S(1)} %maximum_add_fusion.1.rest_0_), channel_id=1, source_target_pairs={{0,32},{1,3},{2,34},{3,17},{4,36},{5,7},{6,38},{7,21},{8,40},{9,11... | collective-permute-start | bytes 245768 | tf_op jit(solution)/shard_map/ppermute | solution.py:502
  58.1 6.5 %collective-permute-start.14 = (bf16[160,256]{1,0:T(8,128)(2,1)S(1)}, bf16[160,256]{1,0:T(8,128)(2,1)S(1)}, u32[]{:S(2)}, u32[]{:S(2)}) collective-permute-start(bf16[160,256]{1,0:T(8,128)(2,1)S(1)} %maximum_add_fusion.1.rest_0_), channel_id=1, source_target_pairs={{0,64},{1,17},{2,66},{3,19},{4,68},{5,21},{6,70},{7,23},{8,72},{9,... | collective-permute-start | bytes 245768 | tf_op jit(solution)/shard_map/ppermute | solution.py:502
  61.3 3.3 %collective-permute-start.15 = (bf16[160,256]{1,0:T(8,128)(2,1)S(1)}, bf16[160,256]{1,0:T(8,128)(2,1)S(1)}, u32[]{:S(2)}, u32[]{:S(2)}) collective-permute-start(bf16[160,256]{1,0:T(8,128)(2,1)S(1)} %maximum_add_fusion.1.rest_0_), channel_id=1, source_target_pairs={{0,96},{1,19},{2,98},{3,1},{4,100},{5,23},{6,102},{7,5},{8,104},{9... | collective-permute-start | bytes 245768 | tf_op jit(solution)/shard_map/ppermute | solution.py:502
  64.7 16.3 %collective-permute-start.16 = (bf16[640,256]{1,0:T(8,128)(2,1)S(1)}, bf16[640,256]{1,0:T(8,128)(2,1)S(1)}, u32[]{:S(2)}, u32[]{:S(2)}) collective-permute-start(bf16[640,256]{1,0:T(8,128)(2,1)S(1)} %maximum_add_fusion.rest_0_.p0), channel_id=1, source_target_pairs={{0,2},{1,5},{2,16},{3,7},{4,6},{5,9},{6,20},{7,11},{8,10},{9,13},{... | collective-permute-start | bytes 983048 | tf_op jit(solution)/shard_map/ppermute | solution.py:502
  65.2 15.8 %collective-permute-start.17 = (bf16[640,256]{1,0:T(8,128)(2,1)S(1)}, bf16[640,256]{1,0:T(8,128)(2,1)S(1)}, u32[]{:S(2)}, u32[]{:S(2)}) collective-permute-start(bf16[640,256]{1,0:T(8,128)(2,1)S(1)} %maximum_add_fusion.rest_0_.p0), channel_id=1, source_target_pairs={{0,16},{1,9},{2,18},{3,11},{4,20},{5,13},{6,22},{7,15},{8,24},{9,1... | collective-permute-start | bytes 983048 | tf_op jit(solution)/shard_map/ppermute | solution.py:502
  68.1 13.0 %collective-permute-start.18 = (bf16[640,256]{1,0:T(8,128)(2,1)S(1)}, bf16[640,256]{1,0:T(8,128)(2,1)S(1)}, u32[]{:S(2)}, u32[]{:S(2)}) collective-permute-start(bf16[640,256]{1,0:T(8,128)(2,1)S(1)} %maximum_add_fusion.rest_0_.p0), channel_id=1, source_target_pairs={{0,18},{1,13},{2,0},{3,15},{4,22},{5,1},{6,4},{7,3},{8,26},{9,5},{... | collective-permute-start | bytes 983048 | tf_op jit(solution)/shard_map/ppermute | solution.py:502
  68.6 17.7 %collective-permute-start.19 = (bf16[640,256]{1,0:T(8,128)(2,1)S(1)}, bf16[640,256]{1,0:T(8,128)(2,1)S(1)}, u32[]{:S(2)}, u32[]{:S(2)}) collective-permute-start(bf16[640,256]{1,0:T(8,128)(2,1)S(1)} %maximum_add_fusion.rest_0_.p0), channel_id=1, source_target_pairs={{0,1},{1,0},{2,3},{3,2},{4,5},{5,4},{6,7},{7,6},{8,9},{9,8},{10,11... | collective-permute-start | bytes 983048 | tf_op jit(solution)/shard_map/ppermute | solution.py:508
  81.1 5.3 %collective-permute-start.20 = (bf16[640,256]{1,0:T(8,128)(2,1)S(1)}, bf16[640,256]{1,0:T(8,128)(2,1)S(1)}, u32[]{:S(2)}, u32[]{:S(2)}) collective-permute-start(bf16[640,256]{1,0:T(8,128)(2,1)S(1)} %get-tuple-element.52.p1), channel_id=1, source_target_pairs={{0,1},{1,0},{2,3},{3,2},{4,5},{5,4},{6,7},{7,6},{8,9},{9,8},{10,11... | collective-permute-start | bytes 983048 | tf_op jit(solution)/shard_map/ppermute | solution.py:508
  85.2 1.7 %collective-permute-start.21 = (bf16[640,256]{1,0:T(8,128)(2,1)S(1)}, bf16[640,256]{1,0:T(8,128)(2,1)S(1)}, u32[]{:S(2)}, u32[]{:S(2)}) collective-permute-start(bf16[640,256]{1,0:T(8,128)(2,1)S(1)} %get-tuple-element.51.p2), channel_id=1, source_target_pairs={{0,1},{1,0},{2,3},{3,2},{4,5},{5,4},{6,7},{7,6},{8,9},{9,8},{10,11... | collective-permute-start | bytes 983048 | tf_op jit(solution)/shard_map/ppermute | solution.py:508
  85.3 2.1 %collective-permute-start.22 = (bf16[640,256]{1,0:T(8,128)(2,1)S(1)}, bf16[640,256]{1,0:T(8,128)(2,1)S(1)}, u32[]{:S(2)}, u32[]{:S(2)}) collective-permute-start(bf16[640,256]{1,0:T(8,128)(2,1)S(1)} %get-tuple-element.50.p3), channel_id=1, source_target_pairs={{0,1},{1,0},{2,3},{3,2},{4,5},{5,4},{6,7},{7,6},{8,9},{9,8},{10,11... | collective-permute-start | bytes 983048 | tf_op jit(solution)/shard_map/ppermute | solution.py:508
  85.7 18.7 %collective-permute-start.23 = (f32[4,1024]{1,0:T(4,128)S(1)}, f32[4,1024]{1,0:T(4,128)S(1)}, u32[]{:S(2)}, u32[]{:S(2)}) collective-permute-start(f32[4,1024]{1,0:T(4,128)S(1)} %get-tuple-element.49), channel_id=1, source_target_pairs={{0,1},{1,2},{2,3},{3,4},{4,5},{5,6},{6,7},{7,8},{8,9},{9,10},{10,1... | collective-permute-start | bytes 49160 | tf_op jit(solution)/shard_map/ppermute | solution.py:565
  86.3 18.0 %collective-permute-start.24 = (f32[4,1024]{1,0:T(4,128)S(1)}, f32[4,1024]{1,0:T(4,128)S(1)}, u32[]{:S(2)}, u32[]{:S(2)}) collective-permute-start(f32[4,1024]{1,0:T(4,128)S(1)} %get-tuple-element.48), channel_id=1, source_target_pairs={{1,0},{2,1},{3,2},{4,3},{5,4},{6,5},{7,6},{8,7},{9,8},{10,9},{11,1... | collective-permute-start | bytes 49160 | tf_op jit(solution)/shard_map/ppermute | solution.py:566
  94.1 19.0 %all-to-all-start.1 = ((f32[128,1,128]{2,1,0:T(1,128)}), f32[128,1,128]{2,1,0:T(1,128)S(1)}, u32[]{:S(2)}, u32[]{:S(2)}) async-start(f32[128,1,128]{2,1,0:T(1,128)} %bitcast.9), calls=%async_computation.1 | async-start | bytes 131072 | tf_op jit(solution)/shard_map/all_to_all | solution.py:584
  103.2 0.7 copy-start.15
  109.8 3.4 %copy-start.4 = (bf16[48,5120]{1,0:T(8,128)(2,1)S(1)}, bf16[48,5120]{1,0:T(8,128)(2,1)}, u32[]{:S(2)}) copy-start(bf16[48,5120]{1,0:T(8,128)(2,1)} %get-tuple-element.39.atoms_in) | copy-start | bytes 1474564
  109.8 3.4 %copy-start.8 = (bf16[48,1024]{1,0:T(8,128)(2,1)S(1)}, bf16[48,1024]{1,0:T(8,128)(2,1)}, u32[]{:S(2)}) copy-start(bf16[48,1024]{1,0:T(8,128)(2,1)} %get-tuple-element.40.slots_in) | copy-start | bytes 294916

commit v4 on v3

--- a/solution.py
+++ b/solution.py
@@ -455,7 +455,7 @@
             )
         return carry
 
-    lax.fori_loop(0, ML_DEV // 2, tile, 0, unroll=10)
+    lax.fori_loop(0, ML_DEV // 2, tile, 0, unroll=20)
     for copy in copies[2:]:
         copy.wait()
     for s in range(nslots):
@@ -484,7 +484,7 @@
             pltpu.VMEM(slots.shape, slots.dtype),
             pltpu.SemaphoreType.DMA((4 + len(pieces),)),
         ],
-        compiler_params=vmem_mib(12),
+        compiler_params=vmem_mib(28),
         name="embed_forces",
     )(mm, tab, charges, blocks, count, atoms, slots, *pieces)
 
@@ -536,7 +536,7 @@
     tab = tab.reshape(NDEV, 2 * LANES)
     ids = ml_edges.reshape(-1, 1)
     blocks = own_rows // LANES
-    cuts = (0, 12, 44, 52, 60, 76, 100, blocks - 12, blocks)
+    cuts = (0, 12, 44, 52, 68, 100, blocks - 12, blocks)
     far = ml_coords
 
     def pairs(i, *after, before=far, behind=far):
@@ -551,12 +551,11 @@
     pot = functools.reduce(jnp.add, ring_parts(pot, "c"))
     pot = stand(functools.reduce(jnp.add, stage_parts(pot, 0)), zero)
     pot = functools.reduce(jnp.add, stage_parts(pot, 1))
-    pieces[2], zero = pairs(2, pot)
-    pot = stand(functools.reduce(jnp.add, stage_parts(pot, 2)), zero)
+    pot = functools.reduce(jnp.add, stage_parts(pot, 2))
     feat1, proj = first_layer(
         me, ids, pot, basis, kinds, species_table, rows, msg_weight, radial_weight, mix_weight
     )
-    for i, stage in ((3, 0), (4, 1)):
+    for i, stage in ((2, 0), (3, 1)):
         pieces[i], zero = pairs(i, proj)
         proj = stand(jnp.concatenate(stage_parts(proj, stage), axis=0), zero)
     halo = HALO_BLOCKS * LANES
@@ -564,7 +563,7 @@
     down = [(j, i) for i, j in up]
     before = lax.ppermute(stand(mm_atoms[:, own_rows - halo :], zero), ALL, up)
     behind = lax.ppermute(stand(mm_atoms[:, :halo], zero), ALL, down)
-    pieces[5], zero = pairs(5, proj)
+    pieces[4], zero = pairs(4, proj)
     parts = stage_parts(proj, 2)
     parts[1:] = [stand(part, zero) for part in parts[1:]]
     parts = parts + [ring_parts(part, "c")[1] for part in parts]
@@ -578,8 +577,8 @@
         rows,
         *parts,
     )
-    pieces[6], _ = pairs(6, charges)
-    for i in (0, 7):
+    pieces[5], _ = pairs(5, charges)
+    for i in (0, 6):
         pieces[i], _ = pairs(i, charges, before=before, behind=behind)
     charges = lax.all_to_all(charges, ALL, 0, 0, tiled=True)
     mm_force = embed(embed_blocks, embed_count, mm_atoms, tab, charges, atoms, slots, pieces, kappa)

time: 122 us -> 121 us (level)
  waiting for transfers between devices: 6.62 us -> 8.36 us
  starting transfers between devices: 57.2 us -> 55.7 us
    ppermute x18, waiting for transfers between devices: 2.18 us -> 3.84 us  [stage_parts(): parts.append(lax.ppermute(value, ALL, pairs))]
    ppermute x5, starting transfers between devices: 12.9 us -> 11.4 us  [ring_parts(): lax.ppermute(value, axis, [(i, (i + k) % n) for i in range(n)])]
    pallas_call x8 -> x7, Pallas kernels: 25.2 us -> 25 us  [pair_forces(): pl.pallas_call(functools.partial(pair_kernel, first, count), grid=(count...]
  transfers between devices with their start and end apart: 27 -> 27, of which waited for: 11 -> 12; matrix products, arithmetic and copies ran while one was open for 1% -> 1% of each run, Pallas kernels for 29% -> 29%
where the time goes in v4:
time: 121 us
  starting transfers between devices  55.7 us (46%)
  Pallas kernels  50.5 us (42%)
  waiting for transfers between devices  8.36 us (7%)
  local copies, waits for them, and re-layouts  3.87 us (3%)
  between operations  1.84 us (2%)
    pallas_call x7, Pallas kernels, pair_forces(): pl.pallas_call(functools.partial(pair_kernel, first, count), grid=(count...  25 us
    ppermute x18, starting transfers between devices, stage_parts(): parts.append(lax.ppermute(value, ALL, pairs))  23.1 us
    all_to_all x1, starting transfers between devices, body(): lax.all_to_all(spread(ml_coords, ml_species[None]), ALL, 0, 0, tiled=True)  11.5 us
    ppermute x5, starting transfers between devices, ring_parts(): lax.ppermute(value, axis, [(i, (i + k) % n) for i in range(n)])  11.4 us
    all_to_all x1, starting transfers between devices, body(): charges = lax.all_to_all(charges, ALL, 0, 0, tiled=True)  9.09 us
    pallas_call x1, Pallas kernels, embed(): pl.pallas_call(functools.partial(embed_kernel, scale), out_shape=jax.Shap...  7.8 us
    pallas_call x1, Pallas kernels, second_layer(): pl.pallas_call(second_layer_kernel, out_shape=(jax.ShapeDtypeStruct((NDEV...  6.72 us
    pallas_call x1, Pallas kernels, field(): pl.pallas_call(functools.partial(field_kernel, scale), out_shape=(jax.Sha...  4.69 us
  transfers between devices with their start and end apart: 27, of which 12 were waited for; matrix products, arithmetic and copies ran while one was open for 1% of the time, Pallas kernels for 29%

profile of v4, /device:TPU:1, one launch (start us, length us, event | category | flops | bytes accessed | tf_op | source)
XLA Modules:
  0.0 120.5 jit_solution(15116677310873785589)
XLA Ops:
  0.6 1.5 %spread.1 = f32[128,1,256]{2,1,0:T(1,128)} custom-call(f32[3,40]{1,0:T(4,128)} %right.9, s32[1,40]{1,0:T(1,128)} %bitcast.25), custom_call_target="tpu_custom_call" | custom-call | tf_op jit(solution)/shard_map/spread/pallas_call | solution.py:123
  2.1 11.5 %all-to-all-start = ((f32[128,1,256]{2,1,0:T(1,128)}), f32[128,1,256]{2,1,0:T(1,128)S(1)}, u32[]{:S(2)}, u32[]{:S(2)}) async-start(f32[128,1,256]{2,1,0:T(1,128)} %spread.1), calls=%async_computation | async-start | bytes 262144 | tf_op jit(solution)/shard_map/all_to_all | solution.py:535
  13.6 0.0 copy-start.10
  14.4 0.0 copy-start
  14.4 1.2 %copy-done = s32[16,16384]{1,0:T(8,128)S(1)} copy-done((s32[16,16384]{1,0:T(8,128)S(1)}, s32[16,16384]{1,0:T(8,128)}, u32[]{:S(2)}) %copy-start) | copy-done | bytes 1048600
  15.6 6.0 %pair_forces.7 = (f32[3,4096]{1,0:T(4,128)S(1)}, f32[1,1024]{1,0:T(1,128)}) custom-call(f32[3,40]{1,0:T(4,128)S(1)} %copy-done.6, f32[4,16384]{1,0:T(4,128)S(1)} %copy-done.2, f32[3,40]{1,0:T(4,128)S(1)} %copy-done.6, s32[16,16384]{1,0:T(8,128)S(1)} %copy-done, s32[1,8]{1,0:T(1,128)S(1)} %copy-done.10, f32[2,8,256]{2,1,0:T(8,128)S(1)} %copy-done.7), custom_call_target="tpu_custom_call" | custom-call | flops 320000000 | bytes 524288 | tf_op jit(solution)/shard_map/pair_forces/pallas_call | solution.py:88
  21.6 2.3 %all-to-all-done = f32[128,1,256]{2,1,0:T(1,128)S(1)} async-done(((f32[128,1,256]{2,1,0:T(1,128)}), f32[128,1,256]{2,1,0:T(1,128)S(1)}, u32[]{:S(2)}, u32[]{:S(2)}) %all-to-all-start) | async-done | bytes 131104 | tf_op jit(solution)/shard_map/all_to_all | solution.py:535
  23.8 4.7 %field.1 = (f32[40,128]{1,0:T(8,128)S(1)}, bf16[48,5120]{1,0:T(8,128)(2,1)}, bf16[48,1024]{1,0:T(8,128)(2,1)}) custom-call(s32[1,8]{1,0:T(1,128)S(1)} %copy-done.10, s32[1]{0:T(128)S(6)} %copy.31.count_in, f32[4,16384]{1,0:T(4,128)S(1)} %copy-done.2, f32[128,256]{1,0:T(8,128)S(1)} %bitcast.16, f32[3,4096]{1,0:T(4,128)S(1)} %get-tuple-element.23.after.rest_1_), custom_call_target="tpu_custom_call" | custom-call | tf_op jit(solution)/shard_map/field/pallas_call | solution.py:193
  28.5 0.5 collective-permute-start
  29.0 0.8 collective-permute-done
  29.9 0.3 collective-permute-start.1
  30.2 1.8 %collective-permute-start.2 = (f32[40,128]{1,0:T(8,128)S(1)}, f32[40,128]{1,0:T(8,128)S(1)}, u32[]{:S(2)}, u32[]{:S(2)}) collective-permute-start(f32[40,128]{1,0:T(8,128)S(1)} %add.114), channel_id=1, source_target_pairs={{0,8},{1,65},{2,10},{3,67},{4,12},{5,69},{6,14},{7,71},{8,0},{9,73... | collective-permute-start | bytes 61448 | tf_op jit(solution)/shard_map/ppermute | solution.py:502
  31.9 0.7 collective-permute-start.3
  32.7 0.1 copy.23
  32.7 0.7 reshape.14.ids.ids_in
  33.5 0.7 copy-done.11
  34.1 2.9 %geometry.1 = (bf16[1280,128]{1,0:T(8,128)(2,1)S(1)}, bf16[1344,128]{1,0:T(8,128)(2,1)S(1)}, f32[4,256]{1,0:T(4,128)S(1)}, f32[1,128]{1,0:T(1,128)S(1)}) custom-call(s32[1]{0:T(128)} %bitcast.me, s32[1280,1]{1,0:T(8,128)S(1)} %reshape.14.ids.ids_in, f32[128,256]{1,0:T(8,128)S(1)} %bitcast.17, f32[1,256]{1,0:T(1,128)S(1)} %bitcast.21, f32[1,256]{1,0:T(1,128)S(1)} %bitcast.22, ...), custom_call_target="tpu_custom_call" | custom-call | tf_op jit(solution)/shard_map/geometry/pallas_call | solution.py:270
  37.0 0.0 copy-start.3
  37.0 0.0 copy-start.9
  37.1 1.2 collective-permute-start.4
  38.2 2.5 %collective-permute-start.5 = (f32[40,128]{1,0:T(8,128)S(1)}, f32[40,128]{1,0:T(8,128)S(1)}, u32[]{:S(2)}, u32[]{:S(2)}) collective-permute-start(f32[40,128]{1,0:T(8,128)S(1)} %add_add_fusion.2), channel_id=1, source_target_pairs={{0,64},{1,17},{2,66},{3,19},{4,68},{5,21},{6,70},{7,23},{8,72},{9,... | collective-permute-start | bytes 61448 | tf_op jit(solution)/shard_map/ppermute | solution.py:502
  40.7 1.1 collective-permute-start.6
  41.8 0.5 collective-permute-done.5
  42.4 1.0 collective-permute-done.6
  43.4 1.8 %collective-permute-start.7 = (f32[40,128]{1,0:T(8,128)S(1)}, f32[40,128]{1,0:T(8,128)S(1)}, u32[]{:S(2)}, u32[]{:S(2)}) collective-permute-start(f32[40,128]{1,0:T(8,128)S(1)} %add_add_fusion.1), channel_id=1, source_target_pairs={{0,2},{1,5},{2,16},{3,7},{4,6},{5,9},{6,20},{7,11},{8,10},{9,13},{... | collective-permute-start | bytes 61448 | tf_op jit(solution)/shard_map/ppermute | solution.py:502
  45.2 2.6 %collective-permute-start.8 = (f32[40,128]{1,0:T(8,128)S(1)}, f32[40,128]{1,0:T(8,128)S(1)}, u32[]{:S(2)}, u32[]{:S(2)}) collective-permute-start(f32[40,128]{1,0:T(8,128)S(1)} %add_add_fusion.1), channel_id=1, source_target_pairs={{0,16},{1,9},{2,18},{3,11},{4,20},{5,13},{6,22},{7,15},{8,24},{9,1... | collective-permute-start | bytes 61448 | tf_op jit(solution)/shard_map/ppermute | solution.py:502
  47.8 0.9 collective-permute-start.9
  48.7 0.6 collective-permute-done.8
  49.3 1.4 %collective-permute-done.9 = f32[40,128]{1,0:T(8,128)S(1)} collective-permute-done((f32[40,128]{1,0:T(8,128)S(1)}, f32[40,128]{1,0:T(8,128)S(1)}, u32[]{:S(2)}, u32[]{:S(2)}) %collective-permute-start.9) | collective-permute-done | bytes 20512 | tf_op jit(solution)/shard_map/ppermute | solution.py:502
  50.8 1.9 %first_layer.1 = (f32[40,384]{1,0:T(8,128)S(1)}, bf16[40,256]{1,0:T(8,128)(2,1)S(1)}) custom-call(s32[1]{0:T(128)} %bitcast.me, s32[1280,1]{1,0:T(8,128)S(1)} %reshape.14.ids.ids_in, f32[40,128]{1,0:T(8,128)S(1)} %add_add_fusion.pot, bf16[1280,128]{1,0:T(8,128)(2,1)S(1)} %get-tuple-element.25.basis.basis_in, bf16[1344,128]{1,0:T(8,128)(2,1)S(1)} %get-tuple-element.27.kinds, ...), custom_call_target="tpu_custom_call" | custom-call | tf_op jit(solution)/shard_map/first_layer/pallas_call | solution.py:320
  52.7 0.3 collective-permute-start.10
  53.0 0.9 collective-permute-start.11
  53.9 1.6 %collective-permute-start.12 = (bf16[40,256]{1,0:T(8,128)(2,1)S(1)}, bf16[40,256]{1,0:T(8,128)(2,1)S(1)}, u32[]{:S(2)}, u32[]{:S(2)}) collective-permute-start(bf16[40,256]{1,0:T(8,128)(2,1)S(1)} %get-tuple-element.30.rest_0_), channel_id=1, source_target_pairs={{0,12},{1,97},{2,14},{3,99},{4,0},{5,101},{6,2},{7,103},{8,4},{9,1... | collective-permute-start | bytes 61448 | tf_op jit(solution)/shard_map/ppermute | solution.py:502
  55.5 1.6 %pair_forces.8 = (f32[3,1024]{1,0:T(4,128)S(1)}, f32[1,1024]{1,0:T(1,128)S(1)}) custom-call(f32[3,40]{1,0:T(4,128)S(1)} %copy-done.6, f32[4,16384]{1,0:T(4,128)S(1)} %copy-done.2, f32[3,40]{1,0:T(4,128)S(1)} %copy-done.6, s32[16,16384]{1,0:T(8,128)S(1)} %copy-done.1, bf16[40,256]{1,0:T(8,128)(2,1)S(1)} %get-tuple-element.30.rest_0_), custom_call_target="tpu_custom_call" | custom-call | flops 80000000 | bytes 131072 | tf_op jit(solution)/shard_map/pair_forces/pallas_call | solution.py:88
  57.1 0.1 collective-permute-done.11
  57.2 0.2 collective-permute-done.12
  57.4 0.1 collective-permute-start.13
  57.5 3.2 %collective-permute-start.14 = (bf16[160,256]{1,0:T(8,128)(2,1)S(1)}, bf16[160,256]{1,0:T(8,128)(2,1)S(1)}, u32[]{:S(2)}, u32[]{:S(2)}) collective-permute-start(bf16[160,256]{1,0:T(8,128)(2,1)S(1)} %maximum_add_fusion.1.rest_0_), channel_id=1, source_target_pairs={{0,64},{1,17},{2,66},{3,19},{4,68},{5,21},{6,70},{7,23},{8,72},{9,... | collective-permute-start | bytes 245768 | tf_op jit(solution)/shard_map/ppermute | solution.py:502
  60.7 0.2 collective-permute-start.15
  60.8 3.0 %pair_forces.9 = (f32[3,2048]{1,0:T(4,128)S(1)}, f32[1,1024]{1,0:T(1,128)S(1)}) custom-call(f32[3,40]{1,0:T(4,128)S(1)} %copy-done.6, f32[4,16384]{1,0:T(4,128)S(1)} %copy-done.2, f32[3,40]{1,0:T(4,128)S(1)} %copy-done.6, s32[16,16384]{1,0:T(8,128)S(1)} %copy-done.1, bf16[160,256]{1,0:T(8,128)(2,1)S(1)} %maximum_add_fusion.1.rest_0_), custom_call_target="tpu_custom_call" | custom-call | flops 160000000 | bytes 262144 | tf_op jit(solution)/shard_map/pair_forces/pallas_call | solution.py:88
  63.9 0.0 collective-permute-done.15
  64.0 0.1 maximum_add_fusion.rest_0_.p0
  64.0 0.1 collective-permute-start.16
  64.1 3.3 %collective-permute-start.17 = (bf16[640,256]{1,0:T(8,128)(2,1)S(1)}, bf16[640,256]{1,0:T(8,128)(2,1)S(1)}, u32[]{:S(2)}, u32[]{:S(2)}) collective-permute-start(bf16[640,256]{1,0:T(8,128)(2,1)S(1)} %maximum_add_fusion.rest_0_.p0), channel_id=1, source_target_pairs={{0,16},{1,9},{2,18},{3,11},{4,20},{5,13},{6,22},{7,15},{8,24},{9,1... | collective-permute-start | bytes 983048 | tf_op jit(solution)/shard_map/ppermute | solution.py:502
  67.4 0.6 collective-permute-start.18
  68.0 7.9 %collective-permute-start.19 = (bf16[640,256]{1,0:T(8,128)(2,1)S(1)}, bf16[640,256]{1,0:T(8,128)(2,1)S(1)}, u32[]{:S(2)}, u32[]{:S(2)}) collective-permute-start(bf16[640,256]{1,0:T(8,128)(2,1)S(1)} %maximum_add_fusion.rest_0_.p0), channel_id=1, source_target_pairs={{0,1},{1,0},{2,3},{3,2},{4,5},{5,4},{6,7},{7,6},{8,9},{9,8},{10,11... | collective-permute-start | bytes 983048 | tf_op jit(solution)/shard_map/ppermute | solution.py:508
  75.8 6.0 %pair_forces.10 = (f32[3,4096]{1,0:T(4,128)S(1)}, f32[1,1024]{1,0:T(1,128)S(1)}) custom-call(f32[3,40]{1,0:T(4,128)S(1)} %copy-done.6, f32[4,16384]{1,0:T(4,128)S(1)} %copy-done.2, f32[3,40]{1,0:T(4,128)S(1)} %copy-done.6, s32[16,16384]{1,0:T(8,128)S(1)} %copy-done.1, bf16[640,256]{1,0:T(8,128)(2,1)S(1)} %maximum_add_fusion.rest_0_.p0), custom_call_target="tpu_custom_call" | custom-call | flops 320000000 | bytes 524288 | tf_op jit(solution)/shard_map/pair_forces/pallas_call | solution.py:88
  81.9 0.1 broadcast_add_fusion
  81.9 2.6 %collective-permute-start.20 = (bf16[640,256]{1,0:T(8,128)(2,1)S(1)}, bf16[640,256]{1,0:T(8,128)(2,1)S(1)}, u32[]{:S(2)}, u32[]{:S(2)}) collective-permute-start(bf16[640,256]{1,0:T(8,128)(2,1)S(1)} %get-tuple-element.48.p1), channel_id=1, source_target_pairs={{0,1},{1,0},{2,3},{3,2},{4,5},{5,4},{6,7},{7,6},{8,9},{9,8},{10,11... | collective-permute-start | bytes 983048 | tf_op jit(solution)/shard_map/ppermute | solution.py:508
  84.5 0.1 collective-permute-start.21
  84.6 0.4 collective-permute-start.22
  85.1 0.6 collective-permute-start.23
  85.7 0.1 collective-permute-done.20.p5
  85.8 0.5 collective-permute-done.21.p6
  86.3 0.5 collective-permute-done.22.p7
  86.7 6.7 %second_layer.1 = (f32[128,128]{1,0:T(8,128)}, f32[1,128]{1,0:T(1,128)}) custom-call(s32[1]{0:T(128)} %bitcast.me, s32[1280,1]{1,0:T(8,128)S(1)} %reshape.14.ids.ids_in, bf16[1280,128]{1,0:T(8,128)(2,1)S(1)} %get-tuple-element.25.basis.basis_in, f32[40,384]{1,0:T(8,128)S(1)} %get-tuple-element.29.feat1, f32[2,8,256]{2,1,0:T(8,128)S(1)} %copy-done.7, ...), custom_call_target="tpu_custom_call" | custom-call | tf_op jit(solution)/shard_map/second_layer/pallas_call | solution.py:399
  93.5 9.1 %all-to-all-start.1 = ((f32[128,1,128]{2,1,0:T(1,128)}), f32[128,1,128]{2,1,0:T(1,128)S(1)}, u32[]{:S(2)}, u32[]{:S(2)}) async-start(f32[128,1,128]{2,1,0:T(1,128)} %bitcast.8), calls=%async_computation.1 | async-start | bytes 131072 | tf_op jit(solution)/shard_map/all_to_all | solution.py:583
  102.6 0.6 copy-done.15
  103.2 0.5 slice_bitcast_fusion
  103.7 2.7 %pair_forces.13 = (f32[3,1536]{1,0:T(4,128)S(1)}, f32[1,1024]{1,0:T(1,128)}) custom-call(f32[4,1024]{1,0:T(4,128)S(1)} %collective-permute-done.23.left, f32[4,16384]{1,0:T(4,128)S(1)} %copy-done.2, f32[4,1024]{1,0:T(4,128)S(1)} %collective-permute-done.24.right, s32[16,16384]{1,0:T(8,128)S(1)} %copy-done.1, f32[128,128]{1,0:T(8,128)} %get-tuple-element.35.rest_0_), custom_call_target="tpu_custom_call" | custom-call | flops 120000000 | bytes 196608 | tf_op jit(solution)/shard_map/pair_forces/pallas_call | solution.py:88
  106.4 2.7 %pair_forces.11 = (f32[3,1536]{1,0:T(4,128)S(1)}, f32[1,1024]{1,0:T(1,128)}) custom-call(f32[4,1024]{1,0:T(4,128)S(1)} %collective-permute-done.23.left, f32[4,16384]{1,0:T(4,128)S(1)} %copy-done.2, f32[4,1024]{1,0:T(4,128)S(1)} %collective-permute-done.24.right, s32[16,16384]{1,0:T(8,128)S(1)} %copy-done.1, f32[128,128]{1,0:T(8,128)} %get-tuple-element.35.rest_0_), custom_call_target="tpu_custom_call" | custom-call | flops 120000000 | bytes 196608 | tf_op jit(solution)/shard_map/pair_forces/pallas_call | solution.py:88
  109.1 3.1 %pair_forces.12 = (f32[3,2048]{1,0:T(4,128)S(1)}, f32[1,1024]{1,0:T(1,128)}) custom-call(f32[3,40]{1,0:T(4,128)S(1)} %copy-done.6, f32[4,16384]{1,0:T(4,128)S(1)} %copy-done.2, f32[3,40]{1,0:T(4,128)S(1)} %copy-done.6, s32[16,16384]{1,0:T(8,128)S(1)} %copy-done.1, f32[128,128]{1,0:T(8,128)} %get-tuple-element.35.rest_0_), custom_call_target="tpu_custom_call" | custom-call | flops 160000000 | bytes 262144 | tf_op jit(solution)/shard_map/pair_forces/pallas_call | solution.py:88
  112.1 0.4 all-to-all-done.1
  112.5 7.8 %embed_forces.1 = f32[3,16384]{1,0:T(4,128)} custom-call(f32[4,16384]{1,0:T(4,128)S(1)} %copy-done.2, f32[128,256]{1,0:T(8,128)S(1)} %bitcast.18, f32[128,128]{1,0:T(8,128)S(1)} %bitcast.19, s32[1,8]{1,0:T(1,128)S(1)} %copy-done.10, s32[1]{0:T(128)S(6)} %copy.31.count_in, bf16[48,5120]{1,0:T(8,128)(2,1)S(1)} %copy-done.4, bf16[48,1024]{1,0:T(8,128)(2,1)S(1)} %copy-done.8, ...), custom_call_target="tpu_custom_call" | custom-call | tf_op jit(solution)/shard_map/embed_forces/pallas_call | solution.py:472
  (50 shorter events, 0.2 us)
Async XLA Ops:
  0.6 13.7 %copy-start.2 = (f32[4,16384]{1,0:T(4,128)S(1)}, f32[4,16384]{1,0:T(4,128)}, u32[]{:S(2)}) copy-start(f32[4,16384]{1,0:T(4,128)} %mm.3) | copy-start | bytes 786436
  2.1 12.2 %copy-start.6 = (f32[3,40]{1,0:T(4,128)S(1)}, f32[3,40]{1,0:T(4,128)}, u32[]{:S(2)}) copy-start(f32[3,40]{1,0:T(4,128)} %right.9) | copy-start | bytes 1444
  2.1 12.2 %copy-start.7 = (f32[2,8,256]{2,1,0:T(8,128)S(1)}, f32[2,8,256]{2,1,0:T(8,128)}, u32[]{:S(2)}) copy-start(f32[2,8,256]{2,1,0:T(8,128)} %radial_in.1) | copy-start | bytes 49156
  2.1 21.7 %all-to-all-start = ((f32[128,1,256]{2,1,0:T(1,128)}), f32[128,1,256]{2,1,0:T(1,128)S(1)}, u32[]{:S(2)}, u32[]{:S(2)}) async-start(f32[128,1,256]{2,1,0:T(1,128)} %spread.1), calls=%async_computation | async-start | bytes 262144 | tf_op jit(solution)/shard_map/all_to_all | solution.py:535
  13.6 0.7 copy-start.10
  14.4 1.2 %copy-start = (s32[16,16384]{1,0:T(8,128)S(1)}, s32[16,16384]{1,0:T(8,128)}, u32[]{:S(2)}) copy-start(s32[16,16384]{1,0:T(8,128)} %nb.13) | copy-start | bytes 3145732
  28.5 1.3 %collective-permute-start = (f32[40,128]{1,0:T(8,128)S(1)}, f32[40,128]{1,0:T(8,128)S(1)}, u32[]{:S(2)}, u32[]{:S(2)}) collective-permute-start(f32[40,128]{1,0:T(8,128)S(1)} %get-tuple-element.24.after), channel_id=1, source_target_pairs={{0,1},{1,0},{2,3},{3,2},{4,5},{5,4},{6,7},{7,6},{8,9},{9,8},{10,11... | collective-permute-start | bytes 61448 | tf_op jit(solution)/shard_map/ppermute | solution.py:508
  29.9 2.8 %copy-start.14 = (s32[40,32]{0,1:T(8,128)S(1)}, s32[40,32]{0,1:T(8,128)}, u32[]{:S(2)}) copy-start(s32[40,32]{0,1:T(8,128)} %param.20) | copy-start | bytes 15364
  29.9 7.1 %collective-permute-start.1 = (f32[40,128]{1,0:T(8,128)S(1)}, f32[40,128]{1,0:T(8,128)S(1)}, u32[]{:S(2)}, u32[]{:S(2)}) collective-permute-start(f32[40,128]{1,0:T(8,128)S(1)} %add.114), channel_id=1, source_target_pairs={{0,4},{1,33},{2,6},{3,35},{4,8},{5,37},{6,10},{7,39},{8,12},{9,41}... | collective-permute-start | bytes 61448 | tf_op jit(solution)/shard_map/ppermute | solution.py:502
  30.2 6.8 %collective-permute-start.2 = (f32[40,128]{1,0:T(8,128)S(1)}, f32[40,128]{1,0:T(8,128)S(1)}, u32[]{:S(2)}, u32[]{:S(2)}) collective-permute-start(f32[40,128]{1,0:T(8,128)S(1)} %add.114), channel_id=1, source_target_pairs={{0,8},{1,65},{2,10},{3,67},{4,12},{5,69},{6,14},{7,71},{8,0},{9,73... | collective-permute-start | bytes 61448 | tf_op jit(solution)/shard_map/ppermute | solution.py:502
  31.9 5.1 %collective-permute-start.3 = (f32[40,128]{1,0:T(8,128)S(1)}, f32[40,128]{1,0:T(8,128)S(1)}, u32[]{:S(2)}, u32[]{:S(2)}) collective-permute-start(f32[40,128]{1,0:T(8,128)S(1)} %add.114), channel_id=1, source_target_pairs={{0,12},{1,97},{2,14},{3,99},{4,0},{5,101},{6,2},{7,103},{8,4},{9,1... | collective-permute-start | bytes 61448 | tf_op jit(solution)/shard_map/ppermute | solution.py:502
  32.7 0.7 copy-start.12
  32.7 0.7 copy-start.13
  33.4 0.7 copy-start.11
  34.1 16.6 %copy-start.5 = (bf16[2,256,256]{2,1,0:T(8,128)(2,1)S(1)}, bf16[2,256,256]{2,1,0:T(8,128)(2,1)}, u32[]{:S(2)}) copy-start(bf16[2,256,256]{2,1,0:T(8,128)(2,1)} %msg.1) | copy-start | bytes 786436
  37.0 13.8 %copy-start.3 = (bf16[2,256,256]{2,1,0:T(8,128)(2,1)S(1)}, bf16[2,256,256]{2,1,0:T(8,128)(2,1)}, u32[]{:S(2)}) copy-start(bf16[2,256,256]{2,1,0:T(8,128)(2,1)} %mix_in.1) | copy-start | bytes 786436
  37.0 13.7 %copy-start.9 = (f32[10,256]{1,0:T(8,128)S(1)}, f32[10,256]{1,0:T(8,128)}, u32[]{:S(2)}) copy-start(f32[10,256]{1,0:T(8,128)} %table.1) | copy-start | bytes 30724
  37.1 18.4 %copy-start.1 = (s32[16,16384]{1,0:T(8,128)S(1)}, s32[16,16384]{1,0:T(8,128)}, u32[]{:S(2)}) copy-start(s32[16,16384]{1,0:T(8,128)} %nb.13) | copy-start | bytes 3145732
  37.1 4.8 %collective-permute-start.4 = (f32[40,128]{1,0:T(8,128)S(1)}, f32[40,128]{1,0:T(8,128)S(1)}, u32[]{:S(2)}, u32[]{:S(2)}) collective-permute-start(f32[40,128]{1,0:T(8,128)S(1)} %add_add_fusion.2), channel_id=1, source_target_pairs={{0,32},{1,3},{2,34},{3,17},{4,36},{5,7},{6,38},{7,21},{8,40},{9,11... | collective-permute-start | bytes 61448 | tf_op jit(solution)/shard_map/ppermute | solution.py:502
  38.2 4.1 %collective-permute-start.5 = (f32[40,128]{1,0:T(8,128)S(1)}, f32[40,128]{1,0:T(8,128)S(1)}, u32[]{:S(2)}, u32[]{:S(2)}) collective-permute-start(f32[40,128]{1,0:T(8,128)S(1)} %add_add_fusion.2), channel_id=1, source_target_pairs={{0,64},{1,17},{2,66},{3,19},{4,68},{5,21},{6,70},{7,23},{8,72},{9,... | collective-permute-start | bytes 61448 | tf_op jit(solution)/shard_map/ppermute | solution.py:502
  40.7 2.6 %collective-permute-start.6 = (f32[40,128]{1,0:T(8,128)S(1)}, f32[40,128]{1,0:T(8,128)S(1)}, u32[]{:S(2)}, u32[]{:S(2)}) collective-permute-start(f32[40,128]{1,0:T(8,128)S(1)} %add_add_fusion.2), channel_id=1, source_target_pairs={{0,96},{1,19},{2,98},{3,1},{4,100},{5,23},{6,102},{7,5},{8,104},{9... | collective-permute-start | bytes 61448 | tf_op jit(solution)/shard_map/ppermute | solution.py:502
  43.4 5.4 %collective-permute-start.7 = (f32[40,128]{1,0:T(8,128)S(1)}, f32[40,128]{1,0:T(8,128)S(1)}, u32[]{:S(2)}, u32[]{:S(2)}) collective-permute-start(f32[40,128]{1,0:T(8,128)S(1)} %add_add_fusion.1), channel_id=1, source_target_pairs={{0,2},{1,5},{2,16},{3,7},{4,6},{5,9},{6,20},{7,11},{8,10},{9,13},{... | collective-permute-start | bytes 61448 | tf_op jit(solution)/shard_map/ppermute | solution.py:502
  45.2 4.1 %collective-permute-start.8 = (f32[40,128]{1,0:T(8,128)S(1)}, f32[40,128]{1,0:T(8,128)S(1)}, u32[]{:S(2)}, u32[]{:S(2)}) collective-permute-start(f32[40,128]{1,0:T(8,128)S(1)} %add_add_fusion.1), channel_id=1, source_target_pairs={{0,16},{1,9},{2,18},{3,11},{4,20},{5,13},{6,22},{7,15},{8,24},{9,1... | collective-permute-start | bytes 61448 | tf_op jit(solution)/shard_map/ppermute | solution.py:502
  47.8 2.9 %collective-permute-start.9 = (f32[40,128]{1,0:T(8,128)S(1)}, f32[40,128]{1,0:T(8,128)S(1)}, u32[]{:S(2)}, u32[]{:S(2)}) collective-permute-start(f32[40,128]{1,0:T(8,128)S(1)} %add_add_fusion.1), channel_id=1, source_target_pairs={{0,18},{1,13},{2,0},{3,15},{4,22},{5,1},{6,4},{7,3},{8,26},{9,5},{... | collective-permute-start | bytes 61448 | tf_op jit(solution)/shard_map/ppermute | solution.py:502
  52.7 4.4 %collective-permute-start.10 = (bf16[40,256]{1,0:T(8,128)(2,1)S(1)}, bf16[40,256]{1,0:T(8,128)(2,1)S(1)}, u32[]{:S(2)}, u32[]{:S(2)}) collective-permute-start(bf16[40,256]{1,0:T(8,128)(2,1)S(1)} %get-tuple-element.30.rest_0_), channel_id=1, source_target_pairs={{0,4},{1,33},{2,6},{3,35},{4,8},{5,37},{6,10},{7,39},{8,12},{9,41}... | collective-permute-start | bytes 61448 | tf_op jit(solution)/shard_map/ppermute | solution.py:502
  53.0 4.1 %collective-permute-start.11 = (bf16[40,256]{1,0:T(8,128)(2,1)S(1)}, bf16[40,256]{1,0:T(8,128)(2,1)S(1)}, u32[]{:S(2)}, u32[]{:S(2)}) collective-permute-start(bf16[40,256]{1,0:T(8,128)(2,1)S(1)} %get-tuple-element.30.rest_0_), channel_id=1, source_target_pairs={{0,8},{1,65},{2,10},{3,67},{4,12},{5,69},{6,14},{7,71},{8,0},{9,73... | collective-permute-start | bytes 61448 | tf_op jit(solution)/shard_map/ppermute | solution.py:502
  53.9 3.5 %collective-permute-start.12 = (bf16[40,256]{1,0:T(8,128)(2,1)S(1)}, bf16[40,256]{1,0:T(8,128)(2,1)S(1)}, u32[]{:S(2)}, u32[]{:S(2)}) collective-permute-start(bf16[40,256]{1,0:T(8,128)(2,1)S(1)} %get-tuple-element.30.rest_0_), channel_id=1, source_target_pairs={{0,12},{1,97},{2,14},{3,99},{4,0},{5,101},{6,2},{7,103},{8,4},{9,1... | collective-permute-start | bytes 61448 | tf_op jit(solution)/shard_map/ppermute | solution.py:502
  57.4 6.5 %collective-permute-start.13 = (bf16[160,256]{1,0:T(8,128)(2,1)S(1)}, bf16[160,256]{1,0:T(8,128)(2,1)S(1)}, u32[]{:S(2)}, u32[]{:S(2)}) collective-permute-start(bf16[160,256]{1,0:T(8,128)(2,1)S(1)} %maximum_add_fusion.1.rest_0_), channel_id=1, source_target_pairs={{0,32},{1,3},{2,34},{3,17},{4,36},{5,7},{6,38},{7,21},{8,40},{9,11... | collective-permute-start | bytes 245768 | tf_op jit(solution)/shard_map/ppermute | solution.py:502
  57.5 6.4 %collective-permute-start.14 = (bf16[160,256]{1,0:T(8,128)(2,1)S(1)}, bf16[160,256]{1,0:T(8,128)(2,1)S(1)}, u32[]{:S(2)}, u32[]{:S(2)}) collective-permute-start(bf16[160,256]{1,0:T(8,128)(2,1)S(1)} %maximum_add_fusion.1.rest_0_), channel_id=1, source_target_pairs={{0,64},{1,17},{2,66},{3,19},{4,68},{5,21},{6,70},{7,23},{8,72},{9,... | collective-permute-start | bytes 245768 | tf_op jit(solution)/shard_map/ppermute | solution.py:502
  60.7 3.3 %collective-permute-start.15 = (bf16[160,256]{1,0:T(8,128)(2,1)S(1)}, bf16[160,256]{1,0:T(8,128)(2,1)S(1)}, u32[]{:S(2)}, u32[]{:S(2)}) collective-permute-start(bf16[160,256]{1,0:T(8,128)(2,1)S(1)} %maximum_add_fusion.1.rest_0_), channel_id=1, source_target_pairs={{0,96},{1,19},{2,98},{3,1},{4,100},{5,23},{6,102},{7,5},{8,104},{9... | collective-permute-start | bytes 245768 | tf_op jit(solution)/shard_map/ppermute | solution.py:502
  64.0 17.8 %collective-permute-start.16 = (bf16[640,256]{1,0:T(8,128)(2,1)S(1)}, bf16[640,256]{1,0:T(8,128)(2,1)S(1)}, u32[]{:S(2)}, u32[]{:S(2)}) collective-permute-start(bf16[640,256]{1,0:T(8,128)(2,1)S(1)} %maximum_add_fusion.rest_0_.p0), channel_id=1, source_target_pairs={{0,2},{1,5},{2,16},{3,7},{4,6},{5,9},{6,20},{7,11},{8,10},{9,13},{... | collective-permute-start | bytes 983048 | tf_op jit(solution)/shard_map/ppermute | solution.py:502
  64.1 17.7 %collective-permute-start.17 = (bf16[640,256]{1,0:T(8,128)(2,1)S(1)}, bf16[640,256]{1,0:T(8,128)(2,1)S(1)}, u32[]{:S(2)}, u32[]{:S(2)}) collective-permute-start(bf16[640,256]{1,0:T(8,128)(2,1)S(1)} %maximum_add_fusion.rest_0_.p0), channel_id=1, source_target_pairs={{0,16},{1,9},{2,18},{3,11},{4,20},{5,13},{6,22},{7,15},{8,24},{9,1... | collective-permute-start | bytes 983048 | tf_op jit(solution)/shard_map/ppermute | solution.py:502
  67.4 14.5 %collective-permute-start.18 = (bf16[640,256]{1,0:T(8,128)(2,1)S(1)}, bf16[640,256]{1,0:T(8,128)(2,1)S(1)}, u32[]{:S(2)}, u32[]{:S(2)}) collective-permute-start(bf16[640,256]{1,0:T(8,128)(2,1)S(1)} %maximum_add_fusion.rest_0_.p0), channel_id=1, source_target_pairs={{0,18},{1,13},{2,0},{3,15},{4,22},{5,1},{6,4},{7,3},{8,26},{9,5},{... | collective-permute-start | bytes 983048 | tf_op jit(solution)/shard_map/ppermute | solution.py:502
  68.0 17.7 %collective-permute-start.19 = (bf16[640,256]{1,0:T(8,128)(2,1)S(1)}, bf16[640,256]{1,0:T(8,128)(2,1)S(1)}, u32[]{:S(2)}, u32[]{:S(2)}) collective-permute-start(bf16[640,256]{1,0:T(8,128)(2,1)S(1)} %maximum_add_fusion.rest_0_.p0), channel_id=1, source_target_pairs={{0,1},{1,0},{2,3},{3,2},{4,5},{5,4},{6,7},{7,6},{8,9},{9,8},{10,11... | collective-permute-start | bytes 983048 | tf_op jit(solution)/shard_map/ppermute | solution.py:508
  81.9 3.9 %collective-permute-start.20 = (bf16[640,256]{1,0:T(8,128)(2,1)S(1)}, bf16[640,256]{1,0:T(8,128)(2,1)S(1)}, u32[]{:S(2)}, u32[]{:S(2)}) collective-permute-start(bf16[640,256]{1,0:T(8,128)(2,1)S(1)} %get-tuple-element.48.p1), channel_id=1, source_target_pairs={{0,1},{1,0},{2,3},{3,2},{4,5},{5,4},{6,7},{7,6},{8,9},{9,8},{10,11... | collective-permute-start | bytes 983048 | tf_op jit(solution)/shard_map/ppermute | solution.py:508
  84.5 1.7 %collective-permute-start.21 = (bf16[640,256]{1,0:T(8,128)(2,1)S(1)}, bf16[640,256]{1,0:T(8,128)(2,1)S(1)}, u32[]{:S(2)}, u32[]{:S(2)}) collective-permute-start(bf16[640,256]{1,0:T(8,128)(2,1)S(1)} %get-tuple-element.47.p2), channel_id=1, source_target_pairs={{0,1},{1,0},{2,3},{3,2},{4,5},{5,4},{6,7},{7,6},{8,9},{9,8},{10,11... | collective-permute-start | bytes 983048 | tf_op jit(solution)/shard_map/ppermute | solution.py:508
  84.6 2.1 %collective-permute-start.22 = (bf16[640,256]{1,0:T(8,128)(2,1)S(1)}, bf16[640,256]{1,0:T(8,128)(2,1)S(1)}, u32[]{:S(2)}, u32[]{:S(2)}) collective-permute-start(bf16[640,256]{1,0:T(8,128)(2,1)S(1)} %get-tuple-element.46.p3), channel_id=1, source_target_pairs={{0,1},{1,0},{2,3},{3,2},{4,5},{5,4},{6,7},{7,6},{8,9},{9,8},{10,11... | collective-permute-start | bytes 983048 | tf_op jit(solution)/shard_map/ppermute | solution.py:508
  85.1 18.6 %collective-permute-start.23 = (f32[4,1024]{1,0:T(4,128)S(1)}, f32[4,1024]{1,0:T(4,128)S(1)}, u32[]{:S(2)}, u32[]{:S(2)}) collective-permute-start(f32[4,1024]{1,0:T(4,128)S(1)} %get-tuple-element.45), channel_id=1, source_target_pairs={{0,1},{1,2},{2,3},{3,4},{4,5},{5,6},{6,7},{7,8},{8,9},{9,10},{10,1... | collective-permute-start | bytes 49160 | tf_op jit(solution)/shard_map/ppermute | solution.py:564
  85.7 18.0 %collective-permute-start.24 = (f32[4,1024]{1,0:T(4,128)S(1)}, f32[4,1024]{1,0:T(4,128)S(1)}, u32[]{:S(2)}, u32[]{:S(2)}) collective-permute-start(f32[4,1024]{1,0:T(4,128)S(1)} %get-tuple-element.44), channel_id=1, source_target_pairs={{1,0},{2,1},{3,2},{4,3},{5,4},{6,5},{7,6},{8,7},{9,8},{10,9},{11,1... | collective-permute-start | bytes 49160 | tf_op jit(solution)/shard_map/ppermute | solution.py:565
  93.5 19.1 %all-to-all-start.1 = ((f32[128,1,128]{2,1,0:T(1,128)}), f32[128,1,128]{2,1,0:T(1,128)S(1)}, u32[]{:S(2)}, u32[]{:S(2)}) async-start(f32[128,1,128]{2,1,0:T(1,128)} %bitcast.8), calls=%async_computation.1 | async-start | bytes 131072 | tf_op jit(solution)/shard_map/all_to_all | solution.py:583
  102.6 0.6 copy-start.15
  109.1 3.5 %copy-start.4 = (bf16[48,5120]{1,0:T(8,128)(2,1)S(1)}, bf16[48,5120]{1,0:T(8,128)(2,1)}, u32[]{:S(2)}) copy-start(bf16[48,5120]{1,0:T(8,128)(2,1)} %get-tuple-element.36.atoms_in) | copy-start | bytes 1474564
  109.1 3.5 %copy-start.8 = (bf16[48,1024]{1,0:T(8,128)(2,1)S(1)}, bf16[48,1024]{1,0:T(8,128)(2,1)}, u32[]{:S(2)}) copy-start(bf16[48,1024]{1,0:T(8,128)(2,1)} %get-tuple-element.37.slots_in) | copy-start | bytes 294916
